TPU v7x, 32 devices: a whole 2x2x4 slice. The times are simulated.
32 devices in a mesh: dp: 4 (over x, core), chan: 8 (over z, y).
Axes of the slice: x: 2, y: 2, z: 4, core: 2. Of those that a mesh axis runs over, the one named last changes fastest.
Arguments:
- features: bfloat16 [512, 2, 128, 256], P('chan', None, 'dp'), may hold values from -6 to 6
- latent: bfloat16 [2, 512], replicated, may hold values from -6 to 6
- affine: bfloat16 [512, 512], replicated, may hold values from -0.25 to 0.25
- affine_bias: float32 [512], replicated, may hold values from 0.5 to 1.5
- weight: bfloat16 [3, 3, 512, 512], P(None, None, 'chan'), may hold values from -0.09375 to 0.09375
- out_bias: float32 [512], P('chan'), may hold values from -3 to 3
- cotangent: bfloat16 [512, 2, 128, 256], P('chan', None, 'dp'), may hold values from -6 to 6
- latents_all: bfloat16 [2048, 512], P(('dp', 'chan')), may hold values from -6 to 6
- labels: int32 [2048], P(('dp', 'chan')), may hold values from 0 to 999
- class_means: float32 [1000, 512], replicated, may hold values from -6 to 6
Outputs:
- output: bfloat16 [512, 2, 128, 256], P('chan', None, 'dp')
- grad_features: float32 [512, 2, 128, 256], P('chan', None, 'dp')
- grad_latent: float32 [2, 512], replicated
- grad_affine: float32 [512, 512], replicated
- grad_affine_bias: float32 [512], replicated
- grad_weight: float32 [3, 3, 512, 512], P(None, None, 'chan')
- grad_bias: float32 [512], P('chan')
- class_target: float32 [1000, 512], replicated
All inputs are finite; a program needn't handle non-finite values.
Results may differ from a plain program's by a relative error of at most 0.0053.
Values may be sent and summed in bfloat16 or wider, within the bound.
No kernel may reach another device: no remote copies, remote signals or barrier semaphores. Data moves between devices by JAX's collectives and lax.ppermute only.
A program may use at most 512 MiB of HBM per device.

v0:
```python
import jax
import jax.numpy as jnp
from jax import lax
from jax.sharding import PartitionSpec as P


def extended_2(shard, sides, width):
    for axis, dim in sides:
        size, length = (lax.axis_size(axis), shard.shape[dim])
        up = [(i, (i + 1) % size) for i in range(size - 1)]
        down = [(j, i) for i, j in up]
        last = lax.slice_in_dim(shard, length - width, length, axis=dim)
        first = lax.slice_in_dim(shard, 0, width, axis=dim)
        before = lax.ppermute(last, axis, up)
        after = lax.ppermute(first, axis, down)
        shard = jnp.concatenate([before, shard, after], axis=dim)
    return shard


def shortened(shard):

    def short(part):
        return part.astype(jnp.bfloat16) if part.dtype == jnp.float32 else part

    return jax.tree.map(short, shard)


def sinc_taps():
    offset = jnp.arange(12).astype(jnp.float32) - 5.5
    window = 0.5 + 0.5 * jnp.cos(jnp.pi * offset / 6.0)
    values = jnp.sinc(offset * 0.5) * window
    return values / jnp.sum(values)


def pad_dim(values, dim_at, margin):
    widths = [(0, 0)] * values.ndim
    widths[dim_at] = (margin, margin)
    return jnp.pad(values, widths)


def up_taps(values, dim_at, factor):
    tap_values = sinc_taps()
    extent = values.shape[dim_at] - 6
    parities = []
    for parity in range(2):
        summed = None
        for offset in range(-3, 4):
            tap_id = 2 * offset + parity + 5
            if 0 <= tap_id < 12:
                addend = (
                    factor
                    * tap_values[tap_id]
                    * lax.slice_in_dim(values, 3 - offset, 3 - offset + extent, axis=dim_at)
                )
                summed = addend if summed is None else summed + addend
        parities.append(summed)
    return jnp.stack(parities, axis=dim_at)


def down_taps(phased, dim_at, factor):
    tap_values = sinc_taps()
    extent = phased.shape[dim_at + 1] - 6
    summed = None
    for parity in range(2):
        picked = lax.index_in_dim(phased, parity, dim_at, keepdims=False)
        for offset in range(-3, 4):
            tap_id = 2 * offset + parity + 5
            if 0 <= tap_id < 12:
                addend = (
                    factor
                    * tap_values[tap_id]
                    * lax.slice_in_dim(picked, 3 + offset, 3 + offset + extent, axis=dim_at)
                )
                summed = addend if summed is None else summed + addend
    return summed


def pad_cols(extended):
    return jnp.pad(extended, ((0, 0), (0, 0), (0, 0), (1, 1)))


def conv_forward(extended, kernel):
    row_span = extended.shape[2] - 2
    col_span = extended.shape[3]
    padded = pad_cols(extended)
    result = jnp.zeros((kernel.shape[2], extended.shape[1], row_span, col_span), jnp.float32)
    for tap_row in range(3):
        for tap_col in range(3):
            result = result + jnp.einsum(
                "oi,ibrw->obrw",
                kernel[tap_row, tap_col],
                padded[:, :, tap_row : tap_row + row_span, tap_col : tap_col + col_span],
                preferred_element_type=jnp.float32,
            )
    return result


def conv_inputs(extended_grad, kernel):
    row_span = extended_grad.shape[2] - 2
    col_span = extended_grad.shape[3]
    padded = pad_cols(extended_grad)
    result = jnp.zeros((kernel.shape[3], extended_grad.shape[1], row_span, col_span), jnp.float32)
    for tap_row in range(3):
        for tap_col in range(3):
            result = result + jnp.einsum(
                "oi,obrw->ibrw",
                kernel[tap_row, tap_col],
                padded[
                    :, :, 2 - tap_row : 2 - tap_row + row_span, 2 - tap_col : 2 - tap_col + col_span
                ],
                preferred_element_type=jnp.float32,
            )
    return result


def conv_weight(grad_rows, extended):
    row_span = grad_rows.shape[2]
    col_span = grad_rows.shape[3]
    padded = pad_cols(extended)
    stacked = []
    for tap_row in range(3):
        row_parts = []
        for tap_col in range(3):
            row_parts.append(
                jnp.einsum(
                    "obrw,ibrw->oi",
                    grad_rows,
                    padded[:, :, tap_row : tap_row + row_span, tap_col : tap_col + col_span],
                    preferred_element_type=jnp.float32,
                )
            )
        stacked.append(jnp.stack(row_parts))
    return jnp.stack(stacked)


def conv_rims(value):
    return extended_2(value, (("dp", 2),), 1)


def per_device(
    features,
    latent,
    affine,
    affine_bias,
    weight,
    out_bias,
    cotangent,
    latents_all,
    labels,
    class_means,
):
    highest = lax.Precision.HIGHEST
    own_chans = features.shape[0]
    row_count = features.shape[2]
    dp_total = lax.axis_size("dp")
    chan_first = lax.axis_index("chan") * own_chans
    styles = jnp.dot(latent, affine, preferred_element_type=jnp.float32) + affine_bias
    own_style = lax.dynamic_slice_in_dim(styles, chan_first, own_chans, 1)
    scale_own = own_style.T[:, :, None, None]
    modded = (features.astype(jnp.float32) * scale_own).astype(jnp.bfloat16)
    weight_full = weight.astype(jnp.float32)
    weight_sq = jnp.sum(weight_full * weight_full, axis=(0, 1))
    demod_scale = lax.rsqrt(jnp.dot(styles * styles, weight_sq.T, precision=highest) + 1e-08)
    demod_grid = demod_scale.T[:, :, None, None]
    extended = conv_rims(modded)
    gathered = lax.all_gather(extended, "chan", axis=0, tiled=True)
    raw_conv = conv_forward(gathered, weight)
    biased = raw_conv * demod_grid + out_bias[:, None, None, None]
    position = lax.axis_index("dp") * row_count - 3 + jnp.arange(row_count + 6)
    inside = ((position >= 0) & (position < row_count * dp_total)).astype(jnp.float32)[
        None, None, None, :, None, None
    ]
    biased_ext = extended_2(biased, (("dp", 2),), 6)
    wide_rows = up_taps(pad_dim(biased_ext, 3, 3), 3, 2.0)
    upsampled = up_taps(wide_rows, 2, 2.0)
    active = jax.nn.silu(upsampled) * inside
    narrow = down_taps(active, 2, 1.0)
    output = down_taps(pad_dim(narrow, 4, 3), 3, 1.0).astype(jnp.bfloat16)
    g_narrow = up_taps(pad_dim(cotangent.astype(jnp.float32), 3, 3), 3, 1.0)
    g_active = up_taps(pad_dim(g_narrow, 2, 6), 2, 1.0) * inside
    sigmoid_up = jax.nn.sigmoid(upsampled)
    g_up = g_active * sigmoid_up * (1.0 + upsampled * (1.0 - sigmoid_up))
    g_wide = down_taps(pad_dim(g_up, 3, 6), 2, 2.0)
    g_extended = down_taps(pad_dim(g_wide, 4, 3), 3, 2.0)
    rim_parts = jnp.concatenate([g_extended[:, :, :6], g_extended[:, :, row_count + 6 :]], axis=2)
    received = extended_2(shortened(rim_parts), (("dp", 2),), 6).astype(rim_parts.dtype)
    g_pre = g_extended[:, :, 6 : row_count + 6]
    g_pre = g_pre.at[:, :, :6].add(received[:, :, :6])
    g_pre = g_pre.at[:, :, row_count - 6 :].add(received[:, :, 18:])
    g_bias_part = jnp.sum(g_pre, axis=(1, 2, 3))
    g_demod = jnp.sum(g_pre * raw_conv, axis=(2, 3)).T
    g_raw = (g_pre * demod_grid).astype(jnp.bfloat16)
    grad_extended = conv_rims(g_raw)
    g_modded = lax.psum_scatter(
        conv_inputs(grad_extended, weight), "chan", scatter_dimension=0, tiled=True
    )
    g_weight_conv = conv_weight(g_raw, gathered)
    grad_features = g_modded * scale_own
    g_style_own = jnp.sum(g_modded * features.astype(jnp.float32), axis=(2, 3)).T
    g_dsq = -0.5 * g_demod * demod_scale * demod_scale * demod_scale
    g_wsq = jnp.dot(g_dsq.T, styles * styles, precision=highest)
    g_weight_part = g_weight_conv + 2.0 * weight_full * g_wsq[None, None]
    g_style_part = 2.0 * styles * jnp.dot(g_dsq, weight_sq, precision=highest)
    g_style_part = g_style_part + lax.dynamic_update_slice_in_dim(
        jnp.zeros_like(g_style_part), g_style_own, chan_first, 1
    )
    grad_weight, grad_bias = lax.psum((g_weight_part, g_bias_part), "dp")
    class_ids = jnp.arange(class_means.shape[0])[:, None]
    one_hot = labels[None, :] == class_ids
    sums_part = jnp.dot(
        one_hot.astype(jnp.bfloat16), latents_all, preferred_element_type=jnp.float32
    )
    counts_part = jnp.sum(one_hot.astype(jnp.float32), axis=1)
    g_style, class_sums, counts = lax.psum((g_style_part, sums_part, counts_part), ("dp", "chan"))
    grad_affine_bias = jnp.sum(g_style, axis=0)
    grad_affine = jnp.dot(latent.astype(jnp.float32).T, g_style, precision=highest)
    grad_latent = jnp.dot(g_style, affine.astype(jnp.float32).T, precision=highest)
    target = jnp.where(
        counts[:, None] > 0, class_sums / jnp.maximum(counts, 1.0)[:, None], class_means
    )
    return (
        output,
        grad_features,
        grad_latent,
        grad_affine,
        grad_affine_bias,
        grad_weight,
        grad_bias,
        target,
    )


def solution(mesh):
    in_specs = (
        P("chan", None, "dp", None),
        P(),
        P(),
        P(),
        P(None, None, "chan", None),
        P("chan"),
        P("chan", None, "dp", None),
        P(("dp", "chan"), None),
        P(("dp", "chan")),
        P(),
    )
    out_specs = (
        P("chan", None, "dp", None),
        P("chan", None, "dp", None),
        P(),
        P(),
        P(),
        P(None, None, "chan", None),
        P("chan"),
        P(),
    )
    return jax.shard_map(
        per_device, mesh=mesh, in_specs=in_specs, out_specs=out_specs, check_vma=False
    )
```

profile of v0, /device:TPU:0, one launch (start us, length us, event | category | flops | bytes accessed | tf_op | source)
XLA Modules:
  0.0 1555.6 jit_solution(12438604936616160276)
XLA Ops:
  35.8 19.9 %fusion.105 = (f32[64,2,32,1,256]{4,0,2,1,3:T(8,128)}, f32[64,2,32,1,256]{4,0,2,1,3:T(8,128)}) fusion(f32[64,2,32,256]{3,0,2,1:T(8,128)S(1)} %copy_convert_fusion, f32[]{:T(128)} %bitcast.35, f32[]{:T(128)} %bitcast.34, f32[]{:T(128)} %bitcast.33, f32[]{:T(128)} %bitcast.32, f32[]{:T(128)} %bitcast.31, f32[]{:T(128)} %bitcast, f32[]{:T(128)} %bitcast.42, ...), kind=kLoop, calls=%fused_computation.195 | loop fusion | flops 23068672 | bytes 12582960 | tf_op jit(solution)/shard_map/stack | solution.py:57
  64.4 13.5 fusion.56
  78.0 290.1 %all-gather.2.cloned.1.call-done = bf16[512,2,34,256]{3,0,2,1:T(8,128)(2,1)} async-done(((bf16[64,2,34,256]{3,0,2,1:T(8,128)(2,1)}), bf16[512,2,34,256]{3,0,2,1:T(8,128)(2,1)}) %all-gather.2.cloned.1.call-update) | async-done | bytes 17825808 | tf_op jit(solution)/shard_map/all_gather | solution.py:166
  368.1 11.1 fusion.19
  380.5 6.6 fusion.21
  387.1 6.7 fusion.23
  393.8 6.9 fusion.25
  400.6 4.5 fusion.4
  405.1 4.5 fusion.8
  409.7 4.6 fusion.12
  414.3 6.6 fusion.17
  420.9 20.0 %fusion.125 = (f32[64,2,32,256]{3,0,2,1:T(8,128)S(1)}, f32[2,32,256,64]{2,3,1,0:T(8,128)}) fusion(f32[64]{0:T(128)S(1)} %copy-done.22, f32[64,2]{0,1:T(2,128)S(1)} %bitcast.233, bf16[512,2,34,256]{3,0,2,1:T(8,128)(2,1)} %all-gather.2.cloned.1.call-done, bf16[3,3,64,512]{3,2,1,0:T(8,128)(2,1)} %param.19, f32[2,32,256,64]{2,3,1,0:T(8,128)} %fusion.4, ...), kind=kOutput, calls=%fused_computation.229 | convolution fusion | flops 1084227584 | bytes 59835136 | tf_op jit(solution)/shard_map/oi,ibrw->obrw/dot_general | solution.py:89
  444.1 28.4 %fusion.54 = f32[64,2,1,38,2,256]{5,0,3,1,4,2:T(8,128)} fusion(f32[64,2,44,2,256]{4,0,2,1,3:T(8,128)} %copy-done.1, f32[]{:T(128)} %bitcast.42, f32[]{:T(128)} %bitcast.41, f32[]{:T(128)} %bitcast.40, f32[]{:T(128)} %bitcast.39, f32[]{:T(128)} %bitcast.38, f32[]{:T(128)} %bitcast.37), kind=kLoop, calls=%fused_computation.107 | loop fusion | flops 27394048 | bytes 69730328 | tf_op jit(solution)/shard_map/stack | solution.py:57
  475.6 38.8 %fusion.82 = (f32[64,2,44,1,256]{4,0,2,1,3:T(8,128)}, f32[64,2,44,1,256]{4,0,2,1,3:T(8,128)}) fusion(f32[64,2,44,256]{3,0,2,1:T(8,128)} %pad_maximum_fusion.2, f32[]{:T(128)S(6)} %mul.819, f32[]{:T(128)S(6)} %mul.816, f32[]{:T(128)S(6)} %mul.813, f32[]{:T(128)S(6)} %mul.810, f32[]{:T(128)S(6)} %mul.807, f32[]{:T(128)S(6)} %mul.796, f32[]{:T(128)S(6)} %mul.837, ...), kind=kLoop, calls=%fused_computation.157 | loop fusion | flops 31719424 | bytes 17301552 | tf_op jit(solution)/shard_map/stack | solution.py:57
  514.4 49.8 %fusion.43 = (f32[64,2,1,38,2,256]{5,0,3,1,4,2:T(8,128)}, f32[64,2,1,38,2,256]{5,0,3,1,4,2:T(8,128)}) fusion(f32[64,2,44,1,256]{4,0,2,1,3:T(8,128)} %get-tuple-element.67, f32[64,2,44,1,256]{4,0,2,1,3:T(8,128)} %get-tuple-element.68, f32[]{:T(128)S(6)} %mul.819, f32[]{:T(128)S(6)} %mul.816, f32[]{:T(128)S(6)} %mul.813, f32[]{:T(128)S(6)} %mul.810, ...), kind=kLoop, calls=%fused_computation.95 | loop fusion | flops 84672512 | bytes 31457328 | tf_op jit(solution)/shard_map/stack | solution.py:57
  564.2 23.5 %fusion.1 = (f32[64,2,2,38,2,256]{5,0,3,1,4,2:T(8,128)S(1)}, f32[64,2,2,38,2,256]{5,0,3,1,4,2:T(8,128)}) fusion(f32[64,2,1,38,2,256]{5,0,3,1,4,2:T(8,128)} %fusion.54, f32[64,2,1,38,2,256]{5,0,3,1,4,2:T(8,128)} %fusion.56, f32[64,2,1,38,2,256]{5,0,3,1,4,2:T(8,128)} %get-tuple-element.64, f32[64,2,1,38,2,256]{5,0,3,1,4,2:T(8,128)} %get-tuple-element.63, ...), kind=kLoop, calls=%fused_computation.24 | loop fusion | flops 64749568 | bytes 79691928 | tf_op jit(solution)/shard_map/mul | solution.py:182
  587.8 9.3 fusion.14
  597.1 50.4 %fusion.28 = f32[64,2,44,2,256]{4,0,2,1,3:T(8,128)} fusion(f32[64,2,50,2,256]{4,0,2,1,3:T(8,128)} %get-tuple-element.58, f32[64,2,50,2,256]{4,0,2,1,3:T(8,128)} %get-tuple-element.57, f32[]{:T(128)S(6)} %mul.837, f32[]{:T(128)S(6)} %mul.834, f32[]{:T(128)S(6)} %mul.831, f32[]{:T(128)S(6)} %mul.828, f32[]{:T(128)S(6)} %mul.825, f32[]{:T(128)S(6)} %mul.822, ...), kind=kLoop, calls=%fused_computation.66 | loop fusion | flops 66322432 | bytes 149946416 | tf_op jit(solution)/shard_map/add | solution.py:74
  647.5 10.9 fusion.64
  658.4 46.9 %fusion.238 = (bf16[64,2,44,256]{3,0,2,1:T(8,128)(2,1)S(1)}, f32[64,2,44,256]{3,0,2,1:T(8,128)}) fusion(f32[64,2,44,262]{3,0,2,1:T(8,128)} %get-tuple-element.62, f32[]{:T(128)S(6)} %mul.837, f32[]{:T(128)S(6)} %mul.834, f32[]{:T(128)S(6)} %mul.831, f32[]{:T(128)S(6)} %mul.828, f32[]{:T(128)S(6)} %mul.825, f32[]{:T(128)S(6)} %mul.822, ...), kind=kLoop, calls=%fused_computation.371 | loop fusion | flops 34603008 | bytes 77856816 | tf_op jit(solution)/shard_map/convert.2
  719.4 8.7 collective-permute-start.6
  728.1 13.3 fusion.186
  743.7 13.3 fusion.144
  757.1 13.2 fusion.146
  770.2 13.3 fusion.148
  783.5 13.2 fusion.150
  796.8 13.4 fusion.152
  810.2 13.2 fusion.136
  823.4 13.3 fusion.132
  836.7 92.8 %add_bitcast_fusion = f32[512,2,32,256]{3,0,2,1:T(8,128)} fusion(f32[2,32,256,512]{2,3,1,0:T(8,128)} %fusion.136, f32[2,32,256,512]{2,3,1,0:T(8,128)} %fusion.144, f32[2,32,256,512]{2,3,1,0:T(8,128)} %fusion.146, f32[2,32,256,512]{2,3,1,0:T(8,128)} %fusion.186, f32[2,32,256,512]{2,3,1,0:T(8,128)} %fusion.148, f32[2,32,256,512]{2,3,1,0:T(8,128)} %fusion.150, ...), kind=kOutput, calls=%fused_computation | convolution fusion | flops 1140850688 | bytes 304152576 | tf_op jit(solution)/shard_map/oi,obrw->ibrw/dot_general | solution.py:105
  932.4 15.8 %slice_bitcast_fusion.1 = (f32[64,2,38,2,256]{4,0,2,1,3:T(8,128)}, f32[64,2,38,2,256]{4,0,2,1,3:T(8,128)}) fusion(f32[64,2,2,38,2,256]{5,0,3,1,4,2:T(8,128)} %get-tuple-element.56), kind=kLoop, calls=%fused_computation.112 | loop fusion | bytes 39845888 | tf_op jit(solution)/shard_map/squeeze | solution.py:65
  948.2 45.9 %fusion.66 = f32[64,2,32,2,256]{4,0,2,1,3:T(8,128)} fusion(f32[64,2,38,2,256]{4,0,2,1,3:T(8,128)} %get-tuple-element.60, f32[64,2,38,2,256]{4,0,2,1,3:T(8,128)} %get-tuple-element.59, f32[]{:T(128)} %bitcast.42, f32[]{:T(128)} %bitcast.41, f32[]{:T(128)} %bitcast.40, f32[]{:T(128)} %bitcast.39, f32[]{:T(128)} %bitcast.38, f32[]{:T(128)} %bitcast.37, ...), kind=kLoop, calls=%fused_computation.130 | loop fusion | flops 48234496 | bytes 109051952 | tf_op jit(solution)/shard_map/add | solution.py:74
  994.0 5.7 fusion.78
  999.8 20.6 %fusion.114 = bf16[64,2,32,256]{3,0,2,1:T(8,128)(2,1)} fusion(f32[64,2,32,262]{3,0,2,1:T(8,128)S(1)} %get-tuple-element.66, f32[64,2,32,262]{3,0,2,1:T(8,128)S(1)} %get-tuple-element.65, f32[]{:T(128)} %bitcast.42, f32[]{:T(128)} %bitcast.41, f32[]{:T(128)} %bitcast.40, f32[]{:T(128)} %bitcast.39, f32[]{:T(128)} %bitcast.38, f32[]{:T(128)} %bitcast.37, ...), kind=kLoop, calls=%fused_computation.205 | loop fusion | flops 25165824 | bytes 52428848 | tf_op jit(solution)/shard_map/convert_element_type | solution.py:178
  1024.5 9.4 fusion.168
  1033.9 11.4 fusion.157
  1045.3 10.5 fusion.158
  1055.8 9.4 fusion.165
  1065.2 11.2 fusion.159
  1076.4 11.4 fusion.160
  1087.8 9.6 fusion.162
  1097.4 11.2 fusion.161
  1108.7 11.3 fusion.156
  1120.0 8.2 psum.37
  1132.4 354.3 %reduce-scatter.2.cloned.1.call-done = f32[64,2,32,256]{3,0,2,1:T(8,128)} async-done(((f32[512,2,32,256]{3,0,2,1:T(8,128)}), f32[64,2,32,256]{3,0,2,1:T(8,128)}) %reduce-scatter.2.cloned.1.call-update) | async-done | bytes 4194320 | tf_op jit(solution)/shard_map/reduce_scatter | solution.py:194
  1486.7 6.2 fusion.102
  1493.1 38.6 %all-reduce.8 = (f32[2,512]{1,0:T(2,128)S(1)}, f32[1000]{0:T(1024)S(1)}) all-reduce(f32[2,512]{1,0:T(2,128)S(1)} %add.558, f32[1000]{0:T(1024)S(1)} %convert_reduce_fusion), channel_id=1, replica_groups=mesh['dp'=4,'chan'=8] {'dp','chan'}, use_global_device_ids=true, to_apply=%region_5.7 | all-reduce | flops 2024 | bytes 16192 | tf_op jit(solution)/shard_map/psum | solution.py:214
  1535.3 6.8 copy.44
  (115 shorter events, 73.2 us)
Async XLA Ops:
  8.0 1.0 copy-start
  8.0 23.8 %copy-start.7 = (bf16[3,3,64,512]{3,2,1,0:T(8,128)(2,1)S(1)}, bf16[3,3,64,512]{3,2,1,0:T(8,128)(2,1)}, u32[]{:S(2)}) copy-start(bf16[3,3,64,512]{3,2,1,0:T(8,128)(2,1)} %param.19) | copy-start | bytes 1769476
  8.0 360.1 %all-gather.2.cloned.1.call-start = ((), (), s32[]{:S(2)}) async-start(), calls=%async_computation.1 | async-start | bytes 20054016 | tf_op jit(solution)/shard_map/all_gather | solution.py:166
  9.9 25.9 %copy-start.13 = (f32[2,512]{1,0:T(2,128)}, f32[2,512]{1,0:T(2,128)S(1)}, u32[]{:S(2)}) copy-start(f32[2,512]{1,0:T(2,128)S(1)} %convolution_add_fusion) | copy-start | bytes 12292
  10.0 6.6 copy-start.19
  12.9 3.7 collective-permute-start
  15.3 5.3 collective-permute-start.1
  22.2 1464.5 %reduce-scatter.2.cloned.1.call-start = ((), (), s32[]{:S(2)}) async-start(), calls=%async_computation.2 | async-start | bytes 37748736 | tf_op jit(solution)/shard_map/reduce_scatter | solution.py:194
  32.0 0.7 copy-start.11
  32.8 683.0 %copy-start.16 = (f32[2,64]{1,0:T(2,128)}, f32[2,64]{1,0:T(2,128)S(1)}, u32[]{:S(2)}) copy-start(f32[2,64]{1,0:T(2,128)S(1)} %fusion.171) | copy-start | bytes 1540
  60.1 4.3 copy-start.1
  368.1 12.4 copy-start.2
  414.3 6.6 copy-start.22
  441.0 31.5 %collective-permute-start.2 = (f32[64,2,6,256]{3,0,2,1:T(8,128)S(1)}, f32[64,2,6,256]{3,0,2,1:T(8,128)S(1)}, u32[]{:S(2)}, u32[]{:S(2)}) collective-permute-start(f32[64,2,6,256]{3,0,2,1:T(8,128)S(1)} %get-tuple-element.74), channel_id=1, source_target_pairs={{0,8},{8,16},{16,24},{1,9},{9,17},{17,25},{2,10},{10,18},{18,26},{... | collective-permute-start | bytes 2359304 | tf_op jit(solution)/shard_map/ppermute | solution.py:14
  442.8 29.7 %collective-permute-start.3 = (f32[64,2,6,256]{3,0,2,1:T(8,128)S(1)}, f32[64,2,6,256]{3,0,2,1:T(8,128)S(1)}, u32[]{:S(2)}, u32[]{:S(2)}) collective-permute-start(f32[64,2,6,256]{3,0,2,1:T(8,128)S(1)} %get-tuple-element.75), channel_id=1, source_target_pairs={{8,0},{16,8},{24,16},{9,1},{17,9},{25,17},{10,2},{18,10},{26,18},{... | collective-permute-start | bytes 2359304 | tf_op jit(solution)/shard_map/ppermute | solution.py:15
  705.3 8.2 collective-permute-start.4
  709.6 4.8 collective-permute-start.5
  710.9 5.0 copy-start.6
  715.7 12.5 copy-start.8
  718.1 105.3 %copy-start.4 = (bf16[64,2,32,256]{3,0,2,1:T(8,128)(2,1)}, bf16[64,2,32,256]{3,0,2,1:T(8,128)(2,1)S(1)}, u32[]{:S(2)}) copy-start(bf16[64,2,32,256]{3,0,2,1:T(8,128)(2,1)S(1)} %get-tuple-element.71) | copy-start | bytes 6291460
  718.1 23.3 %collective-permute-start.7 = (bf16[64,2,1,256]{3,0,2,1:T(8,128)(2,1)S(1)}, bf16[64,2,1,256]{3,0,2,1:T(8,128)(2,1)S(1)}, u32[]{:S(2)}, u32[]{:S(2)}) collective-permute-start(bf16[64,2,1,256]{3,0,2,1:T(8,128)(2,1)S(1)} %get-tuple-element.78), channel_id=1, source_target_pairs={{8,0},{16,8},{24,16},{9,1},{17,9},{25,17},{10,2},{18,10},{26,18},{... | collective-permute-start | bytes 196616 | tf_op jit(solution)/shard_map/ppermute | solution.py:15
  719.4 22.0 %collective-permute-start.6 = (bf16[64,2,1,256]{3,0,2,1:T(8,128)(2,1)S(1)}, bf16[64,2,1,256]{3,0,2,1:T(8,128)(2,1)S(1)}, u32[]{:S(2)}, u32[]{:S(2)}) collective-permute-start(bf16[64,2,1,256]{3,0,2,1:T(8,128)(2,1)S(1)} %get-tuple-element.79), channel_id=1, source_target_pairs={{0,8},{8,16},{16,24},{1,9},{9,17},{17,25},{2,10},{10,18},{18,26},{... | collective-permute-start | bytes 196616 | tf_op jit(solution)/shard_map/ppermute | solution.py:14
  743.7 53.0 %copy-start.3 = (bf16[64,2,34,258]{3,0,2,1:T(8,128)(2,1)}, bf16[64,2,34,258]{3,0,2,1:T(8,128)(2,1)S(1)}, u32[]{:S(2)}) copy-start(bf16[64,2,34,258]{3,0,2,1:T(8,128)(2,1)S(1)} %fusion.131) | copy-start | bytes 6736900
  929.5 0.8 copy-start.15
  929.5 0.8 copy-start.23
  929.5 612.6 %all-reduce.14.cloned.1.call-start = ((), (), s32[]{:S(2)}) async-start(), calls=%async_computation.4 | async-start | bytes 4096000 | tf_op jit(solution)/shard_map/psum | solution.py:214
  932.2 613.1 %all-reduce.12.cloned.1.call-start = ((), (), s32[]{:S(2)}) async-start(), calls=%async_computation.3 | async-start | bytes 2359296 | tf_op jit(solution)/shard_map/psum | solution.py:207
  999.7 24.8 %copy-start.5 = (bf16[64,2,32,256]{3,0,2,1:T(8,128)(2,1)S(1)}, bf16[64,2,32,256]{3,0,2,1:T(8,128)(2,1)}, u32[]{:S(2)}) copy-start(bf16[64,2,32,256]{3,0,2,1:T(8,128)(2,1)} %copy-done.4) | copy-start | bytes 6291460
  1108.6 11.4 copy-start.24
  1108.6 21.9 %copy-start.14 = (f32[2,512]{1,0:T(2,128)S(1)}, f32[2,512]{1,0:T(2,128)}, u32[]{:S(2)}) copy-start(f32[2,512]{1,0:T(2,128)} %copy-done.13) | copy-start | bytes 12292
  1108.6 21.9 %copy-start.17 = (f32[2,64]{1,0:T(2,128)S(1)}, f32[2,64]{1,0:T(2,128)}, u32[]{:S(2)}) copy-start(f32[2,64]{1,0:T(2,128)} %copy-done.16) | copy-start | bytes 1540
  1108.6 21.9 %copy-start.18 = (f32[64,2]{0,1:T(2,128)S(1)}, f32[64,2]{0,1:T(2,128)}, u32[]{:S(2)}) copy-start(f32[64,2]{0,1:T(2,128)} %get-tuple-element.50) | copy-start | bytes 1540
  1108.7 22.2 %copy-start.12 = (f32[64,512]{1,0:T(8,128)S(1)}, f32[64,512]{1,0:T(8,128)}, u32[]{:S(2)}) copy-start(f32[64,512]{1,0:T(8,128)} %copy-done.11) | copy-start | bytes 393220
  1120.0 366.7 %copy-start.9 = (bf16[64,2,32,256]{3,2,1,0:T(8,128)(2,1)S(1)}, bf16[64,2,32,256]{3,2,1,0:T(8,128)(2,1)}, u32[]{:S(2)}) copy-start(bf16[64,2,32,256]{3,2,1,0:T(8,128)(2,1)} %param.15) | copy-start | bytes 6291460
  1120.0 366.7 %copy-start.20 = (f32[64,2]{0,1:T(2,128)S(1)}, f32[64,2]{0,1:T(2,128)}, u32[]{:S(2)}) copy-start(f32[64,2]{0,1:T(2,128)} %copy-done.19) | copy-start | bytes 1540
  1132.3 400.4 %copy-start.21 = (bf16[2,512]{1,0:T(2,128)(2,1)S(1)}, bf16[2,512]{1,0:T(2,128)(2,1)}, u32[]{:S(2)}) copy-start(bf16[2,512]{1,0:T(2,128)(2,1)} %param.16) | copy-start | bytes 6148
  1535.3 6.8 copy-start.10
Sparse Core Ops, SparseCore 0:
  22.3 345.6 all-gather.1
  929.7 557.0 reduce-scatter.1
Sparse Core Ops, SparseCore 1:
  935.9 310.8 all-reduce.13
  1249.7 38.1 all-reduce.11
where the time goes:
time: 1570 us; the launch traced here: 1560 us
  waiting for transfers between devices  649 us (41%)
  other arithmetic  374 us (24%)
  matrix products  371 us (24%)
  local copies, waits for them, and re-layouts  68 us (4%)
  blocking collectives  46.8 us (3%)
  between operations  23.9 us (2%)
  starting transfers between devices  22.4 us (1%)
    reduce_scatter x1, waiting for transfers between devices, per_device(): lax.psum_scatter(conv_inputs(grad_extended, weight), 'chan', scatter_dime...  354 us
    all_gather x1, waiting for transfers between devices, per_device(): gathered = lax.all_gather(extended, 'chan', axis=0, tiled=True)  290 us
    dot_general x9, matrix products, conv_inputs(): jnp.einsum('oi,obrw->ibrw', kernel[tap_row, tap_col], padded[:, :, 2 - ta...  199 us
    another operation x6, other arithmetic, up_taps(): return jnp.stack(parities, axis=dim_at)  155 us
    add x2, other arithmetic, down_taps(): summed = addend if summed is None else summed + addend  96.3 us
    dot_general x9, matrix products, conv_weight(): jnp.einsum('obrw,ibrw->oi', grad_rows, padded[:, :, tap_row:tap_row + row...  95.5 us
    dot_general x9, matrix products, conv_forward(): jnp.einsum('oi,ibrw->obrw', kernel[tap_row, tap_col], padded[:, :, tap_ro...  71.5 us
    another operation x1, other arithmetic  46.9 us
  transfers between devices with their start and end apart: 12, of which 4 were waited for; matrix products, arithmetic and copies ran while one was open for 19% of the time, Pallas kernels for 0%

commit v1 on v0

v1 whole, which is shorter than its diff:
```python
import functools

import jax
import jax.numpy as jnp
import ml_dtypes
import numpy as np
from jax import lax
from jax.experimental import pallas as pl
from jax.experimental.pallas import tpu as pltpu
from jax.sharding import PartitionSpec as P

F32 = jnp.float32
BF16 = jnp.bfloat16
IN_VMEM = pl.BlockSpec(memory_space=pltpu.VMEM)
IN_SMEM = pl.BlockSpec(memory_space=pltpu.SMEM)
PARAMS = pltpu.CompilerParams(vmem_limit_bytes=56 << 20)
RIM = 6
GROUP = 16


def struct(shape, dtype):
    return jax.ShapeDtypeStruct(shape, dtype)


def sinc_taps():
    offset = np.arange(12) - 5.5
    values = np.sinc(offset * 0.5) * (0.5 + 0.5 * np.cos(np.pi * offset / 6.0))
    return values / values.sum()


def up_table(size):
    tap = np.arange(2 * size)[None, :] - 2 * np.arange(size)[:, None] + 5
    held = (tap >= 0) & (tap < 12)
    return np.where(held, 2.0 * sinc_taps()[np.clip(tap, 0, 11)], 0.0).astype(np.float32)


def halves(table):
    high = table.astype(ml_dtypes.bfloat16)
    return high, (table - high.astype(np.float32)).astype(ml_dtypes.bfloat16)


def from_neighbours(value, axis, dim, width):
    size, length = lax.axis_size(axis), value.shape[dim]
    up = [(i, i + 1) for i in range(size - 1)]
    down = [(j, i) for i, j in up]
    last = lax.slice_in_dim(value, length - width, length, axis=dim)
    first = lax.slice_in_dim(value, 0, width, axis=dim)
    return lax.ppermute(last, axis, up), lax.ppermute(first, axis, down)


def exchange(parts, axis):
    size = lax.axis_size(axis)
    return [parts[0]] + [
        lax.ppermute(parts[x], axis, [(i, i ^ x) for i in range(size)]) for x in range(1, size)
    ]


def row_parts(rows, me, blocks, span, halo):
    parts = []
    for x in range(lax.axis_size("chan")):
        dest = me ^ x
        part = lax.dynamic_slice(
            rows,
            (dest // blocks, (dest % blocks) * span, 0, 0),
            (1, span + halo, rows.shape[2], rows.shape[3]),
        )
        parts.append(part[0])
    return parts


def fill_shifted(me, parts, scales, shifted, count):
    split = len(parts) // count
    for h in range(split):
        for x in range(count):
            part = parts[h * count + x]
            rows, width, columns = part.shape
            source = me ^ x
            spot = pl.ds(h * width, width)
            column = lax.broadcasted_iota(jnp.int32, (width, columns), 1)
            scale = None if scales is None else scales[source]

            def row_step(row, carry, part=part, source=source, spot=spot, column=column, scale=scale):
                value = part[row].astype(F32)
                if scale is not None:
                    value = (value * scale).astype(BF16).astype(F32)
                before = jnp.where(column == 0, 0.0, pltpu.roll(value, 1, 1))
                after = jnp.where(column == columns - 1, 0.0, pltpu.roll(value, columns - 1, 1))
                shifted[row, 0, source, spot] = before.astype(BF16)
                shifted[row, 1, source, spot] = value.astype(BF16)
                shifted[row, 2, source, spot] = after.astype(BF16)
                return carry

            lax.fori_loop(0, rows, row_step, 0)


def convolved(taps, shifted, row, channels, columns):
    total = None
    for i in range(3):
        for j in range(3):
            term = jnp.dot(
                taps[3 * i + j],
                shifted[row + i, j].reshape(channels, columns),
                preferred_element_type=F32,
            )
            total = term if total is None else total + term
    return total


def forward_kernel(count, split, me_ref, taps, scales, *refs):
    parts, outs = refs[:count], refs[count : count + split * count]
    shifted, sums = refs[-2:]
    me = me_ref[0]
    _, _, _, own, columns = shifted.shape
    width = own // split
    fill_shifted(me, parts, scales, shifted, count)

    def row_step(row, carry):
        total = convolved(taps, shifted, row, count * own, columns)
        sums[...] = total.astype(BF16).reshape(sums.shape)
        for h in range(split):
            for x in range(count):
                outs[h * count + x][row] = sums[me ^ x, h * width : (h + 1) * width]
        return carry

    lax.fori_loop(0, outs[0].shape[0], row_step, 0)


def conv_forward(me, taps, scales, parts, split):
    count = len(parts)
    rows, own, columns = parts[0].shape
    outs = pl.pallas_call(
        functools.partial(forward_kernel, count, split),
        out_shape=[struct((rows - 2, own // split, columns), BF16)] * (count * split),
        in_specs=[IN_SMEM] + [IN_VMEM] * (2 + count),
        out_specs=[IN_VMEM] * (count * split),
        scratch_shapes=[
            pltpu.VMEM((rows, 3, count, own, columns), BF16),
            pltpu.VMEM((count, own, columns), BF16),
        ],
        compiler_params=PARAMS,
        name="conv_forward",
    )(me, taps, scales, *parts)
    return [outs[h * count : (h + 1) * count] for h in range(split)]


def backward_kernel(count, split, me_ref, taps, *refs):
    grads, feats = refs[: count * split], refs[count * split : count * (split + 1)]
    outs = refs[count * (split + 1) : count * (split + 2)]
    style_ref, shifted, sums = refs[count * (split + 2) :]
    me = me_ref[0]
    _, _, _, own, columns = shifted.shape
    fill_shifted(me, grads, None, shifted, count)
    style_ref[...] = jnp.zeros_like(style_ref)

    def row_step(row, carry):
        total = convolved(taps, shifted, row, count * own, columns)
        sums[...] = total.reshape(sums.shape)
        for x in range(count):
            value = sums[me ^ x]
            outs[x][row] = value.astype(BF16)
            product = value * feats[x][row + 1].astype(F32)
            style_ref[me ^ x] += jnp.sum(product, axis=1, keepdims=True)
        return carry

    lax.fori_loop(0, outs[0].shape[0], row_step, 0)


def conv_backward(me, taps, grads, feats):
    count = len(feats)
    split = len(grads) // count
    rows, own, columns = feats[0].shape
    outs = pl.pallas_call(
        functools.partial(backward_kernel, count, split),
        out_shape=[struct((rows - 2, own, columns), BF16)] * count + [struct((count, own, 1), F32)],
        in_specs=[IN_SMEM] + [IN_VMEM] * (1 + len(grads) + count),
        out_specs=[IN_VMEM] * (count + 1),
        scratch_shapes=[
            pltpu.VMEM((rows, 3, count, own, columns), BF16),
            pltpu.VMEM((count, own, columns), F32),
        ],
        compiler_params=PARAMS,
        name="conv_backward",
    )(me, taps, *grads, *feats)
    return outs[:-1], outs[-1]


def weight_kernel(count, split, me_ref, scales, *refs):
    grads, feats = refs[: count * split], refs[count * split : count * (split + 1)]
    out, shifted, rows_ref = refs[count * (split + 1) :]
    me = me_ref[0]
    rows, _, _, own, columns = shifted.shape
    width = own // split
    channels = count * own
    fill_shifted(me, feats, scales, shifted, count)
    for h in range(split):
        for x in range(count):
            rows_ref[:, me ^ x, h * width : (h + 1) * width] = grads[h * count + x][1 : rows - 1]

    def tap_step(tap, carry):
        i, j = lax.div(tap, 3), lax.rem(tap, 3)
        total = None
        for row in range(rows - 2):
            term = lax.dot_general(
                rows_ref[row].reshape(channels, columns),
                shifted[row + i, j].reshape(channels, columns),
                (((1,), (1,)), ((), ())),
                preferred_element_type=F32,
            )
            total = term if total is None else total + term
        out[tap] = total.astype(BF16)
        return carry

    lax.fori_loop(0, 9, tap_step, 0)


def conv_weight(me, scales, grads, feats):
    count = len(feats)
    split = len(grads) // count
    rows, own, columns = feats[0].shape
    return pl.pallas_call(
        functools.partial(weight_kernel, count, split),
        out_shape=struct((9, count * own, count * own), BF16),
        in_specs=[IN_SMEM] + [IN_VMEM] * (1 + len(grads) + count),
        out_specs=IN_VMEM,
        scratch_shapes=[
            pltpu.VMEM((rows, 3, count, own, columns), BF16),
            pltpu.VMEM((rows - 2, count, own, columns), BF16),
        ],
        compiler_params=PARAMS,
        name="conv_weight",
    )(me, scales, *grads, *feats)


def gather_kernel(count, me_ref, *refs):
    parts, (out, first, last) = refs[:count], refs[count:]
    me = me_ref[0]
    items, rows, _, _ = out.shape
    blocks = count // items
    span = rows // blocks
    for x in range(count):
        source = me ^ x
        out[source // blocks, pl.ds((source % blocks) * span, span)] = parts[x][...]
    first[...] = out[:, :RIM]
    last[...] = out[:, rows - RIM :]


def gather_rows(me, parts, items):
    count = len(parts)
    span, width, columns = parts[0].shape
    rows = span * count // items
    rim = struct((items, RIM, width, columns), BF16)
    return pl.pallas_call(
        functools.partial(gather_kernel, count),
        out_shape=[struct((items, rows, width, columns), BF16), rim, rim],
        in_specs=[IN_SMEM] + [IN_VMEM] * count,
        out_specs=[IN_VMEM] * 3,
        compiler_params=PARAMS,
        name="gather_rows",
    )(me, *parts)


def sinc_kernel(
    edge_ref,
    raw,
    before,
    after,
    cotangent,
    demod,
    bias,
    up_high,
    up_low,
    down_high,
    down_low,
    up_sums,
    out,
    grad_raw,
    grad_bias,
    grad_demod,
    wide,
    wide_grad,
    narrow,
    narrow_grad,
):
    items, rows, width, columns = raw.shape
    extent = rows + 2 * RIM
    first, last = edge_ref[0], edge_ref[1]
    tap = [float(value) for value in sinc_taps()[:6]]
    lane_tiles = 2 * columns // 128

    def widened(values):
        flat = values.reshape(-1, columns)
        total = jnp.dot(flat, up_high[...], preferred_element_type=F32)
        total = total + jnp.dot(flat, up_low[...], preferred_element_type=F32)
        return total.reshape(-1, GROUP, 2 * columns)

    def narrowed(values):
        flat = values.reshape(rows * GROUP, 2 * columns)
        high = flat.astype(BF16)
        low = (flat - high.astype(F32)).astype(BF16)
        total = jnp.dot(high, down_high[...], preferred_element_type=F32)
        total = total + jnp.dot(high, down_low[...], preferred_element_type=F32)
        total = total + jnp.dot(low, down_high[...], preferred_element_type=F32)
        return total.reshape(rows, GROUP, columns)

    def tile_step(index, carry):
        lanes = pl.ds(pl.multiple_of(lax.rem(index, lane_tiles) * 128, 128), 128)
        subs = pl.ds(pl.multiple_of(lax.div(index, lane_tiles) * 8, 8), 8)
        sums, picked = [{}, {}], [{}, {}]
        for row in range(extent):
            for which, ref in ((0, wide), (1, wide_grad)):
                value = ref[row, subs, lanes]
                products = [value * (2.0 * tap[t]) for t in range(6)]
                for offset in range(-3, 4):
                    pair = row - RIM + offset
                    for parity in range(2):
                        t = 2 * offset + parity + 5
                        if -3 <= pair < rows + 3 and 0 <= t < 12:
                            term = products[min(t, 11 - t)]
                            key = 2 * pair + parity
                            sums[which][key] = sums[which][key] + term if key in sums[which] else term
            pair = row - RIM - 3
            if pair < -3:
                continue
            for key in (2 * pair, 2 * pair + 1):
                value, grad = sums[0].pop(key), sums[1].pop(key)
                sigmoid = 1.0 / (1.0 + jnp.exp(-value))
                active = value * sigmoid
                grad = grad * (sigmoid + active * (1.0 - sigmoid))
                if pair < 0:
                    active, grad = active * first, grad * first
                if pair >= rows:
                    active, grad = active * last, grad * last
                picked[0][key], picked[1][key] = active, grad
            centre = pair - 3
            if centre >= 0:
                for which, ref in ((0, narrow), (1, narrow_grad)):
                    store = picked[which]
                    total = None
                    for t in range(6):
                        term = tap[t] * (store[2 * centre + t - 5] + store[2 * centre + 6 - t])
                        total = term if total is None else total + term
                    ref[centre, subs, lanes] = total
                    store.pop(2 * centre - 5)
                    store.pop(2 * centre - 4)
        return carry

    for item in range(items):
        for group in range(width // GROUP):
            at = slice(group * GROUP, (group + 1) * GROUP)
            scale = demod[item, at]
            shift = bias[at] * up_sums[...]
            wide[:RIM] = widened(before[item, :, at]) * scale + shift * first
            wide[RIM : RIM + rows] = widened(raw[item, :, at]) * scale + shift
            wide[RIM + rows :] = widened(after[item, :, at]) * scale + shift * last
            wide_grad[...] = widened(cotangent[item, :, at])
            lax.fori_loop(0, GROUP // 8 * lane_tiles, tile_step, 0)
            result = narrowed(narrow[...])
            out[at, item] = jnp.swapaxes(result, 0, 1).astype(BF16)
            grad = narrowed(narrow_grad[...])
            grad_raw[item, :, at] = (grad * scale).astype(BF16)
            own = raw[item, :, at].astype(F32)
            grad_bias[item, at] = jnp.sum(jnp.sum(grad, axis=0), axis=1, keepdims=True)
            grad_demod[item, at] = jnp.sum(jnp.sum(grad * own, axis=0), axis=1, keepdims=True)


def sinc_both(edges, raw, before, after, cotangent, demod, bias, tables):
    items, rows, width, columns = raw.shape
    wide = pltpu.VMEM((rows + 2 * RIM, GROUP, 2 * columns), F32)
    narrow = pltpu.VMEM((rows, GROUP, 2 * columns), F32)
    return pl.pallas_call(
        sinc_kernel,
        out_shape=[
            struct((width, items, rows, columns), BF16),
            struct((items, rows, width, columns), BF16),
            struct((items, width, 1), F32),
            struct((items, width, 1), F32),
        ],
        in_specs=[IN_SMEM] + [IN_VMEM] * 11,
        out_specs=[IN_VMEM] * 4,
        scratch_shapes=[wide, wide, narrow, narrow],
        compiler_params=PARAMS,
        name="sinc_both",
    )(edges, raw, before, after, cotangent, demod, bias, *tables)


def scale_kernel(count, me_ref, scales, *refs):
    parts, (out, gathered) = refs[:count], refs[count:]
    me = me_ref[0]
    width, items, rows, columns = out.shape
    blocks = count // items
    span = rows // blocks
    for x in range(count):
        source = me ^ x
        gathered[source // blocks, pl.ds((source % blocks) * span, span)] = parts[x][...]
    for item in range(items):
        for group in range(width // GROUP):
            at = slice(group * GROUP, (group + 1) * GROUP)
            value = gathered[item, :, at].astype(F32) * scales[item, at]
            out[at, item] = jnp.swapaxes(value, 0, 1)


def scaled(me, scales, parts, items):
    count = len(parts)
    span, width, columns = parts[0].shape
    rows = span * count // items
    return pl.pallas_call(
        functools.partial(scale_kernel, count),
        out_shape=struct((width, items, rows, columns), F32),
        in_specs=[IN_SMEM] + [IN_VMEM] * (1 + count),
        out_specs=IN_VMEM,
        scratch_shapes=[pltpu.VMEM((items, rows, width, columns), BF16)],
        compiler_params=PARAMS,
        name="scale_features",
    )(me, scales, *parts)


def summed_over_dp(values, me):
    bit = 1
    while bit < lax.axis_size("dp"):
        pairs = values.reshape((values.shape[0] // 2, 2) + values.shape[1:])
        side = (me // bit) % 2
        keep = lax.dynamic_index_in_dim(pairs, side, 1, keepdims=False)
        send = lax.dynamic_index_in_dim(pairs, 1 - side, 1, keepdims=False)
        got = lax.ppermute(send, "dp", [(i, i ^ bit) for i in range(lax.axis_size("dp"))])
        values = (keep.astype(F32) + got.astype(F32)).astype(BF16)
        bit *= 2
    return values[0]


def per_device(
    features,
    latent,
    affine,
    affine_bias,
    weight,
    out_bias,
    cotangent,
    latents_all,
    labels,
    class_means,
):
    highest = lax.Precision.HIGHEST
    own, items, rows, columns = features.shape
    channels = weight.shape[3]
    count = lax.axis_size("chan")
    dp_total = lax.axis_size("dp")
    me = lax.axis_index("chan")
    me_dp = lax.axis_index("dp")
    me_ref = me.astype(jnp.int32)[None]
    blocks = count // items
    span = rows // blocks
    split = max(1, min(2, own // GROUP))
    width = own // split

    before, after = from_neighbours(features, "dp", 2, 1)
    extended = jnp.transpose(jnp.concatenate([before, features, after], axis=2), (1, 2, 0, 3))
    feats = exchange(row_parts(extended, me, blocks, span, 2), "chan")
    gathered = lax.all_gather(weight, "chan", axis=2, tiled=True)
    taps_forward = gathered.reshape(9, channels, channels)
    taps_backward = jnp.transpose(gathered[::-1, ::-1], (0, 1, 3, 2)).reshape(9, channels, channels)

    styles = jnp.dot(latent, affine, preferred_element_type=F32) + affine_bias
    own_style = lax.dynamic_slice_in_dim(styles, me * own, own, 1)
    weight_full = weight.astype(F32)
    weight_sq = jnp.sum(weight_full * weight_full, axis=(0, 1))
    demod = lax.rsqrt(jnp.dot(styles * styles, weight_sq.T, precision=highest) + 1e-08)
    item = me // blocks
    item_scales = lax.dynamic_index_in_dim(styles, item, 0, keepdims=False).reshape(count, own, 1)

    cot_before, cot_after = from_neighbours(cotangent, "dp", 2, RIM)
    cot = jnp.transpose(jnp.concatenate([cot_before, cotangent, cot_after], axis=2), (1, 2, 0, 3))
    table = up_table(columns)
    tables = halves(table) + halves(0.5 * table.T) + (np.sum(table, axis=0)[None],)
    edges = jnp.stack([me_dp > 0, me_dp < dp_total - 1]).astype(F32)

    raw_parts = conv_forward(me_ref, taps_forward, item_scales, feats, split)
    results, grad_parts, bias_parts, demod_parts = [], [], [], []
    for h in range(split):
        at = slice(h * width, (h + 1) * width)
        raw, head, tail = gather_rows(me_ref, exchange(raw_parts[h], "chan"), items)
        size = dp_total
        up = [(i, i + 1) for i in range(size - 1)]
        before = lax.ppermute(tail, "dp", up)
        after = lax.ppermute(head, "dp", [(j, i) for i, j in up])
        result, grad_raw, bias_part, demod_part = sinc_both(
            edges,
            raw,
            before,
            after,
            cot[:, :, at],
            demod[:, at, None],
            out_bias[at, None],
            tables,
        )
        results.append(result)
        bias_parts.append(bias_part)
        demod_parts.append(demod_part)
        before, after = from_neighbours(grad_raw, "dp", 1, 1)
        grad_extended = jnp.concatenate([before, grad_raw, after], axis=1)
        grad_parts += exchange(row_parts(grad_extended, me, blocks, span, 2), "chan")
    output = jnp.concatenate(results, axis=0)
    bias_part = jnp.sum(jnp.concatenate(bias_parts, axis=1)[:, :, 0], axis=0)
    g_demod = jnp.concatenate(demod_parts, axis=1)[:, :, 0]

    modded_parts, style_part = conv_backward(me_ref, taps_backward, grad_parts, feats)
    modded_parts = exchange(modded_parts, "chan")
    grad_features = scaled(me_ref, own_style[:, :, None], modded_parts, items)

    grad_bias, g_demod_sum = lax.psum((bias_part, g_demod), "dp")
    cube = demod * demod * demod
    g_style_part = 2.0 * styles * jnp.dot(-0.5 * g_demod * cube, weight_sq, precision=highest)
    g_style_part = g_style_part + jnp.where(
        jnp.arange(items)[:, None] == item, style_part.reshape(1, channels), 0.0
    )
    g_wsq = jnp.dot((-0.5 * g_demod_sum * cube).T, styles * styles, precision=highest)

    g_weight = conv_weight(me_ref, item_scales, grad_parts, feats)
    share = channels // dp_total
    g_weight = jnp.moveaxis(g_weight.reshape(9, count, own, dp_total, share), 3, 0)
    g_weight = summed_over_dp(g_weight, me_dp)
    sent = [lax.dynamic_index_in_dim(g_weight, me ^ x, 1, keepdims=False) for x in range(count)]
    g_weight = sum(part.astype(F32) for part in exchange(sent, "chan"))
    g_weight = lax.all_gather(g_weight, "dp", axis=2, tiled=True).reshape(weight.shape)
    grad_weight = g_weight + 2.0 * weight_full * g_wsq

    all_latents = lax.all_gather(latents_all, ("dp", "chan"), axis=0, tiled=True)
    all_labels = lax.all_gather(labels, ("dp", "chan"), axis=0, tiled=True)
    one_hot = all_labels[None, :] == jnp.arange(class_means.shape[0])[:, None]
    class_sums = jnp.dot(one_hot.astype(BF16), all_latents, preferred_element_type=F32)
    counts = jnp.sum(one_hot.astype(F32), axis=1)
    target = jnp.where(
        counts[:, None] > 0, class_sums / jnp.maximum(counts, 1.0)[:, None], class_means
    )

    g_style = lax.psum(g_style_part, ("dp", "chan"))
    grad_affine_bias = jnp.sum(g_style, axis=0)
    grad_affine = jnp.dot(latent.astype(F32).T, g_style, precision=highest)
    grad_latent = jnp.dot(g_style, affine.astype(F32).T, precision=highest)
    return (
        output,
        grad_features,
        grad_latent,
        grad_affine,
        grad_affine_bias,
        grad_weight,
        grad_bias,
        target,
    )


def solution(mesh):
    in_specs = (
        P("chan", None, "dp", None),
        P(),
        P(),
        P(),
        P(None, None, "chan", None),
        P("chan"),
        P("chan", None, "dp", None),
        P(("dp", "chan"), None),
        P(("dp", "chan")),
        P(),
    )
    out_specs = (
        P("chan", None, "dp", None),
        P("chan", None, "dp", None),
        P(),
        P(),
        P(),
        P(None, None, "chan", None),
        P("chan"),
        P(),
    )
    return jax.shard_map(
        per_device, mesh=mesh, in_specs=in_specs, out_specs=out_specs, check_vma=False
    )
```

time: 1570 us -> 673 us (0.43)
  the two profiles are of different devices: /device:TPU:0 before, /device:TPU:8 now
where the time goes in v1:
time: 673 us; the launch traced here: 665 us
  waiting for transfers between devices  200 us (30%)
  Pallas kernels  149 us (22%)
  blocking collectives  110 us (16%)
  starting transfers between devices  103 us (15%)
  local copies, waits for them, and re-layouts  61 us (9%)
  between operations  17.2 us (3%)
  other arithmetic  16.4 us (2%)
  matrix products  8.43 us (1%)
    ppermute x49, waiting for transfers between devices, exchange(): lax.ppermute(parts[x], axis, [(i, i ^ x) for i in range(size)])  193 us
    ppermute x49, starting transfers between devices, exchange(): lax.ppermute(parts[x], axis, [(i, i ^ x) for i in range(size)])  77.5 us
    unnamed x1, blocking collectives  61.7 us
    pallas_call x2, Pallas kernels, sinc_both(): pl.pallas_call(sinc_kernel, out_shape=[struct((width, items, rows, column...  50.5 us
    psum x1, blocking collectives, per_device(): g_style = lax.psum(g_style_part, ('dp', 'chan'))  41.3 us
    pallas_call x1, Pallas kernels, conv_backward(): pl.pallas_call(functools.partial(backward_kernel, count, split), out_shap...  30.6 us
    pallas_call x1, Pallas kernels, conv_weight(): pl.pallas_call(functools.partial(weight_kernel, count, split), out_shape=...  29.5 us
    pallas_call x1, Pallas kernels, conv_forward(): pl.pallas_call(functools.partial(forward_kernel, count, split), out_shape...  28.5 us
  transfers between devices with their start and end apart: 66, of which 28 were waited for; matrix products, arithmetic and copies ran while one was open for 9% of the time, Pallas kernels for 18%

profile of v1, /device:TPU:8, one launch (start us, length us, event | category | flops | bytes accessed | tf_op | source)
XLA Modules:
  0.0 664.9 jit_solution(1329718705439808589)
XLA Ops:
  21.1 3.0 copy.80
  30.5 3.0 collective-permute-done.2.refs_1_.refs_17_
  35.1 20.8 %collective-permute-done.3.refs_2_.refs_18_ = bf16[10,64,256]{2,1,0:T(8,128)(2,1)} collective-permute-done((bf16[10,64,256]{2,1,0:T(8,128)(2,1)}, bf16[10,64,256]{2,1,0:T(8,128)(2,1)}, u32[]{:S(2)}, u32[]{:S(2)}) %collective-permute-start.3) | collective-permute-done | bytes 327712 | tf_op jit(solution)/shard_map/ppermute | solution.py:54
  56.9 10.9 %collective-permute-done.4.refs_3_.refs_19_ = bf16[10,64,256]{2,1,0:T(8,128)(2,1)} collective-permute-done((bf16[10,64,256]{2,1,0:T(8,128)(2,1)S(1)}, bf16[10,64,256]{2,1,0:T(8,128)(2,1)}, u32[]{:S(2)}, u32[]{:S(2)}) %collective-permute-start.4) | collective-permute-done | bytes 327712 | tf_op jit(solution)/shard_map/ppermute | solution.py:54
  69.0 3.9 collective-permute-start.18
  73.1 6.7 %collective-permute-done.6.refs_5_.refs_21_ = bf16[10,64,256]{2,1,0:T(8,128)(2,1)} collective-permute-done((bf16[10,64,256]{2,1,0:T(8,128)(2,1)S(1)}, bf16[10,64,256]{2,1,0:T(8,128)(2,1)}, u32[]{:S(2)}, u32[]{:S(2)}) %collective-permute-start.6) | collective-permute-done | bytes 327712 | tf_op jit(solution)/shard_map/ppermute | solution.py:54
  79.8 31.6 %collective-permute-done.7.refs_6_.refs_22_ = bf16[10,64,256]{2,1,0:T(8,128)(2,1)} collective-permute-done((bf16[10,64,256]{2,1,0:T(8,128)(2,1)S(1)}, bf16[10,64,256]{2,1,0:T(8,128)(2,1)}, u32[]{:S(2)}, u32[]{:S(2)}) %collective-permute-start.7) | collective-permute-done | bytes 327712 | tf_op jit(solution)/shard_map/ppermute | solution.py:54
  111.4 23.0 %collective-permute-done.8.refs_7_.refs_23_ = bf16[10,64,256]{2,1,0:T(8,128)(2,1)} collective-permute-done((bf16[10,64,256]{2,1,0:T(8,128)(2,1)S(1)}, bf16[10,64,256]{2,1,0:T(8,128)(2,1)}, u32[]{:S(2)}, u32[]{:S(2)}) %collective-permute-start.8) | collective-permute-done | bytes 327712 | tf_op jit(solution)/shard_map/ppermute | solution.py:54
  136.1 28.5 %conv_forward.1 = (bf16[8,32,256]{2,1,0:T(8,128)(2,1)}, bf16[8,32,256]{2,1,0:T(8,128)(2,1)}, bf16[8,32,256]{2,1,0:T(8,128)(2,1)}, bf16[8,32,256]{2,1,0:T(8,128)(...) custom-call(s32[1]{0:T(128)} %bitcast.2.me_ref, ...), custom_call_target="tpu_custom_call" | custom-call | tf_op jit(solution)/shard_map/conv_forward/pallas_call | solution.py:131
  166.4 3.3 collective-permute-start.10
  184.1 4.4 collective-permute-start.22
  188.5 4.5 collective-permute-start.23
  193.0 4.7 collective-permute-start.15
  199.2 3.4 collective-permute-done.15.refs_7_
  212.8 4.5 collective-permute-done.25.refs_6_
  217.3 3.2 collective-permute-done.26.refs_7_
  227.2 25.2 %sinc_both.2 = (bf16[32,2,32,256]{3,2,1,0:T(8,128)(2,1)}, bf16[2,32,32,256]{3,2,1,0:T(8,128)(2,1)}, f32[2,32,1]{2,1,0:T(8,128)}, f32[2,32,1]{2,1,0:T(8,128)}) custom-call(f32[2]{0:T(128)} %add_convert_fusion.1.edge_ref, bf16[2,32,32,256]{3,2,1,0:T(8,128)(2,1)} %get-tuple-element.55.raw, bf16[2,6,32,256]{3,2,1,0:T(8,128)(2,1)} %copy-done.32, ...), custom_call_target="tpu_custom_call" | custom-call | tf_op jit(solution)/shard_map/sinc_both/pallas_call | solution.py:370
  253.2 4.2 collective-permute-start.29
  259.6 25.2 %sinc_both.3 = (bf16[32,2,32,256]{3,2,1,0:T(8,128)(2,1)}, bf16[2,32,32,256]{3,2,1,0:T(8,128)(2,1)}, f32[2,32,1]{2,1,0:T(8,128)}, f32[2,32,1]{2,1,0:T(8,128)}) custom-call(f32[2]{0:T(128)} %add_convert_fusion.1.edge_ref, bf16[2,32,32,256]{3,2,1,0:T(8,128)(2,1)} %get-tuple-element.67.raw, bf16[2,6,32,256]{3,2,1,0:T(8,128)(2,1)} %copy-done.33, ...), custom_call_target="tpu_custom_call" | custom-call | tf_op jit(solution)/shard_map/sinc_both/pallas_call | solution.py:370
  285.6 4.2 collective-permute-start.38
  293.0 2.9 collective-permute-start.33
  302.9 2.8 collective-permute-done.33.refs_3_
  309.7 7.8 %collective-permute-done.35.refs_5_ = bf16[10,32,256]{2,1,0:T(8,128)(2,1)S(1)} collective-permute-done((bf16[10,32,256]{2,1,0:T(8,128)(2,1)S(1)}, bf16[10,32,256]{2,1,0:T(8,128)(2,1)S(1)}, u32[]{:S(2)}, u32[]{:S(2)}) %collective-permute-start.35) | collective-permute-done | bytes 163872 | tf_op jit(solution)/shard_map/ppermute | solution.py:54
  317.5 4.2 collective-permute-start.42
  322.8 7.3 %collective-permute-done.37.refs_7_ = bf16[10,32,256]{2,1,0:T(8,128)(2,1)S(1)} collective-permute-done((bf16[10,32,256]{2,1,0:T(8,128)(2,1)S(1)}, bf16[10,32,256]{2,1,0:T(8,128)(2,1)S(1)}, u32[]{:S(2)}, u32[]{:S(2)}) %collective-permute-start.37) | collective-permute-done | bytes 163872 | tf_op jit(solution)/shard_map/ppermute | solution.py:54
  331.8 12.1 %collective-permute-done.43.refs_12_ = bf16[10,32,256]{2,1,0:T(8,128)(2,1)S(1)} collective-permute-done((bf16[10,32,256]{2,1,0:T(8,128)(2,1)}, bf16[10,32,256]{2,1,0:T(8,128)(2,1)S(1)}, u32[]{:S(2)}, u32[]{:S(2)}) %collective-permute-start.43) | collective-permute-done | bytes 163872 | tf_op jit(solution)/shard_map/ppermute | solution.py:54
  343.9 3.7 collective-permute-done.44.refs_13_
  347.6 4.8 collective-permute-done.45.refs_14_
  352.4 4.6 collective-permute-done.46.refs_15_
  357.6 29.5 %conv_weight.1 = bf16[9,512,512]{2,1,0:T(8,128)(2,1)} custom-call(s32[1]{0:T(128)} %bitcast.2.me_ref, f32[8,64,1]{2,1,0:T(8,128)} %reshape.89.scales, bf16[10,32,256]{2,1,0:T(8,128)(2,1)} %get-tuple-element.158.refs_0_, bf16[10,32,256]{2,1,0:T(8,128)(2,1)} %copy-done.9, bf16[10,32,256]{2,1,0:T(8,128)(2,1)} %copy-done.10, bf16[10,32,256]{2,1,0:T(8,128)(2,1)} %copy-done.11, ...), custom_call_target="tpu_custom_call" | custom-call | tf_op jit(solution)/shard_map/conv_weight/pallas_call | solution.py:220
  387.1 7.7 %reshape.82 = bf16[9,8,64,4,128]{4,3,2,1,0:T(4,128)(2,1)} reshape(bf16[9,512,512]{2,1,0:T(8,128)(2,1)} %conv_weight.1) | data formatting | bytes 9437184 | tf_op jit(solution)/shard_map/reshape | solution.py:519
  394.8 13.6 %constant_dynamic-slice_fusion.2 = (bf16[2,1,9,8,64,128]{5,1,0,4,3,2:T(2,128)(2,1)}, bf16[2,1,9,8,64,128]{5,1,0,4,3,2:T(2,128)(2,1)S(1)}) fusion(bf16[2,2,9,8,64,128]{5,1,0,4,3,2:T(2,128)(2,1)} %bitcast.125, s32[]{:T(128)S(6)} %select_n.288, s32[]{:T(128)S(6)} %select_n.289), kind=kLoop, calls=%fused_computation.73 | loop fusion | bytes 9437192 | tf_op jit(solution)/shard_map/jit(dynamic_index_in_dim)/dynamic_slice | solution.py:422
  409.4 4.4 collective-permute-done.54
  413.8 4.0 fusion.1
  419.6 61.7 %all-reduce = s32[2048]{0:T(1024)S(1)} all-reduce(s32[2048]{0:T(1024)S(1)} %dynamic-update-slice), channel_id=1, replica_groups=mesh['dp'=4,'chan'=8] {'dp','chan'}, use_global_device_ids=true, to_apply=%add | all-reduce | flops 2048 | bytes 16384
  491.2 2.8 collective-permute-start.58
  494.1 10.7 %collective-permute-done.62 = bf16[9,64,128]{2,1,0:T(8,128)(2,1)S(1)} collective-permute-done((bf16[9,64,128]{2,1,0:T(8,128)(2,1)S(1)}, bf16[9,64,128]{2,1,0:T(8,128)(2,1)S(1)}, u32[]{:S(2)}, u32[]{:S(2)}) %collective-permute-start.62) | collective-permute-done | bytes 147488 | tf_op jit(solution)/shard_map/ppermute | solution.py:54
  504.8 2.8 collective-permute-done.61
  510.0 3.0 collective-permute-done.59
  515.7 5.8 divide_select_fusion
  521.5 5.0 reverse_bitcast_fusion
  526.5 6.7 %copy.87 = bf16[3,3,512,512]{3,2,1,0:T(8,128)(2,1)} copy(bf16[3,3,512,512]{2,3,1,0:T(8,128)(2,1)} %reverse_bitcast_fusion) | data formatting | bytes 9437184 | tf_op jit(solution)/shard_map/transpose | solution.py:460
  533.7 7.5 %all-reduce.1 = (f32[2,64]{1,0:T(2,128)S(1)}, f32[64]{0:T(128)}) all-reduce(f32[2,64]{1,0:T(2,128)S(1)} %maximum_bitcast_fusion.1, f32[64]{0:T(128)S(1)} %maximum_reduce_fusion), channel_id=1, replica_groups=mesh['dp'=4,'chan'=8] {'dp'}, use_global_device_ids=true, to_apply=%region_3.4 | all-reduce | flops 192 | bytes 1536 | tf_op jit(solution)/shard_map/psum | solution.py:509
  541.5 30.6 %conv_backward.1 = (bf16[8,64,256]{2,1,0:T(8,128)(2,1)}, bf16[8,64,256]{2,1,0:T(8,128)(2,1)}, bf16[8,64,256]{2,1,0:T(8,128)(2,1)}, bf16[8,64,256]{2,1,0:T(8,128)...) custom-call(s32[1]{0:T(128)} %bitcast.2.me_ref, ...), custom_call_target="tpu_custom_call" | custom-call | tf_op jit(solution)/shard_map/conv_backward/pallas_call | solution.py:172
  582.0 41.3 %psum.21 = f32[2,512]{1,0:T(2,128)S(1)} all-reduce(f32[2,512]{1,0:T(2,128)S(1)} %fusion.5), channel_id=1, replica_groups=mesh['dp'=4,'chan'=8] {'dp','chan'}, use_global_device_ids=true, to_apply=%region_1.2 | all-reduce | flops 1024 | bytes 8192 | tf_op jit(solution)/shard_map/psum | solution.py:535
  630.7 13.3 %collective-permute-done.52.refs_6_ = bf16[8,64,256]{2,1,0:T(8,128)(2,1)S(1)} collective-permute-done((bf16[8,64,256]{2,1,0:T(8,128)(2,1)}, bf16[8,64,256]{2,1,0:T(8,128)(2,1)S(1)}, u32[]{:S(2)}, u32[]{:S(2)}) %collective-permute-start.52) | collective-permute-done | bytes 262176 | tf_op jit(solution)/shard_map/ppermute | solution.py:54
  644.0 5.6 collective-permute-done.53.refs_7_
  649.6 4.8 scale_features.1
  (280 shorter events, 118.5 us)
Async XLA Ops:
  8.0 128.1 %all-gather.4.cloned.1.call-start = ((), (), s32[]{:S(2)}) async-start(), calls=%async_computation | async-start | bytes 5308416 | tf_op jit(solution)/shard_map/all_gather | solution.py:458
  8.7 506.9 %all-gather.8.cloned.1.call-start = ((), (), s32[]{:S(2)}) async-start(), calls=%async_computation.2 | async-start | bytes 2162688 | tf_op jit(solution)/shard_map/all_gather | solution.py:526
  18.0 15.5 %collective-permute-start.2 = (bf16[10,64,256]{2,1,0:T(8,128)(2,1)}, bf16[10,64,256]{2,1,0:T(8,128)(2,1)}, u32[]{:S(2)}, u32[]{:S(2)}) collective-permute-start(bf16[10,64,256]{2,1,0:T(8,128)(2,1)} %get-tuple-element.130), channel_id=1, source_target_pairs={{0,1},{1,0},{2,3},{3,2},{4,5},{5,4},{6,7},{7,6},{8,9},{9,8},{10,11... | collective-permute-start | bytes 983048 | tf_op jit(solution)/shard_map/ppermute | solution.py:54
  19.5 36.4 %collective-permute-start.3 = (bf16[10,64,256]{2,1,0:T(8,128)(2,1)}, bf16[10,64,256]{2,1,0:T(8,128)(2,1)}, u32[]{:S(2)}, u32[]{:S(2)}) collective-permute-start(bf16[10,64,256]{2,1,0:T(8,128)(2,1)} %get-tuple-element.129), channel_id=1, source_target_pairs={{0,2},{1,3},{2,0},{3,1},{4,6},{5,7},{6,4},{7,5},{8,10},{9,11},{10,... | collective-permute-start | bytes 983048 | tf_op jit(solution)/shard_map/ppermute | solution.py:54
  24.2 43.6 %collective-permute-start.4 = (bf16[10,64,256]{2,1,0:T(8,128)(2,1)S(1)}, bf16[10,64,256]{2,1,0:T(8,128)(2,1)}, u32[]{:S(2)}, u32[]{:S(2)}) collective-permute-start(bf16[10,64,256]{2,1,0:T(8,128)(2,1)S(1)} %copy-done.27), channel_id=1, source_target_pairs={{0,3},{1,2},{2,1},{3,0},{4,7},{5,6},{6,5},{7,4},{8,11},{9,10},{10,... | collective-permute-start | bytes 983048 | tf_op jit(solution)/shard_map/ppermute | solution.py:54
  25.7 43.3 %collective-permute-start.5 = (bf16[10,64,256]{2,1,0:T(8,128)(2,1)S(1)}, bf16[10,64,256]{2,1,0:T(8,128)(2,1)}, u32[]{:S(2)}, u32[]{:S(2)}) collective-permute-start(bf16[10,64,256]{2,1,0:T(8,128)(2,1)S(1)} %copy-done.26), channel_id=1, source_target_pairs={{0,4},{1,5},{2,6},{3,7},{4,0},{5,1},{6,2},{7,3},{8,12},{9,13},{10,... | collective-permute-start | bytes 983048 | tf_op jit(solution)/shard_map/ppermute | solution.py:54
  29.2 50.6 %collective-permute-start.6 = (bf16[10,64,256]{2,1,0:T(8,128)(2,1)S(1)}, bf16[10,64,256]{2,1,0:T(8,128)(2,1)}, u32[]{:S(2)}, u32[]{:S(2)}) collective-permute-start(bf16[10,64,256]{2,1,0:T(8,128)(2,1)S(1)} %copy-done.25), channel_id=1, source_target_pairs={{0,5},{1,4},{2,7},{3,6},{4,1},{5,0},{6,3},{7,2},{8,13},{9,12},{10,... | collective-permute-start | bytes 983048 | tf_op jit(solution)/shard_map/ppermute | solution.py:54
  33.5 77.9 %collective-permute-start.7 = (bf16[10,64,256]{2,1,0:T(8,128)(2,1)S(1)}, bf16[10,64,256]{2,1,0:T(8,128)(2,1)}, u32[]{:S(2)}, u32[]{:S(2)}) collective-permute-start(bf16[10,64,256]{2,1,0:T(8,128)(2,1)S(1)} %copy-done.24), channel_id=1, source_target_pairs={{0,6},{1,7},{2,4},{3,5},{4,2},{5,3},{6,0},{7,1},{8,14},{9,15},{10,... | collective-permute-start | bytes 983048 | tf_op jit(solution)/shard_map/ppermute | solution.py:54
  55.9 78.5 %collective-permute-start.8 = (bf16[10,64,256]{2,1,0:T(8,128)(2,1)S(1)}, bf16[10,64,256]{2,1,0:T(8,128)(2,1)}, u32[]{:S(2)}, u32[]{:S(2)}) collective-permute-start(bf16[10,64,256]{2,1,0:T(8,128)(2,1)S(1)} %copy-done.23), channel_id=1, source_target_pairs={{0,7},{1,6},{2,5},{3,4},{4,3},{5,2},{6,1},{7,0},{8,15},{9,14},{10,... | collective-permute-start | bytes 983048 | tf_op jit(solution)/shard_map/ppermute | solution.py:54
  67.7 102.0 %collective-permute-start.19 = (bf16[64,2,6,256]{3,0,2,1:T(8,128)(2,1)}, bf16[64,2,6,256]{3,0,2,1:T(8,128)(2,1)}, u32[]{:S(2)}, u32[]{:S(2)}) collective-permute-start(bf16[64,2,6,256]{3,0,2,1:T(8,128)(2,1)} %get-tuple-element.133), channel_id=1, source_target_pairs={{8,0},{16,8},{24,16},{9,1},{17,9},{25,17},{10,2},{18,10},{26,18},{... | collective-permute-start | bytes 1179656 | tf_op jit(solution)/shard_map/ppermute | solution.py:48
  69.0 102.9 %collective-permute-start.18 = (bf16[64,2,6,256]{3,0,2,1:T(8,128)(2,1)}, bf16[64,2,6,256]{3,0,2,1:T(8,128)(2,1)}, u32[]{:S(2)}, u32[]{:S(2)}) collective-permute-start(bf16[64,2,6,256]{3,0,2,1:T(8,128)(2,1)} %get-tuple-element.132), channel_id=1, source_target_pairs={{0,8},{8,16},{16,24},{1,9},{9,17},{17,25},{2,10},{10,18},{18,26},{... | collective-permute-start | bytes 1179656 | tf_op jit(solution)/shard_map/ppermute | solution.py:48
  169.8 14.3 %collective-permute-start.12 = (bf16[8,32,256]{2,1,0:T(8,128)(2,1)}, bf16[8,32,256]{2,1,0:T(8,128)(2,1)}, u32[]{:S(2)}, u32[]{:S(2)}) collective-permute-start(bf16[8,32,256]{2,1,0:T(8,128)(2,1)} %get-tuple-element.51), channel_id=1, source_target_pairs={{0,4},{1,5},{2,6},{3,7},{4,0},{5,1},{6,2},{7,3},{8,12},{9,13},{10,... | collective-permute-start | bytes 393224 | tf_op jit(solution)/shard_map/ppermute | solution.py:54
  172.0 16.5 %collective-permute-start.13 = (bf16[8,32,256]{2,1,0:T(8,128)(2,1)}, bf16[8,32,256]{2,1,0:T(8,128)(2,1)}, u32[]{:S(2)}, u32[]{:S(2)}) collective-permute-start(bf16[8,32,256]{2,1,0:T(8,128)(2,1)} %get-tuple-element.52), channel_id=1, source_target_pairs={{0,5},{1,4},{2,7},{3,6},{4,1},{5,0},{6,3},{7,2},{8,13},{9,12},{10,... | collective-permute-start | bytes 393224 | tf_op jit(solution)/shard_map/ppermute | solution.py:54
  173.6 19.4 %collective-permute-start.14 = (bf16[8,32,256]{2,1,0:T(8,128)(2,1)}, bf16[8,32,256]{2,1,0:T(8,128)(2,1)}, u32[]{:S(2)}, u32[]{:S(2)}) collective-permute-start(bf16[8,32,256]{2,1,0:T(8,128)(2,1)} %get-tuple-element.53), channel_id=1, source_target_pairs={{0,6},{1,7},{2,4},{3,5},{4,2},{5,3},{6,0},{7,1},{8,14},{9,15},{10,... | collective-permute-start | bytes 393224 | tf_op jit(solution)/shard_map/ppermute | solution.py:54
  178.0 27.8 %collective-permute-start.20 = (bf16[8,32,256]{2,1,0:T(8,128)(2,1)}, bf16[8,32,256]{2,1,0:T(8,128)(2,1)S(1)}, u32[]{:S(2)}, u32[]{:S(2)}) collective-permute-start(bf16[8,32,256]{2,1,0:T(8,128)(2,1)} %get-tuple-element.60), channel_id=1, source_target_pairs={{0,1},{1,0},{2,3},{3,2},{4,5},{5,4},{6,7},{7,6},{8,9},{9,8},{10,11... | collective-permute-start | bytes 393224 | tf_op jit(solution)/shard_map/ppermute | solution.py:54
  179.1 27.5 %collective-permute-start.21 = (bf16[8,32,256]{2,1,0:T(8,128)(2,1)}, bf16[8,32,256]{2,1,0:T(8,128)(2,1)S(1)}, u32[]{:S(2)}, u32[]{:S(2)}) collective-permute-start(bf16[8,32,256]{2,1,0:T(8,128)(2,1)} %get-tuple-element.61), channel_id=1, source_target_pairs={{0,2},{1,3},{2,0},{3,1},{4,6},{5,7},{6,4},{7,5},{8,10},{9,11},{10,... | collective-permute-start | bytes 393224 | tf_op jit(solution)/shard_map/ppermute | solution.py:54
  184.1 24.1 %collective-permute-start.22 = (bf16[8,32,256]{2,1,0:T(8,128)(2,1)}, bf16[8,32,256]{2,1,0:T(8,128)(2,1)S(1)}, u32[]{:S(2)}, u32[]{:S(2)}) collective-permute-start(bf16[8,32,256]{2,1,0:T(8,128)(2,1)} %get-tuple-element.62), channel_id=1, source_target_pairs={{0,3},{1,2},{2,1},{3,0},{4,7},{5,6},{6,5},{7,4},{8,11},{9,10},{10,... | collective-permute-start | bytes 393224 | tf_op jit(solution)/shard_map/ppermute | solution.py:54
  188.5 21.0 %collective-permute-start.23 = (bf16[8,32,256]{2,1,0:T(8,128)(2,1)}, bf16[8,32,256]{2,1,0:T(8,128)(2,1)S(1)}, u32[]{:S(2)}, u32[]{:S(2)}) collective-permute-start(bf16[8,32,256]{2,1,0:T(8,128)(2,1)} %get-tuple-element.63), channel_id=1, source_target_pairs={{0,4},{1,5},{2,6},{3,7},{4,0},{5,1},{6,2},{7,3},{8,12},{9,13},{10,... | collective-permute-start | bytes 393224 | tf_op jit(solution)/shard_map/ppermute | solution.py:54
  208.2 18.2 %collective-permute-start.16 = (bf16[2,6,32,256]{3,2,1,0:T(8,128)(2,1)}, bf16[2,6,32,256]{3,2,1,0:T(8,128)(2,1)S(1)}, u32[]{:S(2)}, u32[]{:S(2)}) collective-permute-start(bf16[2,6,32,256]{3,2,1,0:T(8,128)(2,1)} %get-tuple-element.56), channel_id=1, source_target_pairs={{0,8},{8,16},{16,24},{1,9},{9,17},{17,25},{2,10},{10,18},{18,26},{... | collective-permute-start | bytes 589832 | tf_op jit(solution)/shard_map/ppermute | solution.py:483
  209.5 17.0 %collective-permute-start.17 = (bf16[2,6,32,256]{3,2,1,0:T(8,128)(2,1)}, bf16[2,6,32,256]{3,2,1,0:T(8,128)(2,1)S(1)}, u32[]{:S(2)}, u32[]{:S(2)}) collective-permute-start(bf16[2,6,32,256]{3,2,1,0:T(8,128)(2,1)} %get-tuple-element.57), channel_id=1, source_target_pairs={{8,0},{16,8},{24,16},{9,1},{17,9},{25,17},{10,2},{18,10},{26,18},{... | collective-permute-start | bytes 589832 | tf_op jit(solution)/shard_map/ppermute | solution.py:484
  223.7 35.2 %collective-permute-start.27 = (bf16[2,6,32,256]{3,2,1,0:T(8,128)(2,1)}, bf16[2,6,32,256]{3,2,1,0:T(8,128)(2,1)S(1)}, u32[]{:S(2)}, u32[]{:S(2)}) collective-permute-start(bf16[2,6,32,256]{3,2,1,0:T(8,128)(2,1)} %get-tuple-element.68), channel_id=1, source_target_pairs={{0,8},{8,16},{16,24},{1,9},{9,17},{17,25},{2,10},{10,18},{18,26},{... | collective-permute-start | bytes 589832 | tf_op jit(solution)/shard_map/ppermute | solution.py:483
  225.0 34.0 %collective-permute-start.28 = (bf16[2,6,32,256]{3,2,1,0:T(8,128)(2,1)}, bf16[2,6,32,256]{3,2,1,0:T(8,128)(2,1)S(1)}, u32[]{:S(2)}, u32[]{:S(2)}) collective-permute-start(bf16[2,6,32,256]{3,2,1,0:T(8,128)(2,1)} %get-tuple-element.69), channel_id=1, source_target_pairs={{8,0},{16,8},{24,16},{9,1},{17,9},{25,17},{10,2},{18,10},{26,18},{... | collective-permute-start | bytes 589832 | tf_op jit(solution)/shard_map/ppermute | solution.py:484
  253.2 38.2 %collective-permute-start.29 = (bf16[2,1,32,256]{3,2,1,0:T(8,128)(2,1)S(1)}, bf16[2,1,32,256]{3,2,1,0:T(8,128)(2,1)S(1)}, u32[]{:S(2)}, u32[]{:S(2)}) collective-permute-start(bf16[2,1,32,256]{3,2,1,0:T(8,128)(2,1)S(1)} %get-tuple-element.162), channel_id=1, source_target_pairs={{0,8},{8,16},{16,24},{1,9},{9,17},{17,25},{2,10},{10,18},{18,26},{... | collective-permute-start | bytes 98312 | tf_op jit(solution)/shard_map/ppermute | solution.py:48
  257.4 34.2 %collective-permute-start.30 = (bf16[2,1,32,256]{3,2,1,0:T(8,128)(2,1)S(1)}, bf16[2,1,32,256]{3,2,1,0:T(8,128)(2,1)S(1)}, u32[]{:S(2)}, u32[]{:S(2)}) collective-permute-start(bf16[2,1,32,256]{3,2,1,0:T(8,128)(2,1)S(1)} %get-tuple-element.161), channel_id=1, source_target_pairs={{8,0},{16,8},{24,16},{9,1},{17,9},{25,17},{10,2},{18,10},{26,18},{... | collective-permute-start | bytes 98312 | tf_op jit(solution)/shard_map/ppermute | solution.py:48
  296.5 20.9 %collective-permute-start.35 = (bf16[10,32,256]{2,1,0:T(8,128)(2,1)S(1)}, bf16[10,32,256]{2,1,0:T(8,128)(2,1)S(1)}, u32[]{:S(2)}, u32[]{:S(2)}) collective-permute-start(bf16[10,32,256]{2,1,0:T(8,128)(2,1)S(1)} %get-tuple-element.153), channel_id=1, source_target_pairs={{0,5},{1,4},{2,7},{3,6},{4,1},{5,0},{6,3},{7,2},{8,13},{9,12},{10,... | collective-permute-start | bytes 491528 | tf_op jit(solution)/shard_map/ppermute | solution.py:54
  299.9 22.8 %collective-permute-start.36 = (bf16[10,32,256]{2,1,0:T(8,128)(2,1)S(1)}, bf16[10,32,256]{2,1,0:T(8,128)(2,1)S(1)}, u32[]{:S(2)}, u32[]{:S(2)}) collective-permute-start(bf16[10,32,256]{2,1,0:T(8,128)(2,1)S(1)} %get-tuple-element.152), channel_id=1, source_target_pairs={{0,6},{1,7},{2,4},{3,5},{4,2},{5,3},{6,0},{7,1},{8,14},{9,15},{10,... | collective-permute-start | bytes 491528 | tf_op jit(solution)/shard_map/ppermute | solution.py:54
  301.0 29.0 %collective-permute-start.37 = (bf16[10,32,256]{2,1,0:T(8,128)(2,1)S(1)}, bf16[10,32,256]{2,1,0:T(8,128)(2,1)S(1)}, u32[]{:S(2)}, u32[]{:S(2)}) collective-permute-start(bf16[10,32,256]{2,1,0:T(8,128)(2,1)S(1)} %get-tuple-element.151), channel_id=1, source_target_pairs={{0,7},{1,6},{2,5},{3,4},{4,3},{5,2},{6,1},{7,0},{8,15},{9,14},{10,... | collective-permute-start | bytes 491528 | tf_op jit(solution)/shard_map/ppermute | solution.py:54
  305.7 24.3 %collective-permute-start.40 = (bf16[10,32,256]{2,1,0:T(8,128)(2,1)S(1)}, bf16[10,32,256]{2,1,0:T(8,128)(2,1)S(1)}, u32[]{:S(2)}, u32[]{:S(2)}) collective-permute-start(bf16[10,32,256]{2,1,0:T(8,128)(2,1)S(1)} %get-tuple-element.149), channel_id=1, source_target_pairs={{0,1},{1,0},{2,3},{3,2},{4,5},{5,4},{6,7},{7,6},{8,9},{9,8},{10,11... | collective-permute-start | bytes 491528 | tf_op jit(solution)/shard_map/ppermute | solution.py:54
  307.2 24.3 %collective-permute-start.41 = (bf16[10,32,256]{2,1,0:T(8,128)(2,1)S(1)}, bf16[10,32,256]{2,1,0:T(8,128)(2,1)S(1)}, u32[]{:S(2)}, u32[]{:S(2)}) collective-permute-start(bf16[10,32,256]{2,1,0:T(8,128)(2,1)S(1)} %get-tuple-element.148), channel_id=1, source_target_pairs={{0,2},{1,3},{2,0},{3,1},{4,6},{5,7},{6,4},{7,5},{8,10},{9,11},{10,... | collective-permute-start | bytes 491528 | tf_op jit(solution)/shard_map/ppermute | solution.py:54
  317.5 14.3 %collective-permute-start.42 = (bf16[10,32,256]{2,1,0:T(8,128)(2,1)}, bf16[10,32,256]{2,1,0:T(8,128)(2,1)S(1)}, u32[]{:S(2)}, u32[]{:S(2)}) collective-permute-start(bf16[10,32,256]{2,1,0:T(8,128)(2,1)} %get-tuple-element.147), channel_id=1, source_target_pairs={{0,3},{1,2},{2,1},{3,0},{4,7},{5,6},{6,5},{7,4},{8,11},{9,10},{10,... | collective-permute-start | bytes 491528 | tf_op jit(solution)/shard_map/ppermute | solution.py:54
  322.8 21.2 %collective-permute-start.43 = (bf16[10,32,256]{2,1,0:T(8,128)(2,1)}, bf16[10,32,256]{2,1,0:T(8,128)(2,1)S(1)}, u32[]{:S(2)}, u32[]{:S(2)}) collective-permute-start(bf16[10,32,256]{2,1,0:T(8,128)(2,1)} %get-tuple-element.146), channel_id=1, source_target_pairs={{0,4},{1,5},{2,6},{3,7},{4,0},{5,1},{6,2},{7,3},{8,12},{9,13},{10,... | collective-permute-start | bytes 491528 | tf_op jit(solution)/shard_map/ppermute | solution.py:54
  330.0 17.5 %collective-permute-start.44 = (bf16[10,32,256]{2,1,0:T(8,128)(2,1)}, bf16[10,32,256]{2,1,0:T(8,128)(2,1)S(1)}, u32[]{:S(2)}, u32[]{:S(2)}) collective-permute-start(bf16[10,32,256]{2,1,0:T(8,128)(2,1)} %get-tuple-element.145), channel_id=1, source_target_pairs={{0,5},{1,4},{2,7},{3,6},{4,1},{5,0},{6,3},{7,2},{8,13},{9,12},{10,... | collective-permute-start | bytes 491528 | tf_op jit(solution)/shard_map/ppermute | solution.py:54
  330.1 22.3 %collective-permute-start.45 = (bf16[10,32,256]{2,1,0:T(8,128)(2,1)}, bf16[10,32,256]{2,1,0:T(8,128)(2,1)S(1)}, u32[]{:S(2)}, u32[]{:S(2)}) collective-permute-start(bf16[10,32,256]{2,1,0:T(8,128)(2,1)} %get-tuple-element.144), channel_id=1, source_target_pairs={{0,6},{1,7},{2,4},{3,5},{4,2},{5,3},{6,0},{7,1},{8,14},{9,15},{10,... | collective-permute-start | bytes 491528 | tf_op jit(solution)/shard_map/ppermute | solution.py:54
  331.5 25.4 %collective-permute-start.46 = (bf16[10,32,256]{2,1,0:T(8,128)(2,1)}, bf16[10,32,256]{2,1,0:T(8,128)(2,1)S(1)}, u32[]{:S(2)}, u32[]{:S(2)}) collective-permute-start(bf16[10,32,256]{2,1,0:T(8,128)(2,1)} %get-tuple-element.143), channel_id=1, source_target_pairs={{0,7},{1,6},{2,5},{3,4},{4,3},{5,2},{6,1},{7,0},{8,15},{9,14},{10,... | collective-permute-start | bytes 491528 | tf_op jit(solution)/shard_map/ppermute | solution.py:54
  409.3 245.1 %all-gather.6.cloned.1.call-start = ((), (), s32[]{:S(2)}) async-start(), calls=%async_computation.1 | async-start | bytes 1474560 | tf_op jit(solution)/shard_map/all_gather | solution.py:523
  418.9 63.2 %collective-permute-start.55 = (bf16[1,9,8,64,128]{4,3,1,2,0:T(8,128)(2,1)}, bf16[1,9,8,64,128]{4,3,1,2,0:T(8,128)(2,1)}, u32[]{:S(2)}, u32[]{:S(2)}) collective-permute-start(bf16[1,9,8,64,128]{4,3,1,2,0:T(8,128)(2,1)} %constant_dynamic-slice_fusion), channel_id=1, source_target_pairs={{0,16},{8,24},{16,0},{24,8},{1,17},{9,25},{17,1},{25,9},{2,18},{10... | collective-permute-start | bytes 3538952 | tf_op jit(solution)/shard_map/ppermute | solution.py:424
  485.0 19.8 %collective-permute-start.62 = (bf16[9,64,128]{2,1,0:T(8,128)(2,1)S(1)}, bf16[9,64,128]{2,1,0:T(8,128)(2,1)S(1)}, u32[]{:S(2)}, u32[]{:S(2)}) collective-permute-start(bf16[9,64,128]{2,1,0:T(8,128)(2,1)S(1)} %get-tuple-element.137), channel_id=1, source_target_pairs={{0,7},{1,6},{2,5},{3,4},{4,3},{5,2},{6,1},{7,0},{8,15},{9,14},{10,... | collective-permute-start | bytes 442376 | tf_op jit(solution)/shard_map/ppermute | solution.py:54
  487.8 19.8 %collective-permute-start.61 = (bf16[9,64,128]{2,1,0:T(8,128)(2,1)S(1)}, bf16[9,64,128]{2,1,0:T(8,128)(2,1)S(1)}, u32[]{:S(2)}, u32[]{:S(2)}) collective-permute-start(bf16[9,64,128]{2,1,0:T(8,128)(2,1)S(1)} %get-tuple-element.138), channel_id=1, source_target_pairs={{0,6},{1,7},{2,4},{3,5},{4,2},{5,3},{6,0},{7,1},{8,14},{9,15},{10,... | collective-permute-start | bytes 442376 | tf_op jit(solution)/shard_map/ppermute | solution.py:54
  488.8 21.2 %collective-permute-start.60 = (bf16[9,64,128]{2,1,0:T(8,128)(2,1)S(1)}, bf16[9,64,128]{2,1,0:T(8,128)(2,1)S(1)}, u32[]{:S(2)}, u32[]{:S(2)}) collective-permute-start(bf16[9,64,128]{2,1,0:T(8,128)(2,1)S(1)} %get-tuple-element.139), channel_id=1, source_target_pairs={{0,5},{1,4},{2,7},{3,6},{4,1},{5,0},{6,3},{7,2},{8,13},{9,12},{10,... | collective-permute-start | bytes 442376 | tf_op jit(solution)/shard_map/ppermute | solution.py:54
  490.4 22.7 %collective-permute-start.59 = (bf16[9,64,128]{2,1,0:T(8,128)(2,1)S(1)}, bf16[9,64,128]{2,1,0:T(8,128)(2,1)S(1)}, u32[]{:S(2)}, u32[]{:S(2)}) collective-permute-start(bf16[9,64,128]{2,1,0:T(8,128)(2,1)S(1)} %get-tuple-element.140), channel_id=1, source_target_pairs={{0,4},{1,5},{2,6},{3,7},{4,0},{5,1},{6,2},{7,3},{8,12},{9,13},{10,... | collective-permute-start | bytes 442376 | tf_op jit(solution)/shard_map/ppermute | solution.py:54
  491.2 21.8 %collective-permute-start.58 = (bf16[9,64,128]{2,1,0:T(8,128)(2,1)S(1)}, bf16[9,64,128]{2,1,0:T(8,128)(2,1)S(1)}, u32[]{:S(2)}, u32[]{:S(2)}) collective-permute-start(bf16[9,64,128]{2,1,0:T(8,128)(2,1)S(1)} %get-tuple-element.141), channel_id=1, source_target_pairs={{0,3},{1,2},{2,1},{3,0},{4,7},{5,6},{6,5},{7,4},{8,11},{9,10},{10,... | collective-permute-start | bytes 442376 | tf_op jit(solution)/shard_map/ppermute | solution.py:54
  572.1 51.2 %collective-permute-start.47 = (bf16[8,64,256]{2,1,0:T(8,128)(2,1)}, bf16[8,64,256]{2,1,0:T(8,128)(2,1)}, u32[]{:S(2)}, u32[]{:S(2)}) collective-permute-start(bf16[8,64,256]{2,1,0:T(8,128)(2,1)} %get-tuple-element.74), channel_id=1, source_target_pairs={{0,1},{1,0},{2,3},{3,2},{4,5},{5,4},{6,7},{7,6},{8,9},{9,8},{10,11... | collective-permute-start | bytes 786440 | tf_op jit(solution)/shard_map/ppermute | solution.py:54
  572.6 51.8 %collective-permute-start.48 = (bf16[8,64,256]{2,1,0:T(8,128)(2,1)}, bf16[8,64,256]{2,1,0:T(8,128)(2,1)}, u32[]{:S(2)}, u32[]{:S(2)}) collective-permute-start(bf16[8,64,256]{2,1,0:T(8,128)(2,1)} %get-tuple-element.75), channel_id=1, source_target_pairs={{0,2},{1,3},{2,0},{3,1},{4,6},{5,7},{6,4},{7,5},{8,10},{9,11},{10,... | collective-permute-start | bytes 786440 | tf_op jit(solution)/shard_map/ppermute | solution.py:54
  576.7 54.0 %collective-permute-start.49 = (bf16[8,64,256]{2,1,0:T(8,128)(2,1)}, bf16[8,64,256]{2,1,0:T(8,128)(2,1)S(1)}, u32[]{:S(2)}, u32[]{:S(2)}) collective-permute-start(bf16[8,64,256]{2,1,0:T(8,128)(2,1)} %get-tuple-element.76), channel_id=1, source_target_pairs={{0,3},{1,2},{2,1},{3,0},{4,7},{5,6},{6,5},{7,4},{8,11},{9,10},{10,... | collective-permute-start | bytes 786440 | tf_op jit(solution)/shard_map/ppermute | solution.py:54
  577.8 52.9 %collective-permute-start.50 = (bf16[8,64,256]{2,1,0:T(8,128)(2,1)}, bf16[8,64,256]{2,1,0:T(8,128)(2,1)S(1)}, u32[]{:S(2)}, u32[]{:S(2)}) collective-permute-start(bf16[8,64,256]{2,1,0:T(8,128)(2,1)} %get-tuple-element.77), channel_id=1, source_target_pairs={{0,4},{1,5},{2,6},{3,7},{4,0},{5,1},{6,2},{7,3},{8,12},{9,13},{10,... | collective-permute-start | bytes 786440 | tf_op jit(solution)/shard_map/ppermute | solution.py:54
  580.4 50.3 %collective-permute-start.51 = (bf16[8,64,256]{2,1,0:T(8,128)(2,1)}, bf16[8,64,256]{2,1,0:T(8,128)(2,1)S(1)}, u32[]{:S(2)}, u32[]{:S(2)}) collective-permute-start(bf16[8,64,256]{2,1,0:T(8,128)(2,1)} %get-tuple-element.78), channel_id=1, source_target_pairs={{0,5},{1,4},{2,7},{3,6},{4,1},{5,0},{6,3},{7,2},{8,13},{9,12},{10,... | collective-permute-start | bytes 786440 | tf_op jit(solution)/shard_map/ppermute | solution.py:54
  623.3 20.7 %collective-permute-start.52 = (bf16[8,64,256]{2,1,0:T(8,128)(2,1)}, bf16[8,64,256]{2,1,0:T(8,128)(2,1)S(1)}, u32[]{:S(2)}, u32[]{:S(2)}) collective-permute-start(bf16[8,64,256]{2,1,0:T(8,128)(2,1)} %get-tuple-element.79), channel_id=1, source_target_pairs={{0,6},{1,7},{2,4},{3,5},{4,2},{5,3},{6,0},{7,1},{8,14},{9,15},{10,... | collective-permute-start | bytes 786440 | tf_op jit(solution)/shard_map/ppermute | solution.py:54
  624.4 25.2 %collective-permute-start.53 = (bf16[8,64,256]{2,1,0:T(8,128)(2,1)}, bf16[8,64,256]{2,1,0:T(8,128)(2,1)}, u32[]{:S(2)}, u32[]{:S(2)}) collective-permute-start(bf16[8,64,256]{2,1,0:T(8,128)(2,1)} %get-tuple-element.80), channel_id=1, source_target_pairs={{0,7},{1,6},{2,5},{3,4},{4,3},{5,2},{6,1},{7,0},{8,15},{9,14},{10,... | collective-permute-start | bytes 786440 | tf_op jit(solution)/shard_map/ppermute | solution.py:54
  (75 other events, 1171.6 us)
Sparse Core Ops, SparseCore 0:
  11.0 125.0 all-gather.3
Sparse Core Ops, SparseCore 1:
  409.4 55.3 all-gather.7
  515.7 18.7 all-gather.5

commit v2 on v1

v2 whole, which is shorter than its diff:
```python
import functools

import jax
import jax.numpy as jnp
import ml_dtypes
import numpy as np
from jax import lax
from jax.experimental import pallas as pl
from jax.experimental.pallas import tpu as pltpu
from jax.sharding import PartitionSpec as P

F32 = jnp.float32
BF16 = jnp.bfloat16
IN_VMEM = pl.BlockSpec(memory_space=pltpu.VMEM)
IN_HBM = pl.BlockSpec(memory_space=pltpu.HBM)
IN_SMEM = pl.BlockSpec(memory_space=pltpu.SMEM)
PARAMS = pltpu.CompilerParams(vmem_limit_bytes=60 << 20)
RIM = 7
GROUP = 16


def struct(shape, dtype):
    return jax.ShapeDtypeStruct(shape, dtype)


def sinc_taps():
    offset = np.arange(12) - 5.5
    values = np.sinc(offset * 0.5) * (0.5 + 0.5 * np.cos(np.pi * offset / 6.0))
    return values / values.sum()


def up_table(size):
    tap = np.arange(2 * size)[None, :] - 2 * np.arange(size)[:, None] + 5
    held = (tap >= 0) & (tap < 12)
    return np.where(held, 2.0 * sinc_taps()[np.clip(tap, 0, 11)], 0.0).astype(np.float32)


def halves(table):
    high = table.astype(ml_dtypes.bfloat16)
    return high, (table - high.astype(np.float32)).astype(ml_dtypes.bfloat16)


def from_neighbours(value, axis, dim, width):
    size, length = lax.axis_size(axis), value.shape[dim]
    up = [(i, i + 1) for i in range(size - 1)]
    down = [(j, i) for i, j in up]
    last = lax.slice_in_dim(value, length - width, length, axis=dim)
    first = lax.slice_in_dim(value, 0, width, axis=dim)
    return lax.ppermute(last, axis, up), lax.ppermute(first, axis, down)


def swapped(value, axis, bits):
    return lax.ppermute(value, axis, [(i, i ^ bits) for i in range(lax.axis_size(axis))])


def once(value, *others):
    return lax.optimization_barrier((value,) + others)[0]


def exchange(parts, axis):
    size = lax.axis_size(axis)
    return [parts[0]] + [swapped(parts[x], axis, x) for x in range(1, size)]


def started(sems, first, pairs):
    copies = [
        pltpu.make_async_copy(source, target, sems.at[first + index])
        for index, (source, target) in enumerate(pairs)
    ]
    for copy in copies:
        copy.start()
    return copies


def finished(copies):
    for copy in copies:
        copy.wait()


def rows_kernel(count, me_ref, before, value, after, *refs):
    parts, (arrived, rows_first, sems) = refs[:count], refs[count:]
    me = me_ref[0]
    width, items, rows, _ = value.shape
    blocks = count // items
    span = rows // blocks
    finished(started(sems, 0, [(value, arrived)]))
    for item in range(items):
        for group in range(width // GROUP):
            at = slice(group * GROUP, (group + 1) * GROUP)
            rows_first[item, 1 : rows + 1, at] = jnp.swapaxes(arrived[at, item], 0, 1)
        rows_first[item, 0] = before[:, item, 0]
        rows_first[item, rows + 1] = after[:, item, 0]
    pairs = []
    for x in range(count):
        dest = me ^ x
        start = (dest % blocks) * span
        pairs.append((rows_first.at[dest // blocks, pl.ds(start, span + 2)], parts[x]))
    finished(started(sems, 1, pairs))


def row_parts(me, before, value, after, count):
    width, items, rows, columns = value.shape
    span = rows * items // count
    return pl.pallas_call(
        functools.partial(rows_kernel, count),
        out_shape=[struct((span + 2, width, columns), BF16)] * count,
        in_specs=[IN_SMEM, IN_VMEM, IN_HBM, IN_VMEM],
        out_specs=[IN_HBM] * count,
        scratch_shapes=[
            pltpu.VMEM((width, items, rows, columns), BF16),
            pltpu.VMEM((items, rows + 2, width, columns), BF16),
            pltpu.SemaphoreType.DMA((1 + count,)),
        ],
        compiler_params=PARAMS,
        name="row_parts",
    )(me, before, value, after)


def weight_pieces(weight, me_dp, feats):
    size = lax.axis_size("chan")
    shares = min(lax.axis_size("dp"), weight.shape[3] // 128)
    share = weight.shape[3] // shares
    held = lax.dynamic_slice_in_dim(weight, me_dp % shares * share, share, 3).reshape(1, 9, -1, share)
    places = [(0, 0)]
    bit = size // 2
    while bit >= 4:
        held = jnp.concatenate([held, swapped(held, "chan", bit)], axis=0)
        places += [(chan ^ bit, dp) for chan, dp in places]
        bit //= 2
    pieces = [(held, places)]
    for x in range(1, min(size, 4)):
        pieces.append((swapped(held, "chan", x), [(chan ^ x, dp) for chan, dp in places]))
    waits = [feats[-1:], (), feats[-2:-1], (), feats[-3:-2], (), feats[-4:-3], ()]
    bit = shares // 2
    while bit:
        met = []
        for piece, places in pieces:
            got = swapped(once(piece, *(waits.pop(0) if waits else ())), "dp", bit)
            moved = [(chan, dp ^ bit) for chan, dp in places]
            if bit > 1:
                met.append((jnp.concatenate([piece, got], axis=0), places + moved))
            else:
                met += [(piece, places), (got, moved)]
        pieces = met
        bit //= 2
    return [piece for piece, _ in pieces], tuple(tuple(places) for _, places in pieces)


def tap_blocks(me, part, pieces, places, taps):
    share = pieces[0].shape[3]
    pairs = []
    for piece, blocks in zip(pieces, places):
        for index, (chan, dp) in enumerate(blocks):
            lanes = pl.ds(pl.multiple_of((part ^ dp) * share, share), share)
            pairs.append((piece.at[index], taps.at[:, me ^ chan, :, lanes]))
    return pairs


def transposed_kernel(places, me_ref, part_ref, *refs):
    pieces, (out, taps, turned, sems) = refs[:-4], refs[-4:]
    pairs = tap_blocks(me_ref[0], part_ref[0], pieces, places, taps)
    finished(started(sems, 0, pairs))
    channels = taps.shape[3]
    copies = []
    for tap in range(9):
        turned[8 - tap] = jnp.transpose(taps[tap].reshape(channels, channels))
        copies += started(sems, len(pairs) + tap, [(turned.at[8 - tap], out.at[8 - tap])])
    finished(copies)


def transposed_taps(me, part, pieces, places, channels):
    own = pieces[0].shape[2]
    blocks = sum(len(place) for place in places)
    return pl.pallas_call(
        functools.partial(transposed_kernel, places),
        out_shape=struct((9, channels, channels), BF16),
        in_specs=[IN_SMEM, IN_SMEM] + [IN_HBM] * len(pieces),
        out_specs=IN_HBM,
        scratch_shapes=[
            pltpu.VMEM((9, channels // own, own, channels), BF16),
            pltpu.VMEM((9, channels, channels), BF16),
            pltpu.SemaphoreType.DMA((blocks + 9,)),
        ],
        compiler_params=PARAMS,
        name="transposed_taps",
    )(me, part, *pieces)


def arrivals(me, parts, arrived):
    count = arrived.shape[0]
    width = parts[0].shape[1]
    return [
        (part, arrived.at[me ^ (index % count), :, pl.ds(index // count * width, width)])
        for index, part in enumerate(parts)
    ]


def departures(me, results, outs):
    count = results.shape[1]
    width = outs[0].shape[1]
    return [
        (results.at[:, me ^ (index % count), pl.ds(index // count * width, width)], out)
        for index, out in enumerate(outs)
    ]


def fill_shifted(arrived, scales, shifted):
    count, rows, own, columns = arrived.shape

    def row_step(row, carry):
        column = lax.broadcasted_iota(jnp.int32, (own, columns), 1)
        for source in range(count):
            value = arrived[source, row].astype(F32)
            if scales is not None:
                value = (value * scales[source]).astype(BF16).astype(F32)
            before = jnp.where(column == 0, 0.0, pltpu.roll(value, 1, 1))
            after = jnp.where(column == columns - 1, 0.0, pltpu.roll(value, columns - 1, 1))
            shifted[row, 0, source] = before.astype(BF16)
            shifted[row, 1, source] = value.astype(BF16)
            shifted[row, 2, source] = after.astype(BF16)
        return carry

    lax.fori_loop(0, rows, row_step, 0)


def convolved(taps, shifted, row, channels, columns):
    total = None
    for i in range(3):
        for j in range(3):
            term = jnp.dot(
                taps[3 * i + j].reshape(channels, channels),
                shifted[row + i, j].reshape(channels, columns),
                preferred_element_type=F32,
            )
            total = term if total is None else total + term
    return total


def forward_kernel(count, places, me_ref, part_ref, scales, *refs):
    pieces, refs = refs[: len(places)], refs[len(places) :]
    parts, outs = refs[:count], refs[count:-6]
    arrived, shifted, taps, results, wide_scales, sems = refs[-6:]
    me = me_ref[0]
    rows, _, own, columns = results.shape
    arriving = started(sems, 0, arrivals(me, parts, arrived))
    tapping = started(sems, count, tap_blocks(me, part_ref[0], pieces, places, taps))
    wide_scales[...] = jnp.broadcast_to(scales[...], wide_scales.shape)
    finished(arriving)
    fill_shifted(arrived, wide_scales, shifted)
    finished(tapping)

    def row_step(row, carry):
        total = convolved(taps, shifted, row, count * own, columns)
        results[row] = total.astype(BF16).reshape(count, own, columns)
        return carry

    lax.fori_loop(0, rows, row_step, 0)
    finished(started(sems, 0, departures(me, results, outs)))


def conv_forward(me, part, pieces, places, scales, parts, split):
    count = len(parts)
    rows, own, columns = parts[0].shape
    blocks = sum(len(place) for place in places)
    outs = pl.pallas_call(
        functools.partial(forward_kernel, count, places),
        out_shape=[struct((rows - 2, own // split, columns), BF16)] * (count * split),
        in_specs=[IN_SMEM, IN_SMEM, IN_VMEM] + [IN_HBM] * (len(pieces) + count),
        out_specs=[IN_HBM] * (count * split),
        scratch_shapes=[
            pltpu.VMEM((count, rows, own, columns), BF16),
            pltpu.VMEM((rows, 3, count, own, columns), BF16),
            pltpu.VMEM((9, count, own, count * own), BF16),
            pltpu.VMEM((rows - 2, count, own, columns), BF16),
            pltpu.VMEM((count, own, columns), F32),
            pltpu.SemaphoreType.DMA((count * split + blocks,)),
        ],
        compiler_params=PARAMS,
        name="conv_forward",
    )(me, part, scales, *pieces, *parts)
    return [outs[h * count : (h + 1) * count] for h in range(split)]


def backward_kernel(count, split, me_ref, _, taps_ref, *refs):
    grads, refs = refs[: count * split], refs[count * split :]
    feats, outs, style_ref = refs[:count], refs[count : 2 * count], refs[2 * count]
    arrived, arrived_feats, shifted, taps, results, sems = refs[2 * count + 1 :]
    me = me_ref[0]
    rows, _, own, columns = results.shape
    arriving = started(sems, 0, arrivals(me, grads, arrived))
    tapping = started(
        sems,
        count * split,
        [(taps_ref, taps)] + arrivals(me, feats, arrived_feats),
    )
    finished(arriving)
    fill_shifted(arrived, None, shifted)
    finished(tapping)
    style_ref[...] = jnp.zeros_like(style_ref)

    def row_step(row, carry):
        total = convolved(taps, shifted, row, count * own, columns).reshape(count, own, columns)
        results[row] = total.astype(BF16)
        product = total * arrived_feats[:, row + 1].astype(F32)
        style_ref[...] += jnp.sum(product, axis=2, keepdims=True)
        return carry

    lax.fori_loop(0, rows, row_step, 0)
    finished(started(sems, 0, departures(me, results, outs)))


def conv_backward(me, earlier, taps, grads, feats):
    count = len(feats)
    split = len(grads) // count
    rows, own, columns = feats[0].shape
    channels = count * own
    outs = pl.pallas_call(
        functools.partial(backward_kernel, count, split),
        out_shape=[struct((rows - 2, own, columns), BF16)] * count + [struct((count, own, 1), F32)],
        in_specs=[IN_SMEM] + [IN_HBM] * (2 + len(grads) + count),
        out_specs=[IN_HBM] * count + [IN_VMEM],
        scratch_shapes=[
            pltpu.VMEM((count, rows, own, columns), BF16),
            pltpu.VMEM((count, rows, own, columns), BF16),
            pltpu.VMEM((rows, 3, count, own, columns), BF16),
            pltpu.VMEM((9, channels, channels), BF16),
            pltpu.VMEM((rows - 2, count, own, columns), BF16),
            pltpu.SemaphoreType.DMA((len(grads) + count + 1,)),
        ],
        compiler_params=PARAMS,
        name="conv_backward",
    )(me, earlier, taps, *grads, *feats)
    return outs[:-1], outs[-1]


def weight_kernel(count, split, me_ref, core_ref, scales, *refs):
    grads, refs = refs[: count * split], refs[count * split :]
    feats, (keep, send) = refs[:count], refs[count : count + 2]
    arrived, arrived_feats, shifted, rows_ref, results, wide_scales, sems = refs[count + 2 :]
    me, core = me_ref[0], core_ref[0]
    rows, _, own, columns = rows_ref.shape
    channels = count * own
    half = channels // 2
    arriving = started(sems, 0, arrivals(me, feats, arrived_feats))
    arriving_grads = started(sems, count, arrivals(me, grads, arrived))
    wide_scales[...] = jnp.broadcast_to(scales[...], wide_scales.shape)
    finished(arriving)
    fill_shifted(arrived_feats, wide_scales, shifted)
    finished(arriving_grads)
    for source in range(count):
        rows_ref[:, source] = arrived[source, 1 : rows + 1]

    def leaving(tap):
        return [
            pltpu.make_async_copy(results.at[core, tap], keep.at[tap], sems.at[2 * tap]),
            pltpu.make_async_copy(results.at[1 - core, tap], send.at[tap], sems.at[2 * tap + 1]),
        ]

    def tap_step(tap, carry):
        i, j = lax.div(tap, 3), lax.rem(tap, 3)
        total = None
        for row in range(rows):
            term = lax.dot_general(
                rows_ref[row].reshape(channels, columns),
                shifted[row + i, j].reshape(channels, columns),
                (((1,), (1,)), ((), ())),
                preferred_element_type=F32,
            )
            total = term if total is None else total + term
        total = total.astype(BF16)
        results[0, tap], results[1, tap] = total[:, :half], total[:, half:]
        for copy in leaving(tap):
            copy.start()
        return carry

    lax.fori_loop(0, 9, tap_step, 0)
    for tap in range(9):
        finished(leaving(tap))


def conv_weight(me, core, scales, grads, feats):
    count = len(feats)
    split = len(grads) // count
    rows, own, columns = feats[0].shape
    channels = count * own
    return pl.pallas_call(
        functools.partial(weight_kernel, count, split),
        out_shape=[struct((9, channels, channels // 2), BF16)] * 2,
        in_specs=[IN_SMEM, IN_SMEM, IN_VMEM] + [IN_HBM] * (len(grads) + count),
        out_specs=[IN_HBM] * 2,
        scratch_shapes=[
            pltpu.VMEM((count, rows, own, columns), BF16),
            pltpu.VMEM((count, rows, own, columns), BF16),
            pltpu.VMEM((rows, 3, count, own, columns), BF16),
            pltpu.VMEM((rows - 2, count, own, columns), BF16),
            pltpu.VMEM((2, 9, channels, channels // 2), BF16),
            pltpu.VMEM((count, own, columns), F32),
            pltpu.SemaphoreType.DMA((max(18, len(grads) + count),)),
        ],
        compiler_params=PARAMS,
        name="conv_weight",
    )(me, core, scales, *grads, *feats)


def row_blocks(me, parts, rows_ref, start):
    count = len(parts)
    blocks = count // rows_ref.shape[0]
    span = parts[0].shape[0]
    pairs = []
    for x, part in enumerate(parts):
        source = me ^ x
        at = pl.ds(start + (source % blocks) * span, span)
        pairs.append((part, rows_ref.at[source // blocks, at]))
    return pairs


def rims_kernel(count, me_ref, *refs):
    parts, (first, last, arrived, sems) = refs[:count], refs[count:]
    rows = arrived.shape[1]
    finished(started(sems, 0, row_blocks(me_ref[0], parts, arrived, 0)))
    pairs = [
        (arrived.at[:, pl.ds(0, RIM)], first),
        (arrived.at[:, pl.ds(rows - RIM, RIM)], last),
    ]
    finished(started(sems, count, pairs))


def rims(me, parts, items):
    count = len(parts)
    span, width, columns = parts[0].shape
    rim = struct((items, RIM, width, columns), BF16)
    return pl.pallas_call(
        functools.partial(rims_kernel, count),
        out_shape=[rim, rim],
        in_specs=[IN_SMEM] + [IN_HBM] * count,
        out_specs=[IN_HBM] * 2,
        scratch_shapes=[
            pltpu.VMEM((items, span * count // items, width, columns), BF16),
            pltpu.SemaphoreType.DMA((count + 2,)),
        ],
        compiler_params=PARAMS,
        name="rims",
    )(me, *parts)


def sinc_kernel(count, first_channel, me_ref, edge_ref, demod, bias, up_sums, *refs):
    (before, after, cotangent), table_refs, parts = refs[:3], refs[3:7], refs[7 : 7 + count]
    refs = refs[7 + count + (first_channel > 0) :]
    (out, grad_bias, grad_demod), grad_parts = refs[:3], refs[3 : 3 + count]
    raw, cot, tables, out_rows, grad_raw = refs[3 + count : 8 + count]
    wide, wide_grad, narrow, narrow_grad, sems = refs[8 + count :]
    me = me_ref[0]
    items, extent, width, columns = raw.shape
    rows = extent - 2 * RIM
    first, last = edge_ref[0], edge_ref[1]
    tap = [float(value) for value in sinc_taps()[:6]]
    lane_tiles = 2 * columns // 128
    own_channels = pl.ds(first_channel, width)
    up_high, up_low, down_high, down_low = tables
    pairs = row_blocks(me, parts, raw, RIM) + list(zip(table_refs, tables))
    pairs += [
        (before, raw.at[:, pl.ds(0, RIM)]),
        (after, raw.at[:, pl.ds(RIM + rows, RIM)]),
        (cotangent.at[:, :, own_channels], cot),
    ]
    finished(started(sems, 0, pairs))

    def widened(values):
        flat = values.reshape(-1, columns)
        total = jnp.dot(flat, up_high[...], preferred_element_type=F32)
        total = total + jnp.dot(flat, up_low[...], preferred_element_type=F32)
        return total.reshape(-1, GROUP, 2 * columns)

    def narrowed(values):
        flat = values.reshape(-1, 2 * columns)
        high = flat.astype(BF16)
        low = (flat - high.astype(F32)).astype(BF16)
        total = jnp.dot(high, down_high[...], preferred_element_type=F32)
        total = total + jnp.dot(high, down_low[...], preferred_element_type=F32)
        total = total + jnp.dot(low, down_high[...], preferred_element_type=F32)
        return total.reshape(-1, GROUP, columns)

    def tile_step(index, carry):
        lanes = pl.ds(pl.multiple_of(lax.rem(index, lane_tiles) * 128, 128), 128)
        subs = pl.ds(pl.multiple_of(lax.div(index, lane_tiles) * 8, 8), 8)
        sums, picked = [{}, {}], [{}, {}]
        for row in range(extent):
            for which, ref in ((0, wide), (1, wide_grad)):
                value = ref[row, subs, lanes]
                products = [value * (2.0 * tap[t]) for t in range(6)]
                for offset in range(-3, 4):
                    pair = row - RIM + offset
                    for parity in range(2):
                        t = 2 * offset + parity + 5
                        if -4 <= pair < rows + 4 and 0 <= t < 12:
                            term = products[min(t, 11 - t)]
                            key = 2 * pair + parity
                            sums[which][key] = sums[which][key] + term if key in sums[which] else term
            pair = row - RIM - 3
            if pair < -4:
                continue
            for key in (2 * pair, 2 * pair + 1):
                value, grad = sums[0].pop(key), sums[1].pop(key)
                sigmoid = 1.0 / (1.0 + jnp.exp(-value))
                active = value * sigmoid
                grad = grad * (sigmoid + active * (1.0 - sigmoid))
                if pair < 0:
                    active, grad = active * first, grad * first
                if pair >= rows:
                    active, grad = active * last, grad * last
                picked[0][key], picked[1][key] = active, grad
            centre = pair - 3
            if centre >= -1:
                for which, ref in ((0, narrow), (1, narrow_grad)):
                    store = picked[which]
                    if which == 1 or 0 <= centre < rows:
                        total = None
                        for t in range(6):
                            term = tap[t] * (store[2 * centre + t - 5] + store[2 * centre + 6 - t])
                            total = term if total is None else total + term
                        ref[centre + which, subs, lanes] = total
                    for key in (2 * centre - 6, 2 * centre - 5, 2 * centre - 4):
                        store.pop(key, None)
        return carry

    leaving = []
    for item in range(items):
        for group in range(width // GROUP):
            at = slice(group * GROUP, (group + 1) * GROUP)
            scale = demod[item, at]
            shift = bias[at] * up_sums[...]
            spread = widened(raw[item, :, at]) * scale
            wide[:RIM] = spread[:RIM] + shift * first
            wide[RIM : RIM + rows] = spread[RIM : RIM + rows] + shift
            wide[RIM + rows :] = spread[RIM + rows :] + shift * last
            wide_grad[...] = widened(cot[item, :, at])
            lax.fori_loop(0, GROUP // 8 * lane_tiles, tile_step, 0)
            result = narrowed(narrow[...])
            out_rows[at, item] = jnp.swapaxes(result, 0, 1).astype(BF16)
            target = out.at[pl.ds(first_channel + group * GROUP, GROUP), item]
            source = out_rows.at[pl.ds(group * GROUP, GROUP), item]
            leaving += started(sems, len(leaving), [(source, target)])
            grad = narrowed(narrow_grad[...])
            scaled_grad = grad * scale
            grad_raw[item, 0, at] = (scaled_grad[0] * first).astype(BF16)
            grad_raw[item, 1 : rows + 1, at] = scaled_grad[1 : rows + 1].astype(BF16)
            grad_raw[item, rows + 1, at] = (scaled_grad[rows + 1] * last).astype(BF16)
            grad = grad[1 : rows + 1]
            own = raw[item, RIM : RIM + rows, at].astype(F32)
            grad_bias[item, at] = jnp.sum(jnp.sum(grad, axis=0), axis=1, keepdims=True)
            grad_demod[item, at] = jnp.sum(jnp.sum(grad * own, axis=0), axis=1, keepdims=True)
    blocks = count // items
    span = rows // blocks
    pairs = []
    for x in range(count):
        dest = me ^ x
        pairs.append((grad_raw.at[dest // blocks, pl.ds((dest % blocks) * span, span + 2)], grad_parts[x]))
    finished(leaving + started(sems, len(leaving), pairs))


def sinc_both(me, edges, demod, bias, tables, up_sums, before, after, cotangent, parts, out, first_channel):
    count = len(parts)
    items, extent, own, columns = cotangent.shape
    span, width, _ = parts[0].shape
    rows = extent - 2 * RIM
    wide = pltpu.VMEM((extent, GROUP, 2 * columns), F32)
    outs = pl.pallas_call(
        functools.partial(sinc_kernel, count, first_channel),
        out_shape=[
            struct((own, items, rows, columns), BF16),
            struct((items, width, 1), F32),
            struct((items, width, 1), F32),
        ]
        + [struct((span + 2, width, columns), BF16)] * count,
        in_specs=[IN_SMEM, IN_SMEM] + [IN_VMEM] * 3 + [IN_HBM] * (7 + count + len(out)),
        out_specs=[IN_HBM, IN_VMEM, IN_VMEM] + [IN_HBM] * count,
        input_output_aliases={12 + count: 0} if out else {},
        scratch_shapes=[
            pltpu.VMEM((items, extent, width, columns), BF16),
            pltpu.VMEM((items, extent, width, columns), BF16),
            [pltpu.VMEM(table.shape, BF16) for table in tables],
            pltpu.VMEM((width, items, rows, columns), BF16),
            pltpu.VMEM((items, rows + 2, width, columns), BF16),
            wide,
            wide,
            pltpu.VMEM((rows, GROUP, 2 * columns), F32),
            pltpu.VMEM((rows + 2, GROUP, 2 * columns), F32),
            pltpu.SemaphoreType.DMA((count + max(7, items * width // GROUP),)),
        ],
        compiler_params=PARAMS,
        name="sinc_both",
    )(me, edges, demod, bias, up_sums, before, after, cotangent, *tables, *parts, *out)
    return outs[0], outs[1], outs[2], outs[3:]


def scale_kernel(count, me_ref, scales, *refs):
    parts, (out, arrived, results, sems) = refs[:count], refs[count:]
    width, items, _, _ = out.shape
    finished(started(sems, 0, row_blocks(me_ref[0], parts, arrived, 0)))
    leaving = []
    for item in range(items):
        for group in range(width // GROUP):
            at = slice(group * GROUP, (group + 1) * GROUP)
            value = arrived[item, :, at].astype(F32) * scales[item, at]
            results[at, item] = jnp.swapaxes(value, 0, 1)
            spot = pl.ds(group * GROUP, GROUP)
            leaving += started(sems, len(leaving), [(results.at[spot, item], out.at[spot, item])])
    finished(leaving)


def scaled(me, scales, parts, items):
    count = len(parts)
    span, width, columns = parts[0].shape
    rows = span * count // items
    return pl.pallas_call(
        functools.partial(scale_kernel, count),
        out_shape=struct((width, items, rows, columns), F32),
        in_specs=[IN_SMEM, IN_VMEM] + [IN_HBM] * count,
        out_specs=IN_HBM,
        scratch_shapes=[
            pltpu.VMEM((items, rows, width, columns), BF16),
            pltpu.VMEM((width, items, rows, columns), F32),
            pltpu.SemaphoreType.DMA((max(count, items * width // GROUP),)),
        ],
        compiler_params=PARAMS,
        name="scale_features",
    )(me, scales, *parts)


def summed_everywhere(value):
    for axis in ("dp", "chan"):
        size = lax.axis_size(axis)
        bit = 1
        while bit < size:
            value = value + lax.ppermute(value, axis, [(i, i ^ bit) for i in range(size)])
            bit *= 2
    return value


def per_device(
    features,
    latent,
    affine,
    affine_bias,
    weight,
    out_bias,
    cotangent,
    latents_all,
    labels,
    class_means,
):
    highest = lax.Precision.HIGHEST
    own, items, rows, columns = features.shape
    channels = weight.shape[3]
    count = lax.axis_size("chan")
    dp_total = lax.axis_size("dp")
    me = lax.axis_index("chan")
    me_dp = lax.axis_index("dp")
    me_ref = me.astype(jnp.int32)[None]
    blocks = count // items
    span = rows // blocks
    split = max(1, min(2, own // GROUP))
    width = own // split

    before, after = from_neighbours(features, "dp", 2, 1)
    prepared = row_parts(me_ref, before, features, after, count)
    feats = exchange(prepared, "chan")
    core = (me_dp % 2).astype(jnp.int32)[None]
    pieces, places = weight_pieces(weight, me_dp, feats)
    part = (me_dp % (channels // pieces[0].shape[3])).astype(jnp.int32)[None]

    styles = jnp.dot(latent, affine, preferred_element_type=F32) + affine_bias
    own_style = lax.dynamic_slice_in_dim(styles, me * own, own, 1)
    weight_full = weight.astype(F32)
    weight_sq = jnp.sum(weight_full * weight_full, axis=(0, 1))
    demod = lax.rsqrt(jnp.dot(styles * styles, weight_sq.T, precision=highest) + 1e-08)
    item = me // blocks
    item_scales = lax.dynamic_index_in_dim(styles, item, 0, keepdims=False).reshape(count, own, 1)

    cot_before, cot_after = from_neighbours(cotangent, "dp", 2, RIM)
    cot = jnp.transpose(jnp.concatenate([cot_before, cotangent, cot_after], axis=2), (1, 2, 0, 3))
    table = up_table(columns)
    tables = halves(table) + halves(0.5 * table.T)
    up_sums = np.sum(table, axis=0)[None]
    edges = jnp.stack([me_dp > 0, me_dp < dp_total - 1]).astype(F32)

    raw_parts = conv_forward(me_ref, part, pieces, places, item_scales, feats, split)
    taps_backward = transposed_taps(
        me_ref, part, [once(piece, raw_parts[0][0]) for piece in pieces], places, channels
    )
    output, grad_parts, bias_parts, demod_parts = [], [], [], []
    up = [(i, i + 1) for i in range(dp_total - 1)]
    down = [(j, i) for i, j in up]
    for h in range(split):
        at = slice(h * width, (h + 1) * width)
        arrived = exchange(raw_parts[h], "chan")
        head, tail = rims(me_ref, arrived, items)
        result, bias_part, demod_part, parts = sinc_both(
            me_ref,
            edges,
            demod[:, at, None],
            out_bias[at, None],
            tables,
            up_sums,
            lax.ppermute(tail, "dp", up),
            lax.ppermute(head, "dp", down),
            cot,
            arrived,
            output,
            h * width,
        )
        output = [result]
        bias_parts.append(bias_part)
        demod_parts.append(demod_part)
        grad_parts += exchange(parts, "chan")
    output = output[0]
    bias_part = jnp.sum(jnp.concatenate(bias_parts, axis=1)[:, :, 0], axis=0)
    g_demod = jnp.concatenate(demod_parts, axis=1)[:, :, 0]

    keep, send = conv_weight(me_ref, core, item_scales, grad_parts, feats)
    modded_parts, style_part = conv_backward(me_ref, keep, taps_backward, grad_parts, feats)
    modded_parts = exchange(modded_parts, "chan")
    grad_features = scaled(me_ref, own_style[:, :, None], modded_parts, items)

    grad_bias, g_demod_sum = lax.psum((bias_part, g_demod), "dp")
    cube = demod * demod * demod
    g_style_part = 2.0 * styles * jnp.dot(-0.5 * g_demod * cube, weight_sq, precision=highest)
    g_style_part = g_style_part + jnp.where(
        jnp.arange(items)[:, None] == item, style_part.reshape(1, channels), 0.0
    )
    g_wsq = jnp.dot((-0.5 * g_demod_sum * cube).T, styles * styles, precision=highest)

    lane = channels // 2
    bit = 1
    while True:
        got = lax.ppermute(send, "dp", [(i, i ^ bit) for i in range(dp_total)])
        g_weight = keep.astype(F32) + got.astype(F32)
        bit *= 2
        if bit >= dp_total:
            break
        lane //= 2
        side = (me_dp // bit) % 2
        keep = lax.dynamic_slice_in_dim(g_weight, side * lane, lane, 2).astype(BF16)
        send = lax.dynamic_slice_in_dim(g_weight, (1 - side) * lane, lane, 2).astype(BF16)
    g_weight = g_weight.astype(BF16)
    g_weight = once(g_weight, *modded_parts)
    sent = [lax.dynamic_slice_in_dim(g_weight, (me ^ x) * own, own, 1) for x in range(count)]
    g_weight = sum(part.astype(F32) for part in exchange(sent, "chan"))
    while bit > 1:
        bit //= 2
        got = lax.ppermute(g_weight, "dp", [(i, i ^ bit) for i in range(dp_total)])
        upper = (me_dp // bit) % 2 == 1
        g_weight = jnp.concatenate(
            [jnp.where(upper, got, g_weight), jnp.where(upper, g_weight, got)], axis=2
        )
    grad_weight = g_weight.reshape(weight.shape) + 2.0 * weight_full * g_wsq

    tags = jnp.stack([labels // 64, labels % 64], axis=1).astype(BF16)
    tagged = jnp.concatenate([once(latents_all, head), jnp.pad(tags, ((0, 0), (0, 126)))], axis=1)
    tagged = lax.all_gather(tagged, ("dp", "chan"), axis=0, tiled=True)
    all_latents, tags = tagged[:, :-128], tagged[:, -128:-126].astype(F32)
    all_labels = (tags[:, 0] * 64.0 + tags[:, 1]).astype(jnp.int32)
    one_hot = all_labels[None, :] == jnp.arange(class_means.shape[0])[:, None]
    class_sums = jnp.dot(one_hot.astype(BF16), all_latents, preferred_element_type=F32)
    counts = jnp.sum(one_hot.astype(F32), axis=1)
    target = jnp.where(
        counts[:, None] > 0, class_sums / jnp.maximum(counts, 1.0)[:, None], class_means
    )

    g_style = summed_everywhere(g_style_part)
    grad_affine_bias = jnp.sum(g_style, axis=0)
    grad_affine = jnp.dot(latent.astype(F32).T, g_style, precision=highest)
    grad_latent = jnp.dot(g_style, affine.astype(F32).T, precision=highest)
    return (
        output,
        grad_features,
        grad_latent,
        grad_affine,
        grad_affine_bias,
        grad_weight,
        grad_bias,
        target,
    )


def solution(mesh):
    in_specs = (
        P("chan", None, "dp", None),
        P(),
        P(),
        P(),
        P(None, None, "chan", None),
        P("chan"),
        P("chan", None, "dp", None),
        P(("dp", "chan"), None),
        P(("dp", "chan")),
        P(),
    )
    out_specs = (
        P("chan", None, "dp", None),
        P("chan", None, "dp", None),
        P(),
        P(),
        P(),
        P(None, None, "chan", None),
        P("chan"),
        P(),
    )
    return jax.shard_map(
        per_device, mesh=mesh, in_specs=in_specs, out_specs=out_specs, check_vma=False
    )
```

time: 673 us -> 510 us (0.76)
  the two profiles are of different devices: /device:TPU:8 before, /device:TPU:0 now
where the time goes in v2:
time: 510 us; the launch traced here: 502 us
  starting transfers between devices  156 us (31%)
  waiting for transfers between devices  146 us (29%)
  Pallas kernels  128 us (25%)
  local copies, waits for them, and re-layouts  23.9 us (5%)
  other arithmetic  18.7 us (4%)
  between operations  15.4 us (3%)
  blocking collectives  8.25 us (2%)
  matrix products  6.22 us (1%)
    ppermute x61, waiting for transfers between devices, swapped(): lax.ppermute(value, axis, [(i, i ^ bits) for i in range(lax.axis_size(axi...  134 us
    ppermute x61, starting transfers between devices, swapped(): lax.ppermute(value, axis, [(i, i ^ bits) for i in range(lax.axis_size(axi...  132 us
    pallas_call x2, Pallas kernels, sinc_both(): pl.pallas_call(functools.partial(sinc_kernel, count, first_channel), out_...  55.8 us
    pallas_call x1, Pallas kernels, conv_backward(): pl.pallas_call(functools.partial(backward_kernel, count, split), out_shap...  17.8 us
    pallas_call x1, Pallas kernels, conv_forward(): pl.pallas_call(functools.partial(forward_kernel, count, places), out_shap...  17.7 us
    pallas_call x1, Pallas kernels, conv_weight(): pl.pallas_call(functools.partial(weight_kernel, count, split), out_shape=...  17.5 us
    unnamed x120, local copies, waits for them, and re-layouts  11.9 us
  transfers between devices with their start and end apart: 79, of which 25 were waited for; matrix products, arithmetic and copies ran while one was open for 7% of the time, Pallas kernels for 16%

profile of v2, /device:TPU:0, one launch (start us, length us, event | category | flops | bytes accessed | tf_op | source)
XLA Modules:
  0.0 501.7 jit_solution(3212022960753339729)
XLA Ops:
  8.2 4.1 collective-permute-start
  15.0 3.0 collective-permute-start.1
  19.7 4.9 row_parts.1
  32.2 5.2 %collective-permute-done.3.refs_15_.refs_23_ = bf16[10,64,256]{2,1,0:T(8,128)(2,1)S(1)} collective-permute-done((bf16[10,64,256]{2,1,0:T(8,128)(2,1)}, bf16[10,64,256]{2,1,0:T(8,128)(2,1)S(1)}, u32[]{:S(2)}, u32[]{:S(2)}) %collective-permute-start.3) | collective-permute-done | bytes 327712 | tf_op jit(solution)/shard_map/ppermute | solution.py:53
  38.8 17.2 %collective-permute-done.7 = bf16[2,9,64,128]{3,2,1,0:T(8,128)(2,1)S(1)} collective-permute-done((bf16[2,9,64,128]{3,2,1,0:T(8,128)(2,1)S(1)}, bf16[2,9,64,128]{3,2,1,0:T(8,128)(2,1)S(1)}, u32[]{:S(2)}, u32[]{:S(2)}) %collective-permute-start.7) | collective-permute-done | bytes 294944 | tf_op jit(solution)/shard_map/ppermute | solution.py:53
  61.3 6.1 %collective-permute-done.11.refs_14_.refs_22_ = bf16[10,64,256]{2,1,0:T(8,128)(2,1)S(1)} collective-permute-done((bf16[10,64,256]{2,1,0:T(8,128)(2,1)}, bf16[10,64,256]{2,1,0:T(8,128)(2,1)S(1)}, u32[]{:S(2)}, u32[]{:S(2)}) %collective-permute-start.11) | collective-permute-done | bytes 327712 | tf_op jit(solution)/shard_map/ppermute | solution.py:53
  67.4 7.6 %collective-permute-start.13 = (bf16[10,64,256]{2,1,0:T(8,128)(2,1)S(1)}, bf16[10,64,256]{2,1,0:T(8,128)(2,1)}, u32[]{:S(2)}, u32[]{:S(2)}) collective-permute-start(bf16[10,64,256]{2,1,0:T(8,128)(2,1)S(1)} %copy-done.53), channel_id=1, source_target_pairs={{0,4},{1,5},{2,6},{3,7},{4,0},{5,1},{6,2},{7,3},{8,12},{9,13},{10,... | collective-permute-start | bytes 983048 | tf_op jit(solution)/shard_map/ppermute | solution.py:53
  78.9 5.7 %collective-permute-done.12 = bf16[2,9,64,128]{3,2,1,0:T(8,128)(2,1)S(1)} collective-permute-done((bf16[2,9,64,128]{3,2,1,0:T(8,128)(2,1)S(1)}, bf16[2,9,64,128]{3,2,1,0:T(8,128)(2,1)S(1)}, u32[]{:S(2)}, u32[]{:S(2)}) %collective-permute-start.12) | collective-permute-done | bytes 294944 | tf_op jit(solution)/shard_map/ppermute | solution.py:53
  85.4 4.9 collective-permute-done.13.refs_12_.refs_20_
  93.8 2.8 copy.63
  97.5 4.2 collective-permute-done.20.refs_11_.refs_19_
  103.8 17.7 %conv_forward.1 = (bf16[8,32,256]{2,1,0:T(8,128)(2,1)}, bf16[8,32,256]{2,1,0:T(8,128)(2,1)}, bf16[8,32,256]{2,1,0:T(8,128)(2,1)}, bf16[8,32,256]{2,1,0:T(8,128)(...) custom-call(s32[1]{0:T(128)} %bitcast.me_ref, ...), custom_call_target="tpu_custom_call" | custom-call | tf_op jit(solution)/shard_map/conv_forward/pallas_call | solution.py:265
  125.0 3.2 collective-permute-start.24
  131.0 4.3 collective-permute-done.23.refs_3_.refs_10_
  141.1 2.5 collective-permute-done.34.refs_3_.refs_10_
  144.4 10.3 %collective-permute-start.38 = (bf16[8,32,256]{2,1,0:T(8,128)(2,1)}, bf16[8,32,256]{2,1,0:T(8,128)(2,1)S(1)}, u32[]{:S(2)}, u32[]{:S(2)}) collective-permute-start(bf16[8,32,256]{2,1,0:T(8,128)(2,1)} %get-tuple-element.112), channel_id=1, source_target_pairs={{0,7},{1,6},{2,5},{3,4},{4,3},{5,2},{6,1},{7,0},{8,15},{9,14},{10,... | collective-permute-start | bytes 393224 | tf_op jit(solution)/shard_map/ppermute | solution.py:53
  155.5 2.6 collective-permute-start.26
  159.6 5.1 %collective-permute-start.27 = (bf16[8,32,256]{2,1,0:T(8,128)(2,1)}, bf16[8,32,256]{2,1,0:T(8,128)(2,1)S(1)}, u32[]{:S(2)}, u32[]{:S(2)}) collective-permute-start(bf16[8,32,256]{2,1,0:T(8,128)(2,1)} %get-tuple-element.102), channel_id=1, source_target_pairs={{0,7},{1,6},{2,5},{3,4},{4,3},{5,2},{6,1},{7,0},{8,15},{9,14},{10,... | collective-permute-start | bytes 393224 | tf_op jit(solution)/shard_map/ppermute | solution.py:53
  166.9 7.3 %collective-permute-done.25.refs_5_.refs_12_ = bf16[8,32,256]{2,1,0:T(8,128)(2,1)S(1)} collective-permute-done((bf16[8,32,256]{2,1,0:T(8,128)(2,1)}, bf16[8,32,256]{2,1,0:T(8,128)(2,1)S(1)}, u32[]{:S(2)}, u32[]{:S(2)}) %collective-permute-start.25) | collective-permute-done | bytes 131104 | tf_op jit(solution)/shard_map/ppermute | solution.py:53
  174.2 2.7 collective-permute-start.39
  181.0 4.2 collective-permute-start.28
  189.9 3.1 maximum_bitcast_fusion.refs_2_
  193.0 27.9 %sinc_both.2 = (bf16[64,2,32,256]{3,2,1,0:T(8,128)(2,1)}, f32[2,32,1]{2,1,0:T(8,128)}, f32[2,32,1]{2,1,0:T(8,128)}, bf16[10,32,256]{2,1,0:T(8,128)(2,1)}, bf16[1...) custom-call(s32[1]{0:T(128)} %bitcast.me_ref, ...), custom_call_target="tpu_custom_call" | custom-call | tf_op jit(solution)/shard_map/sinc_both/pallas_call | solution.py:567
  221.6 27.9 %sinc_both.3 = (bf16[64,2,32,256]{3,2,1,0:T(8,128)(2,1)}, f32[2,32,1]{2,1,0:T(8,128)}, f32[2,32,1]{2,1,0:T(8,128)}, bf16[10,32,256]{2,1,0:T(8,128)(2,1)}, bf16[1...) custom-call(s32[1]{0:T(128)} %bitcast.me_ref, ...), custom_call_target="tpu_custom_call", output_to_operand_aliasing={{0}: (20, {})} | custom-call | tf_op jit(solution)/shard_map/sinc_both/pallas_call | solution.py:567
  253.3 3.3 collective-permute-start.51
  261.3 5.0 %collective-permute-done.50.refs_11_ = bf16[10,32,256]{2,1,0:T(8,128)(2,1)S(1)} collective-permute-done((bf16[10,32,256]{2,1,0:T(8,128)(2,1)}, bf16[10,32,256]{2,1,0:T(8,128)(2,1)S(1)}, u32[]{:S(2)}, u32[]{:S(2)}) %collective-permute-start.50) | collective-permute-done | bytes 163872 | tf_op jit(solution)/shard_map/ppermute | solution.py:53
  268.0 11.6 %collective-permute-done.52.refs_13_ = bf16[10,32,256]{2,1,0:T(8,128)(2,1)S(1)} collective-permute-done((bf16[10,32,256]{2,1,0:T(8,128)(2,1)}, bf16[10,32,256]{2,1,0:T(8,128)(2,1)S(1)}, u32[]{:S(2)}, u32[]{:S(2)}) %collective-permute-start.52) | collective-permute-done | bytes 163872 | tf_op jit(solution)/shard_map/ppermute | solution.py:53
  279.7 3.9 collective-permute-start.44
  283.6 6.7 %collective-permute-start.45 = (bf16[10,32,256]{2,1,0:T(8,128)(2,1)}, bf16[10,32,256]{2,1,0:T(8,128)(2,1)S(1)}, u32[]{:S(2)}, u32[]{:S(2)}) collective-permute-start(bf16[10,32,256]{2,1,0:T(8,128)(2,1)} %get-tuple-element.122), channel_id=1, source_target_pairs={{0,5},{1,4},{2,7},{3,6},{4,1},{5,0},{6,3},{7,2},{8,13},{9,12},{10,... | collective-permute-start | bytes 491528 | tf_op jit(solution)/shard_map/ppermute | solution.py:53
  295.8 13.7 %collective-permute-done.45.refs_5_ = bf16[10,32,256]{2,1,0:T(8,128)(2,1)S(1)} collective-permute-done((bf16[10,32,256]{2,1,0:T(8,128)(2,1)}, bf16[10,32,256]{2,1,0:T(8,128)(2,1)S(1)}, u32[]{:S(2)}, u32[]{:S(2)}) %collective-permute-start.45) | collective-permute-done | bytes 163872 | tf_op jit(solution)/shard_map/ppermute | solution.py:53
  310.3 17.5 %conv_weight.1 = (bf16[9,512,256]{2,1,0:T(8,128)(2,1)}, bf16[9,512,256]{2,1,0:T(8,128)(2,1)}) custom-call(s32[1]{0:T(128)} %bitcast.me_ref, s32[1]{0:T(128)} %bitcast.11.core_ref, f32[8,64,1]{2,1,0:T(8,128)} %reshape.60.scales, bf16[10,32,256]{2,1,0:T(8,128)(2,1)} %get-tuple-element.117.refs_0_, bf16[10,32,256]{2,1,0:T(8,128)(2,1)} %copy-done.18, ...), custom_call_target="tpu_custom_call" | custom-call | tf_op jit(solution)/shard_map/conv_weight/pallas_call | solution.py:386
  330.3 2.7 collective-permute-done.67
  334.4 3.0 convert_add_fusion
  340.9 5.2 %transposed_taps.1.taps_ref = bf16[9,512,512]{2,1,0:T(8,128)(2,1)} custom-call(s32[1]{0:T(128)} %bitcast.me_ref, s32[1]{0:T(128)} %bitcast.5.part_ref, bf16[4,9,64,128]{3,2,1,0:T(8,128)(2,1)} %copy-done.1, bf16[4,9,64,128]{3,2,1,0:T(8,128)(2,1)} %collective-permute-done.6.refs_1_, bf16[4,9,64,128]{3,2,1,0:T(8,128)(2,1)} %constant_dynamic-update-slice_fusion.refs_2_, ...), custom_call_target="tpu_custom_call" | custom-call | tf_op jit(solution)/shard_map/transposed_taps/pallas_call | solution.py:174
  346.1 17.8 %conv_backward.1 = (bf16[8,64,256]{2,1,0:T(8,128)(2,1)}, bf16[8,64,256]{2,1,0:T(8,128)(2,1)}, bf16[8,64,256]{2,1,0:T(8,128)(2,1)}, bf16[8,64,256]{2,1,0:T(8,128)...) custom-call(s32[1]{0:T(128)} %bitcast.me_ref, ...), custom_call_target="tpu_custom_call" | custom-call | tf_op jit(solution)/shard_map/conv_backward/pallas_call | solution.py:317
  364.6 5.8 %collective-permute-start.56 = (bf16[8,64,256]{2,1,0:T(8,128)(2,1)}, bf16[8,64,256]{2,1,0:T(8,128)(2,1)}, u32[]{:S(2)}, u32[]{:S(2)}) collective-permute-start(bf16[8,64,256]{2,1,0:T(8,128)(2,1)} %get-tuple-element.144), channel_id=1, source_target_pairs={{0,2},{1,3},{2,0},{3,1},{4,6},{5,7},{6,4},{7,5},{8,10},{9,11},{10,... | collective-permute-start | bytes 786440 | tf_op jit(solution)/shard_map/ppermute | solution.py:53
  375.2 3.6 collective-permute-start.59
  378.8 10.2 %collective-permute-done.56.refs_2_ = bf16[8,64,256]{2,1,0:T(8,128)(2,1)} collective-permute-done((bf16[8,64,256]{2,1,0:T(8,128)(2,1)}, bf16[8,64,256]{2,1,0:T(8,128)(2,1)}, u32[]{:S(2)}, u32[]{:S(2)}) %collective-permute-start.56) | collective-permute-done | bytes 262176 | tf_op jit(solution)/shard_map/ppermute | solution.py:53
  389.0 3.0 collective-permute-start.60
  392.0 3.0 collective-permute-start.61
  398.8 20.1 %collective-permute-done.59.refs_5_ = bf16[8,64,256]{2,1,0:T(8,128)(2,1)S(1)} collective-permute-done((bf16[8,64,256]{2,1,0:T(8,128)(2,1)}, bf16[8,64,256]{2,1,0:T(8,128)(2,1)S(1)}, u32[]{:S(2)}, u32[]{:S(2)}) %collective-permute-start.59) | collective-permute-done | bytes 262176 | tf_op jit(solution)/shard_map/ppermute | solution.py:53
  426.8 15.6 %collective-permute-start.73 = (bf16[9,64,128]{2,1,0:T(8,128)(2,1)S(1)}, bf16[9,64,128]{2,1,0:T(8,128)(2,1)S(1)}, u32[]{:S(2)}, u32[]{:S(2)}) collective-permute-start(bf16[9,64,128]{2,1,0:T(8,128)(2,1)S(1)} %get-tuple-element.201), channel_id=1, source_target_pairs={{0,5},{1,4},{2,7},{3,6},{4,1},{5,0},{6,3},{7,2},{8,13},{9,12},{10,... | collective-permute-start | bytes 442376 | tf_op jit(solution)/shard_map/ppermute | solution.py:53
  447.0 9.6 %collective-permute-done.73 = bf16[9,64,128]{2,1,0:T(8,128)(2,1)S(1)} collective-permute-done((bf16[9,64,128]{2,1,0:T(8,128)(2,1)S(1)}, bf16[9,64,128]{2,1,0:T(8,128)(2,1)S(1)}, u32[]{:S(2)}, u32[]{:S(2)}) %collective-permute-start.73) | collective-permute-done | bytes 147488 | tf_op jit(solution)/shard_map/ppermute | solution.py:53
  461.8 8.2 %all-reduce.1 = (f32[2,64]{1,0:T(2,128)S(1)}, f32[64]{0:T(128)}) all-reduce(f32[2,64]{1,0:T(2,128)S(1)} %maximum_bitcast_fusion.1, f32[64]{0:T(128)S(1)} %maximum_reduce_fusion), channel_id=1, replica_groups=mesh['dp'=4,'chan'=8] {'dp'}, use_global_device_ids=true, to_apply=%region_2.3 | all-reduce | flops 192 | bytes 1536 | tf_op jit(solution)/shard_map/psum | solution.py:725
  470.4 3.3 collective-permute-done.65
  474.9 3.3 collective-permute-done.66
  481.8 4.6 scale_features.1
  490.8 3.6 divide_select_fusion
  (302 shorter events, 117.4 us)
Async XLA Ops:
  7.2 480.8 %all-gather.2.cloned.1.call-start = ((), (), s32[]{:S(2)}) async-start(), calls=%async_computation | async-start | bytes 2703360 | tf_op jit(solution)/shard_map/all_gather | solution.py:760
  8.2 18.8 %collective-permute-start = (bf16[1,9,64,128]{3,2,1,0:T(8,128)(2,1)S(1)}, bf16[1,9,64,128]{3,2,1,0:T(8,128)(2,1)S(1)}, u32[]{:S(2)}, u32[]{:S(2)}) collective-permute-start(bf16[1,9,64,128]{3,2,1,0:T(8,128)(2,1)S(1)} %bitcast.34), channel_id=1, source_target_pairs={{0,4},{1,5},{2,6},{3,7},{4,0},{5,1},{6,2},{7,3},{8,12},{9,13},{10,... | collective-permute-start | bytes 442376 | tf_op jit(solution)/shard_map/ppermute | solution.py:53
  27.0 28.9 %collective-permute-start.7 = (bf16[2,9,64,128]{3,2,1,0:T(8,128)(2,1)S(1)}, bf16[2,9,64,128]{3,2,1,0:T(8,128)(2,1)S(1)}, u32[]{:S(2)}, u32[]{:S(2)}) collective-permute-start(bf16[2,9,64,128]{3,2,1,0:T(8,128)(2,1)S(1)} %pad_maximum_fusion.3), channel_id=1, source_target_pairs={{0,1},{1,0},{2,3},{3,2},{4,5},{5,4},{6,7},{7,6},{8,9},{9,8},{10,11... | collective-permute-start | bytes 884744 | tf_op jit(solution)/shard_map/ppermute | solution.py:53
  27.6 30.2 %collective-permute-start.15 = (bf16[2,9,64,128]{3,2,1,0:T(8,128)(2,1)S(1)}, bf16[2,9,64,128]{3,2,1,0:T(8,128)(2,1)S(1)}, u32[]{:S(2)}, u32[]{:S(2)}) collective-permute-start(bf16[2,9,64,128]{3,2,1,0:T(8,128)(2,1)S(1)} %pad_maximum_fusion.3), channel_id=1, source_target_pairs={{0,3},{1,2},{2,1},{3,0},{4,7},{5,6},{6,5},{7,4},{8,11},{9,10},{10,... | collective-permute-start | bytes 884744 | tf_op jit(solution)/shard_map/ppermute | solution.py:53
  28.1 31.3 %collective-permute-start.10 = (bf16[2,9,64,128]{3,2,1,0:T(8,128)(2,1)S(1)}, bf16[2,9,64,128]{3,2,1,0:T(8,128)(2,1)S(1)}, u32[]{:S(2)}, u32[]{:S(2)}) collective-permute-start(bf16[2,9,64,128]{3,2,1,0:T(8,128)(2,1)S(1)} %pad_maximum_fusion.3), channel_id=1, source_target_pairs={{0,2},{1,3},{2,0},{3,1},{4,6},{5,7},{6,4},{7,5},{8,10},{9,11},{10,... | collective-permute-start | bytes 884744 | tf_op jit(solution)/shard_map/ppermute | solution.py:53
  30.6 44.5 %collective-permute-start.5 = (bf16[10,64,256]{2,1,0:T(8,128)(2,1)}, bf16[10,64,256]{2,1,0:T(8,128)(2,1)S(1)}, u32[]{:S(2)}, u32[]{:S(2)}) collective-permute-start(bf16[10,64,256]{2,1,0:T(8,128)(2,1)} %get-tuple-element.85), channel_id=1, source_target_pairs={{0,5},{1,4},{2,7},{3,6},{4,1},{5,0},{6,3},{7,2},{8,13},{9,12},{10,... | collective-permute-start | bytes 983048 | tf_op jit(solution)/shard_map/ppermute | solution.py:53
  37.4 30.0 %collective-permute-start.11 = (bf16[10,64,256]{2,1,0:T(8,128)(2,1)}, bf16[10,64,256]{2,1,0:T(8,128)(2,1)S(1)}, u32[]{:S(2)}, u32[]{:S(2)}) collective-permute-start(bf16[10,64,256]{2,1,0:T(8,128)(2,1)} %get-tuple-element.87), channel_id=1, source_target_pairs={{0,6},{1,7},{2,4},{3,5},{4,2},{5,3},{6,0},{7,1},{8,14},{9,15},{10,... | collective-permute-start | bytes 983048 | tf_op jit(solution)/shard_map/ppermute | solution.py:53
  55.9 19.0 %collective-permute-start.4 = (bf16[2,9,64,128]{3,2,1,0:T(8,128)(2,1)S(1)}, bf16[2,9,64,128]{3,2,1,0:T(8,128)(2,1)S(1)}, u32[]{:S(2)}, u32[]{:S(2)}) collective-permute-start(bf16[2,9,64,128]{3,2,1,0:T(8,128)(2,1)S(1)} %pad_maximum_fusion.3), channel_id=1, source_target_pairs={{0,16},{8,24},{16,0},{24,8},{1,17},{9,25},{17,1},{25,9},{2,18},{10... | collective-permute-start | bytes 884744 | tf_op jit(solution)/shard_map/ppermute | solution.py:53
  57.8 18.0 %collective-permute-start.8 = (bf16[2,9,64,128]{3,2,1,0:T(8,128)(2,1)S(1)}, bf16[2,9,64,128]{3,2,1,0:T(8,128)(2,1)S(1)}, u32[]{:S(2)}, u32[]{:S(2)}) collective-permute-start(bf16[2,9,64,128]{3,2,1,0:T(8,128)(2,1)S(1)} %collective-permute-done.7), channel_id=1, source_target_pairs={{0,16},{8,24},{16,0},{24,8},{1,17},{9,25},{17,1},{25,9},{2,18},{10... | collective-permute-start | bytes 884744 | tf_op jit(solution)/shard_map/ppermute | solution.py:53
  59.4 18.8 %collective-permute-start.16 = (bf16[2,9,64,128]{3,2,1,0:T(8,128)(2,1)S(1)}, bf16[2,9,64,128]{3,2,1,0:T(8,128)(2,1)S(1)}, u32[]{:S(2)}, u32[]{:S(2)}) collective-permute-start(bf16[2,9,64,128]{3,2,1,0:T(8,128)(2,1)S(1)} %collective-permute-done.15), channel_id=1, source_target_pairs={{0,16},{8,24},{16,0},{24,8},{1,17},{9,25},{17,1},{25,9},{2,18},{10... | collective-permute-start | bytes 884744 | tf_op jit(solution)/shard_map/ppermute | solution.py:53
  67.4 22.9 %collective-permute-start.13 = (bf16[10,64,256]{2,1,0:T(8,128)(2,1)S(1)}, bf16[10,64,256]{2,1,0:T(8,128)(2,1)}, u32[]{:S(2)}, u32[]{:S(2)}) collective-permute-start(bf16[10,64,256]{2,1,0:T(8,128)(2,1)S(1)} %copy-done.53), channel_id=1, source_target_pairs={{0,4},{1,5},{2,6},{3,7},{4,0},{5,1},{6,2},{7,3},{8,12},{9,13},{10,... | collective-permute-start | bytes 983048 | tf_op jit(solution)/shard_map/ppermute | solution.py:53
  75.1 15.3 %collective-permute-start.18 = (bf16[10,64,256]{2,1,0:T(8,128)(2,1)S(1)}, bf16[10,64,256]{2,1,0:T(8,128)(2,1)}, u32[]{:S(2)}, u32[]{:S(2)}) collective-permute-start(bf16[10,64,256]{2,1,0:T(8,128)(2,1)S(1)} %copy-done.52), channel_id=1, source_target_pairs={{0,1},{1,0},{2,3},{3,2},{4,5},{5,4},{6,7},{7,6},{8,9},{9,8},{10,11... | collective-permute-start | bytes 983048 | tf_op jit(solution)/shard_map/ppermute | solution.py:53
  78.2 25.6 %collective-permute-start.6 = (bf16[4,9,64,128]{3,2,1,0:T(8,128)(2,1)S(1)}, bf16[4,9,64,128]{3,2,1,0:T(8,128)(2,1)}, u32[]{:S(2)}, u32[]{:S(2)}) collective-permute-start(bf16[4,9,64,128]{3,2,1,0:T(8,128)(2,1)S(1)} %pad_maximum_fusion.1.refs_0_), channel_id=1, source_target_pairs={{0,8},{8,0},{16,24},{24,16},{1,9},{9,1},{17,25},{25,17},{2,10},{10... | collective-permute-start | bytes 1769480 | tf_op jit(solution)/shard_map/ppermute | solution.py:53
  84.7 19.1 %collective-permute-start.17 = (bf16[4,9,64,128]{3,2,1,0:T(8,128)(2,1)}, bf16[4,9,64,128]{3,2,1,0:T(8,128)(2,1)}, u32[]{:S(2)}, u32[]{:S(2)}) collective-permute-start(bf16[4,9,64,128]{3,2,1,0:T(8,128)(2,1)} %constant_dynamic-update-slice_fusion.4.refs_6_), channel_id=1, source_target_pairs={{0,8},{8,0},{16,24},{24,16},{1,9},{9,1},{17,25},{25,17},{2,10},{10... | collective-permute-start | bytes 1769480 | tf_op jit(solution)/shard_map/ppermute | solution.py:53
  101.7 83.5 %collective-permute-start.30 = (bf16[64,2,7,256]{3,0,2,1:T(8,128)(2,1)}, bf16[64,2,7,256]{3,0,2,1:T(8,128)(2,1)}, u32[]{:S(2)}, u32[]{:S(2)}) collective-permute-start(bf16[64,2,7,256]{3,0,2,1:T(8,128)(2,1)} %get-tuple-element.192), channel_id=1, source_target_pairs={{0,8},{8,16},{16,24},{1,9},{9,17},{17,25},{2,10},{10,18},{18,26},{... | collective-permute-start | bytes 1376264 | tf_op jit(solution)/shard_map/ppermute | solution.py:49
  137.5 52.4 %collective-permute-start.31 = (bf16[64,2,7,256]{3,0,2,1:T(8,128)(2,1)}, bf16[64,2,7,256]{3,0,2,1:T(8,128)(2,1)}, u32[]{:S(2)}, u32[]{:S(2)}) collective-permute-start(bf16[64,2,7,256]{3,0,2,1:T(8,128)(2,1)} %get-tuple-element.193), channel_id=1, source_target_pairs={{8,0},{16,8},{24,16},{9,1},{17,9},{25,17},{10,2},{18,10},{26,18},{... | collective-permute-start | bytes 1376264 | tf_op jit(solution)/shard_map/ppermute | solution.py:49
  138.8 15.9 %collective-permute-start.36 = (bf16[8,32,256]{2,1,0:T(8,128)(2,1)}, bf16[8,32,256]{2,1,0:T(8,128)(2,1)S(1)}, u32[]{:S(2)}, u32[]{:S(2)}) collective-permute-start(bf16[8,32,256]{2,1,0:T(8,128)(2,1)} %get-tuple-element.110), channel_id=1, source_target_pairs={{0,5},{1,4},{2,7},{3,6},{4,1},{5,0},{6,3},{7,2},{8,13},{9,12},{10,... | collective-permute-start | bytes 393224 | tf_op jit(solution)/shard_map/ppermute | solution.py:53
  154.8 19.5 %collective-permute-start.25 = (bf16[8,32,256]{2,1,0:T(8,128)(2,1)}, bf16[8,32,256]{2,1,0:T(8,128)(2,1)S(1)}, u32[]{:S(2)}, u32[]{:S(2)}) collective-permute-start(bf16[8,32,256]{2,1,0:T(8,128)(2,1)} %get-tuple-element.100), channel_id=1, source_target_pairs={{0,5},{1,4},{2,7},{3,6},{4,1},{5,0},{6,3},{7,2},{8,13},{9,12},{10,... | collective-permute-start | bytes 393224 | tf_op jit(solution)/shard_map/ppermute | solution.py:53
  155.5 21.5 %collective-permute-start.26 = (bf16[8,32,256]{2,1,0:T(8,128)(2,1)}, bf16[8,32,256]{2,1,0:T(8,128)(2,1)S(1)}, u32[]{:S(2)}, u32[]{:S(2)}) collective-permute-start(bf16[8,32,256]{2,1,0:T(8,128)(2,1)} %get-tuple-element.101), channel_id=1, source_target_pairs={{0,6},{1,7},{2,4},{3,5},{4,2},{5,3},{6,0},{7,1},{8,14},{9,15},{10,... | collective-permute-start | bytes 393224 | tf_op jit(solution)/shard_map/ppermute | solution.py:53
  159.6 18.7 %collective-permute-start.27 = (bf16[8,32,256]{2,1,0:T(8,128)(2,1)}, bf16[8,32,256]{2,1,0:T(8,128)(2,1)S(1)}, u32[]{:S(2)}, u32[]{:S(2)}) collective-permute-start(bf16[8,32,256]{2,1,0:T(8,128)(2,1)} %get-tuple-element.102), channel_id=1, source_target_pairs={{0,7},{1,6},{2,5},{3,4},{4,3},{5,2},{6,1},{7,0},{8,15},{9,14},{10,... | collective-permute-start | bytes 393224 | tf_op jit(solution)/shard_map/ppermute | solution.py:53
  174.2 18.8 %collective-permute-start.39 = (bf16[2,7,32,256]{3,2,1,0:T(8,128)(2,1)}, bf16[2,7,32,256]{3,2,1,0:T(8,128)(2,1)}, u32[]{:S(2)}, u32[]{:S(2)}) collective-permute-start(bf16[2,7,32,256]{3,2,1,0:T(8,128)(2,1)} %get-tuple-element.113), channel_id=1, source_target_pairs={{0,8},{8,16},{16,24},{1,9},{9,17},{17,25},{2,10},{10,18},{18,26},{... | collective-permute-start | bytes 688136 | tf_op jit(solution)/shard_map/ppermute | solution.py:705
  176.9 16.1 %collective-permute-start.40 = (bf16[2,7,32,256]{3,2,1,0:T(8,128)(2,1)}, bf16[2,7,32,256]{3,2,1,0:T(8,128)(2,1)}, u32[]{:S(2)}, u32[]{:S(2)}) collective-permute-start(bf16[2,7,32,256]{3,2,1,0:T(8,128)(2,1)} %get-tuple-element.114), channel_id=1, source_target_pairs={{8,0},{16,8},{24,16},{9,1},{17,9},{25,17},{10,2},{18,10},{26,18},{... | collective-permute-start | bytes 688136 | tf_op jit(solution)/shard_map/ppermute | solution.py:706
  181.0 39.9 %collective-permute-start.28 = (bf16[2,7,32,256]{3,2,1,0:T(8,128)(2,1)}, bf16[2,7,32,256]{3,2,1,0:T(8,128)(2,1)S(1)}, u32[]{:S(2)}, u32[]{:S(2)}) collective-permute-start(bf16[2,7,32,256]{3,2,1,0:T(8,128)(2,1)} %get-tuple-element.103), channel_id=1, source_target_pairs={{0,8},{8,16},{16,24},{1,9},{9,17},{17,25},{2,10},{10,18},{18,26},{... | collective-permute-start | bytes 688136 | tf_op jit(solution)/shard_map/ppermute | solution.py:705
  185.2 35.7 %collective-permute-start.29 = (bf16[2,7,32,256]{3,2,1,0:T(8,128)(2,1)}, bf16[2,7,32,256]{3,2,1,0:T(8,128)(2,1)}, u32[]{:S(2)}, u32[]{:S(2)}) collective-permute-start(bf16[2,7,32,256]{3,2,1,0:T(8,128)(2,1)} %get-tuple-element.104), channel_id=1, source_target_pairs={{8,0},{16,8},{24,16},{9,1},{17,9},{25,17},{10,2},{18,10},{26,18},{... | collective-permute-start | bytes 688136 | tf_op jit(solution)/shard_map/ppermute | solution.py:706
  256.5 23.1 %collective-permute-start.52 = (bf16[10,32,256]{2,1,0:T(8,128)(2,1)}, bf16[10,32,256]{2,1,0:T(8,128)(2,1)S(1)}, u32[]{:S(2)}, u32[]{:S(2)}) collective-permute-start(bf16[10,32,256]{2,1,0:T(8,128)(2,1)} %get-tuple-element.130), channel_id=1, source_target_pairs={{0,5},{1,4},{2,7},{3,6},{4,1},{5,0},{6,3},{7,2},{8,13},{9,12},{10,... | collective-permute-start | bytes 491528 | tf_op jit(solution)/shard_map/ppermute | solution.py:53
  257.4 22.3 %collective-permute-start.53 = (bf16[10,32,256]{2,1,0:T(8,128)(2,1)}, bf16[10,32,256]{2,1,0:T(8,128)(2,1)S(1)}, u32[]{:S(2)}, u32[]{:S(2)}) collective-permute-start(bf16[10,32,256]{2,1,0:T(8,128)(2,1)} %get-tuple-element.131), channel_id=1, source_target_pairs={{0,6},{1,7},{2,4},{3,5},{4,2},{5,3},{6,0},{7,1},{8,14},{9,15},{10,... | collective-permute-start | bytes 491528 | tf_op jit(solution)/shard_map/ppermute | solution.py:53
  258.9 24.7 %collective-permute-start.54 = (bf16[10,32,256]{2,1,0:T(8,128)(2,1)}, bf16[10,32,256]{2,1,0:T(8,128)(2,1)S(1)}, u32[]{:S(2)}, u32[]{:S(2)}) collective-permute-start(bf16[10,32,256]{2,1,0:T(8,128)(2,1)} %get-tuple-element.132), channel_id=1, source_target_pairs={{0,7},{1,6},{2,5},{3,4},{4,3},{5,2},{6,1},{7,0},{8,15},{9,14},{10,... | collective-permute-start | bytes 491528 | tf_op jit(solution)/shard_map/ppermute | solution.py:53
  266.3 24.1 %collective-permute-start.41 = (bf16[10,32,256]{2,1,0:T(8,128)(2,1)S(1)}, bf16[10,32,256]{2,1,0:T(8,128)(2,1)S(1)}, u32[]{:S(2)}, u32[]{:S(2)}) collective-permute-start(bf16[10,32,256]{2,1,0:T(8,128)(2,1)S(1)} %copy-done.55), channel_id=1, source_target_pairs={{0,1},{1,0},{2,3},{3,2},{4,5},{5,4},{6,7},{7,6},{8,9},{9,8},{10,11... | collective-permute-start | bytes 491528 | tf_op jit(solution)/shard_map/ppermute | solution.py:53
  268.0 23.9 %collective-permute-start.42 = (bf16[10,32,256]{2,1,0:T(8,128)(2,1)S(1)}, bf16[10,32,256]{2,1,0:T(8,128)(2,1)S(1)}, u32[]{:S(2)}, u32[]{:S(2)}) collective-permute-start(bf16[10,32,256]{2,1,0:T(8,128)(2,1)S(1)} %copy-done.54), channel_id=1, source_target_pairs={{0,2},{1,3},{2,0},{3,1},{4,6},{5,7},{6,4},{7,5},{8,10},{9,11},{10,... | collective-permute-start | bytes 491528 | tf_op jit(solution)/shard_map/ppermute | solution.py:53
  279.7 16.1 %collective-permute-start.44 = (bf16[10,32,256]{2,1,0:T(8,128)(2,1)}, bf16[10,32,256]{2,1,0:T(8,128)(2,1)S(1)}, u32[]{:S(2)}, u32[]{:S(2)}) collective-permute-start(bf16[10,32,256]{2,1,0:T(8,128)(2,1)} %get-tuple-element.121), channel_id=1, source_target_pairs={{0,4},{1,5},{2,6},{3,7},{4,0},{5,1},{6,2},{7,3},{8,12},{9,13},{10,... | collective-permute-start | bytes 491528 | tf_op jit(solution)/shard_map/ppermute | solution.py:53
  283.6 25.9 %collective-permute-start.45 = (bf16[10,32,256]{2,1,0:T(8,128)(2,1)}, bf16[10,32,256]{2,1,0:T(8,128)(2,1)S(1)}, u32[]{:S(2)}, u32[]{:S(2)}) collective-permute-start(bf16[10,32,256]{2,1,0:T(8,128)(2,1)} %get-tuple-element.122), channel_id=1, source_target_pairs={{0,5},{1,4},{2,7},{3,6},{4,1},{5,0},{6,3},{7,2},{8,13},{9,12},{10,... | collective-permute-start | bytes 491528 | tf_op jit(solution)/shard_map/ppermute | solution.py:53
  290.4 19.2 %collective-permute-start.46 = (bf16[10,32,256]{2,1,0:T(8,128)(2,1)}, bf16[10,32,256]{2,1,0:T(8,128)(2,1)S(1)}, u32[]{:S(2)}, u32[]{:S(2)}) collective-permute-start(bf16[10,32,256]{2,1,0:T(8,128)(2,1)} %get-tuple-element.123), channel_id=1, source_target_pairs={{0,6},{1,7},{2,4},{3,5},{4,2},{5,3},{6,0},{7,1},{8,14},{9,15},{10,... | collective-permute-start | bytes 491528 | tf_op jit(solution)/shard_map/ppermute | solution.py:53
  291.9 17.7 %collective-permute-start.47 = (bf16[10,32,256]{2,1,0:T(8,128)(2,1)}, bf16[10,32,256]{2,1,0:T(8,128)(2,1)S(1)}, u32[]{:S(2)}, u32[]{:S(2)}) collective-permute-start(bf16[10,32,256]{2,1,0:T(8,128)(2,1)} %get-tuple-element.124), channel_id=1, source_target_pairs={{0,7},{1,6},{2,5},{3,4},{4,3},{5,2},{6,1},{7,0},{8,15},{9,14},{10,... | collective-permute-start | bytes 491528 | tf_op jit(solution)/shard_map/ppermute | solution.py:53
  338.6 53.4 %collective-permute-start.68 = (bf16[9,512,128]{2,1,0:T(8,128)(2,1)}, bf16[9,512,128]{2,1,0:T(8,128)(2,1)}, u32[]{:S(2)}, u32[]{:S(2)}) collective-permute-start(bf16[9,512,128]{2,1,0:T(8,128)(2,1)} %dynamic-slice_convert_fusion), channel_id=1, source_target_pairs={{0,16},{8,24},{16,0},{24,8},{1,17},{9,25},{17,1},{25,9},{2,18},{10... | collective-permute-start | bytes 3538952 | tf_op jit(solution)/shard_map/ppermute | solution.py:736
  364.6 24.5 %collective-permute-start.56 = (bf16[8,64,256]{2,1,0:T(8,128)(2,1)}, bf16[8,64,256]{2,1,0:T(8,128)(2,1)}, u32[]{:S(2)}, u32[]{:S(2)}) collective-permute-start(bf16[8,64,256]{2,1,0:T(8,128)(2,1)} %get-tuple-element.144), channel_id=1, source_target_pairs={{0,2},{1,3},{2,0},{3,1},{4,6},{5,7},{6,4},{7,5},{8,10},{9,11},{10,... | collective-permute-start | bytes 786440 | tf_op jit(solution)/shard_map/ppermute | solution.py:53
  372.3 26.4 %collective-permute-start.57 = (bf16[8,64,256]{2,1,0:T(8,128)(2,1)}, bf16[8,64,256]{2,1,0:T(8,128)(2,1)S(1)}, u32[]{:S(2)}, u32[]{:S(2)}) collective-permute-start(bf16[8,64,256]{2,1,0:T(8,128)(2,1)} %get-tuple-element.145), channel_id=1, source_target_pairs={{0,3},{1,2},{2,1},{3,0},{4,7},{5,6},{6,5},{7,4},{8,11},{9,10},{10,... | collective-permute-start | bytes 786440 | tf_op jit(solution)/shard_map/ppermute | solution.py:53
  373.2 25.6 %collective-permute-start.58 = (bf16[8,64,256]{2,1,0:T(8,128)(2,1)}, bf16[8,64,256]{2,1,0:T(8,128)(2,1)S(1)}, u32[]{:S(2)}, u32[]{:S(2)}) collective-permute-start(bf16[8,64,256]{2,1,0:T(8,128)(2,1)} %get-tuple-element.146), channel_id=1, source_target_pairs={{0,4},{1,5},{2,6},{3,7},{4,0},{5,1},{6,2},{7,3},{8,12},{9,13},{10,... | collective-permute-start | bytes 786440 | tf_op jit(solution)/shard_map/ppermute | solution.py:53
  375.2 43.6 %collective-permute-start.59 = (bf16[8,64,256]{2,1,0:T(8,128)(2,1)}, bf16[8,64,256]{2,1,0:T(8,128)(2,1)S(1)}, u32[]{:S(2)}, u32[]{:S(2)}) collective-permute-start(bf16[8,64,256]{2,1,0:T(8,128)(2,1)} %get-tuple-element.147), channel_id=1, source_target_pairs={{0,5},{1,4},{2,7},{3,6},{4,1},{5,0},{6,3},{7,2},{8,13},{9,12},{10,... | collective-permute-start | bytes 786440 | tf_op jit(solution)/shard_map/ppermute | solution.py:53
  389.0 29.8 %collective-permute-start.60 = (bf16[8,64,256]{2,1,0:T(8,128)(2,1)}, bf16[8,64,256]{2,1,0:T(8,128)(2,1)S(1)}, u32[]{:S(2)}, u32[]{:S(2)}) collective-permute-start(bf16[8,64,256]{2,1,0:T(8,128)(2,1)} %get-tuple-element.148), channel_id=1, source_target_pairs={{0,6},{1,7},{2,4},{3,5},{4,2},{5,3},{6,0},{7,1},{8,14},{9,15},{10,... | collective-permute-start | bytes 786440 | tf_op jit(solution)/shard_map/ppermute | solution.py:53
  392.0 26.8 %collective-permute-start.61 = (bf16[8,64,256]{2,1,0:T(8,128)(2,1)}, bf16[8,64,256]{2,1,0:T(8,128)(2,1)S(1)}, u32[]{:S(2)}, u32[]{:S(2)}) collective-permute-start(bf16[8,64,256]{2,1,0:T(8,128)(2,1)} %get-tuple-element.149), channel_id=1, source_target_pairs={{0,7},{1,6},{2,5},{3,4},{4,3},{5,2},{6,1},{7,0},{8,15},{9,14},{10,... | collective-permute-start | bytes 786440 | tf_op jit(solution)/shard_map/ppermute | solution.py:53
  419.0 24.5 %collective-permute-start.69 = (bf16[9,64,128]{2,1,0:T(8,128)(2,1)S(1)}, bf16[9,64,128]{2,1,0:T(8,128)(2,1)S(1)}, u32[]{:S(2)}, u32[]{:S(2)}) collective-permute-start(bf16[9,64,128]{2,1,0:T(8,128)(2,1)S(1)} %get-tuple-element.198), channel_id=1, source_target_pairs={{0,1},{1,0},{2,3},{3,2},{4,5},{5,4},{6,7},{7,6},{8,9},{9,8},{10,11... | collective-permute-start | bytes 442376 | tf_op jit(solution)/shard_map/ppermute | solution.py:53
  420.4 25.0 %collective-permute-start.75 = (bf16[9,64,128]{2,1,0:T(8,128)(2,1)S(1)}, bf16[9,64,128]{2,1,0:T(8,128)(2,1)S(1)}, u32[]{:S(2)}, u32[]{:S(2)}) collective-permute-start(bf16[9,64,128]{2,1,0:T(8,128)(2,1)S(1)} %get-tuple-element.199), channel_id=1, source_target_pairs={{0,7},{1,6},{2,5},{3,4},{4,3},{5,2},{6,1},{7,0},{8,15},{9,14},{10,... | collective-permute-start | bytes 442376 | tf_op jit(solution)/shard_map/ppermute | solution.py:53
  424.0 18.5 %collective-permute-start.63 = (f32[2,512]{1,0:T(2,128)S(1)}, f32[2,512]{1,0:T(2,128)S(1)}, u32[]{:S(2)}, u32[]{:S(2)}) collective-permute-start(f32[2,512]{1,0:T(2,128)S(1)} %add.147), channel_id=1, source_target_pairs={{0,16},{8,24},{16,0},{24,8},{1,17},{9,25},{17,1},{25,9},{2,18},{10... | collective-permute-start | bytes 12296 | tf_op jit(solution)/shard_map/ppermute | solution.py:635
  425.2 21.1 %collective-permute-start.74 = (bf16[9,64,128]{2,1,0:T(8,128)(2,1)S(1)}, bf16[9,64,128]{2,1,0:T(8,128)(2,1)S(1)}, u32[]{:S(2)}, u32[]{:S(2)}) collective-permute-start(bf16[9,64,128]{2,1,0:T(8,128)(2,1)S(1)} %get-tuple-element.200), channel_id=1, source_target_pairs={{0,6},{1,7},{2,4},{3,5},{4,2},{5,3},{6,0},{7,1},{8,14},{9,15},{10,... | collective-permute-start | bytes 442376 | tf_op jit(solution)/shard_map/ppermute | solution.py:53
  426.8 29.8 %collective-permute-start.73 = (bf16[9,64,128]{2,1,0:T(8,128)(2,1)S(1)}, bf16[9,64,128]{2,1,0:T(8,128)(2,1)S(1)}, u32[]{:S(2)}, u32[]{:S(2)}) collective-permute-start(bf16[9,64,128]{2,1,0:T(8,128)(2,1)S(1)} %get-tuple-element.201), channel_id=1, source_target_pairs={{0,5},{1,4},{2,7},{3,6},{4,1},{5,0},{6,3},{7,2},{8,13},{9,12},{10,... | collective-permute-start | bytes 442376 | tf_op jit(solution)/shard_map/ppermute | solution.py:53
  442.4 16.2 %collective-permute-start.72 = (bf16[9,64,128]{2,1,0:T(8,128)(2,1)S(1)}, bf16[9,64,128]{2,1,0:T(8,128)(2,1)S(1)}, u32[]{:S(2)}, u32[]{:S(2)}) collective-permute-start(bf16[9,64,128]{2,1,0:T(8,128)(2,1)S(1)} %get-tuple-element.202), channel_id=1, source_target_pairs={{0,4},{1,5},{2,6},{3,7},{4,0},{5,1},{6,2},{7,3},{8,12},{9,13},{10,... | collective-permute-start | bytes 442376 | tf_op jit(solution)/shard_map/ppermute | solution.py:53
  443.5 15.2 %collective-permute-start.71 = (bf16[9,64,128]{2,1,0:T(8,128)(2,1)S(1)}, bf16[9,64,128]{2,1,0:T(8,128)(2,1)S(1)}, u32[]{:S(2)}, u32[]{:S(2)}) collective-permute-start(bf16[9,64,128]{2,1,0:T(8,128)(2,1)S(1)} %get-tuple-element.203), channel_id=1, source_target_pairs={{0,3},{1,2},{2,1},{3,0},{4,7},{5,6},{6,5},{7,4},{8,11},{9,10},{10,... | collective-permute-start | bytes 442376 | tf_op jit(solution)/shard_map/ppermute | solution.py:53
  446.3 23.7 %collective-permute-start.64 = (f32[2,512]{1,0:T(2,128)S(1)}, f32[2,512]{1,0:T(2,128)S(1)}, u32[]{:S(2)}, u32[]{:S(2)}) collective-permute-start(f32[2,512]{1,0:T(2,128)S(1)} %add.148), channel_id=1, source_target_pairs={{0,1},{1,0},{2,3},{3,2},{4,5},{5,4},{6,7},{7,6},{8,9},{9,8},{10,11... | collective-permute-start | bytes 12296 | tf_op jit(solution)/shard_map/ppermute | solution.py:635
  (88 other events, 1675.8 us)
Sparse Core Ops, SparseCore 0:
  330.4 86.6 all-gather.1

commit v3 on v2

--- a/solution.py
+++ b/solution.py
@@ -57,9 +57,13 @@
     return lax.optimization_barrier((value,) + others)[0]
 
 
-def exchange(parts, axis):
-    size = lax.axis_size(axis)
-    return [parts[0]] + [swapped(parts[x], axis, x) for x in range(1, size)]
+def order(count, halved=False):
+    return list(range(count)) if halved else [0] + list(range(4, count)) + list(range(1, min(4, count)))
+
+
+def exchange(parts, axis, halved=False):
+    steps = order(lax.axis_size(axis), halved)
+    return [parts[0]] + [swapped(part, axis, x) for part, x in zip(parts[1:], steps[1:])]
 
 
 def started(sems, first, pairs):
@@ -91,10 +95,10 @@
         rows_first[item, 0] = before[:, item, 0]
         rows_first[item, rows + 1] = after[:, item, 0]
     pairs = []
-    for x in range(count):
+    for x, part in zip(order(count), parts):
         dest = me ^ x
         start = (dest % blocks) * span
-        pairs.append((rows_first.at[dest // blocks, pl.ds(start, span + 2)], parts[x]))
+        pairs.append((rows_first.at[dest // blocks, pl.ds(start, span + 2)], part))
     finished(started(sems, 1, pairs))
 
 
@@ -130,7 +134,7 @@
     pieces = [(held, places)]
     for x in range(1, min(size, 4)):
         pieces.append((swapped(held, "chan", x), [(chan ^ x, dp) for chan, dp in places]))
-    waits = [feats[-1:], (), feats[-2:-1], (), feats[-3:-2], (), feats[-4:-3], ()]
+    waits = [feats[1:2], (), feats[2:3], (), feats[3:4], (), feats[4:5], ()]
     bit = shares // 2
     while bit:
         met = []
@@ -187,19 +191,21 @@
 
 
 def arrivals(me, parts, arrived):
-    count = arrived.shape[0]
+    count, _, own, _ = arrived.shape
     width = parts[0].shape[1]
+    steps = order(count, width < own)
     return [
-        (part, arrived.at[me ^ (index % count), :, pl.ds(index // count * width, width)])
+        (part, arrived.at[me ^ steps[index % count], :, pl.ds(index // count * width, width)])
         for index, part in enumerate(parts)
     ]
 
 
 def departures(me, results, outs):
-    count = results.shape[1]
+    _, count, own, _ = results.shape
     width = outs[0].shape[1]
+    steps = order(count, width < own)
     return [
-        (results.at[:, me ^ (index % count), pl.ds(index // count * width, width)], out)
+        (results.at[:, me ^ steps[index % count], pl.ds(index // count * width, width)], out)
         for index, out in enumerate(outs)
     ]
 
@@ -258,164 +264,166 @@
     finished(started(sems, 0, departures(me, results, outs)))
 
 
-def conv_forward(me, part, pieces, places, scales, parts, split):
+def conv_forward(me, part, pieces, places, scales, parts):
     count = len(parts)
     rows, own, columns = parts[0].shape
     blocks = sum(len(place) for place in places)
-    outs = pl.pallas_call(
+    return pl.pallas_call(
         functools.partial(forward_kernel, count, places),
-        out_shape=[struct((rows - 2, own // split, columns), BF16)] * (count * split),
+        out_shape=[struct((rows - 2, own, columns), BF16)] * count,
         in_specs=[IN_SMEM, IN_SMEM, IN_VMEM] + [IN_HBM] * (len(pieces) + count),
-        out_specs=[IN_HBM] * (count * split),
+        out_specs=[IN_HBM] * count,
         scratch_shapes=[
             pltpu.VMEM((count, rows, own, columns), BF16),
             pltpu.VMEM((rows, 3, count, own, columns), BF16),
             pltpu.VMEM((9, count, own, count * own), BF16),
             pltpu.VMEM((rows - 2, count, own, columns), BF16),
             pltpu.VMEM((count, own, columns), F32),
-            pltpu.SemaphoreType.DMA((count * split + blocks,)),
+            pltpu.SemaphoreType.DMA((count + blocks,)),
         ],
         compiler_params=PARAMS,
         name="conv_forward",
     )(me, part, scales, *pieces, *parts)
-    return [outs[h * count : (h + 1) * count] for h in range(split)]
-
-
-def backward_kernel(count, split, me_ref, _, taps_ref, *refs):
+
+
+def backward_kernel(count, split, me_ref, scales, taps_ref, *refs):
     grads, refs = refs[: count * split], refs[count * split :]
-    feats, outs, style_ref = refs[:count], refs[count : 2 * count], refs[2 * count]
-    arrived, arrived_feats, shifted, taps, results, sems = refs[2 * count + 1 :]
+    feats, outs, (style_ref, weight_out) = refs[:count], refs[count : 2 * count], refs[2 * count : 2 * count + 2]
+    arrived, arrived_feats, shifted, modded, taps, results, weight_sums, wide_scales, sems = refs[2 * count + 2 :]
     me = me_ref[0]
     rows, _, own, columns = results.shape
+    channels = count * own
+    shares, _, _, share = weight_sums.shape
     arriving = started(sems, 0, arrivals(me, grads, arrived))
     tapping = started(
         sems,
         count * split,
         [(taps_ref, taps)] + arrivals(me, feats, arrived_feats),
     )
+    wide_scales[...] = jnp.broadcast_to(scales[...], wide_scales.shape)
     finished(arriving)
     fill_shifted(arrived, None, shifted)
     finished(tapping)
     style_ref[...] = jnp.zeros_like(style_ref)
 
     def row_step(row, carry):
-        total = convolved(taps, shifted, row, count * own, columns).reshape(count, own, columns)
+        total = convolved(taps, shifted, row, channels, columns).reshape(count, own, columns)
         results[row] = total.astype(BF16)
         product = total * arrived_feats[:, row + 1].astype(F32)
         style_ref[...] += jnp.sum(product, axis=2, keepdims=True)
         return carry
 
     lax.fori_loop(0, rows, row_step, 0)
-    finished(started(sems, 0, departures(me, results, outs)))
-
-
-def conv_backward(me, earlier, taps, grads, feats):
-    count = len(feats)
-    split = len(grads) // count
-    rows, own, columns = feats[0].shape
-    channels = count * own
-    outs = pl.pallas_call(
-        functools.partial(backward_kernel, count, split),
-        out_shape=[struct((rows - 2, own, columns), BF16)] * count + [struct((count, own, 1), F32)],
-        in_specs=[IN_SMEM] + [IN_HBM] * (2 + len(grads) + count),
-        out_specs=[IN_HBM] * count + [IN_VMEM],
-        scratch_shapes=[
-            pltpu.VMEM((count, rows, own, columns), BF16),
-            pltpu.VMEM((count, rows, own, columns), BF16),
-            pltpu.VMEM((rows, 3, count, own, columns), BF16),
-            pltpu.VMEM((9, channels, channels), BF16),
-            pltpu.VMEM((rows - 2, count, own, columns), BF16),
-            pltpu.SemaphoreType.DMA((len(grads) + count + 1,)),
-        ],
-        compiler_params=PARAMS,
-        name="conv_backward",
-    )(me, earlier, taps, *grads, *feats)
-    return outs[:-1], outs[-1]
-
-
-def weight_kernel(count, split, me_ref, core_ref, scales, *refs):
-    grads, refs = refs[: count * split], refs[count * split :]
-    feats, (keep, send) = refs[:count], refs[count : count + 2]
-    arrived, arrived_feats, shifted, rows_ref, results, wide_scales, sems = refs[count + 2 :]
-    me, core = me_ref[0], core_ref[0]
-    rows, _, own, columns = rows_ref.shape
-    channels = count * own
-    half = channels // 2
-    arriving = started(sems, 0, arrivals(me, feats, arrived_feats))
-    arriving_grads = started(sems, count, arrivals(me, grads, arrived))
-    wide_scales[...] = jnp.broadcast_to(scales[...], wide_scales.shape)
-    finished(arriving)
-    fill_shifted(arrived_feats, wide_scales, shifted)
-    finished(arriving_grads)
-    for source in range(count):
-        rows_ref[:, source] = arrived[source, 1 : rows + 1]
-
-    def leaving(tap):
-        return [
-            pltpu.make_async_copy(results.at[core, tap], keep.at[tap], sems.at[2 * tap]),
-            pltpu.make_async_copy(results.at[1 - core, tap], send.at[tap], sems.at[2 * tap + 1]),
-        ]
+    leaving = started(sems, 0, departures(me, results, outs))
+
+    def modded_step(row, carry):
+        for source in range(count):
+            value = arrived_feats[source, row].astype(F32) * wide_scales[source]
+            modded[row, source] = value.astype(BF16)
+        return carry
+
+    lax.fori_loop(0, rows + 2, modded_step, 0)
+
+    def weight_leaving(tap):
+        return pltpu.make_async_copy(weight_sums.at[:, tap], weight_out.at[:, tap], sems.at[count + tap])
 
     def tap_step(tap, carry):
         i, j = lax.div(tap, 3), lax.rem(tap, 3)
         total = None
         for row in range(rows):
             term = lax.dot_general(
-                rows_ref[row].reshape(channels, columns),
-                shifted[row + i, j].reshape(channels, columns),
+                shifted[row + 1, 2 - j].reshape(channels, columns),
+                modded[row + i].reshape(channels, columns),
                 (((1,), (1,)), ((), ())),
                 preferred_element_type=F32,
             )
             total = term if total is None else total + term
         total = total.astype(BF16)
-        results[0, tap], results[1, tap] = total[:, :half], total[:, half:]
-        for copy in leaving(tap):
-            copy.start()
+        for index in range(shares):
+            weight_sums[index, tap] = total[:, index * share : (index + 1) * share]
+        weight_leaving(tap).start()
         return carry
 
     lax.fori_loop(0, 9, tap_step, 0)
-    for tap in range(9):
-        finished(leaving(tap))
-
-
-def conv_weight(me, core, scales, grads, feats):
+    finished(leaving + [weight_leaving(tap) for tap in range(9)])
+
+
+def conv_backward(me, scales, taps, grads, feats, shares):
     count = len(feats)
     split = len(grads) // count
     rows, own, columns = feats[0].shape
     channels = count * own
-    return pl.pallas_call(
-        functools.partial(weight_kernel, count, split),
-        out_shape=[struct((9, channels, channels // 2), BF16)] * 2,
-        in_specs=[IN_SMEM, IN_SMEM, IN_VMEM] + [IN_HBM] * (len(grads) + count),
-        out_specs=[IN_HBM] * 2,
+    share = channels // shares
+    outs = pl.pallas_call(
+        functools.partial(backward_kernel, count, split),
+        out_shape=[struct((rows - 2, own, columns), BF16)] * count
+        + [struct((count, own, 1), F32), struct((shares, 9, channels, share), BF16)],
+        in_specs=[IN_SMEM, IN_VMEM] + [IN_HBM] * (1 + len(grads) + count),
+        out_specs=[IN_HBM] * count + [IN_VMEM, IN_HBM],
         scratch_shapes=[
             pltpu.VMEM((count, rows, own, columns), BF16),
             pltpu.VMEM((count, rows, own, columns), BF16),
             pltpu.VMEM((rows, 3, count, own, columns), BF16),
+            pltpu.VMEM((rows, count, own, columns), BF16),
+            pltpu.VMEM((9, channels, channels), BF16),
             pltpu.VMEM((rows - 2, count, own, columns), BF16),
-            pltpu.VMEM((2, 9, channels, channels // 2), BF16),
+            pltpu.VMEM((shares, 9, channels, share), BF16),
             pltpu.VMEM((count, own, columns), F32),
-            pltpu.SemaphoreType.DMA((max(18, len(grads) + count),)),
+            pltpu.SemaphoreType.DMA((count + max(9, len(grads) + 1),)),
         ],
         compiler_params=PARAMS,
-        name="conv_weight",
-    )(me, core, scales, *grads, *feats)
-
-
-def row_blocks(me, parts, rows_ref, start):
+        name="conv_backward",
+    )(me, scales, taps, *grads, *feats)
+    return outs[:-2], outs[-2], outs[-1]
+
+
+def finish_kernel(shares, part_ref, weight, factors, *refs):
+    pieces, (out, arrived, sems) = refs[:shares], refs[shares:]
+    part = part_ref[0]
+    share = pieces[0].shape[1]
+    taps, own, _ = out.shape
+    pairs = []
+    for x, piece in enumerate(pieces):
+        lanes = pl.ds(pl.multiple_of((part ^ x) * share, share), share)
+        pairs.append((piece.at[pl.ds(0, taps * own)], arrived.at[:, lanes]))
+    finished(started(sems, 0, pairs))
+    twice = 2.0 * factors[...]
+    for tap in range(taps):
+        out[tap] = arrived[tap * own : (tap + 1) * own].astype(F32) + twice * weight[tap].astype(F32)
+
+
+def finished_weight(part, weight, factors, pieces):
+    _, own, channels = weight.shape
+    shares = len(pieces)
+    return pl.pallas_call(
+        functools.partial(finish_kernel, shares),
+        out_shape=struct((9, own, channels), F32),
+        in_specs=[IN_SMEM, IN_VMEM, IN_VMEM] + [IN_HBM] * shares,
+        out_specs=IN_VMEM,
+        scratch_shapes=[
+            pltpu.VMEM((9 * own, channels), BF16),
+            pltpu.SemaphoreType.DMA((shares,)),
+        ],
+        compiler_params=PARAMS,
+        name="finished_weight",
+    )(part, weight, factors, *pieces)
+
+
+def row_blocks(me, parts, rows_ref, start, first_channel=0):
     count = len(parts)
     blocks = count // rows_ref.shape[0]
     span = parts[0].shape[0]
     pairs = []
-    for x, part in enumerate(parts):
+    channels = pl.ds(first_channel, rows_ref.shape[2])
+    for x, part in zip(order(count), parts):
         source = me ^ x
         at = pl.ds(start + (source % blocks) * span, span)
-        pairs.append((part, rows_ref.at[source // blocks, at]))
+        pairs.append((part.at[:, channels], rows_ref.at[source // blocks, at]))
     return pairs
 
 
 def rims_kernel(count, me_ref, *refs):
-    parts, (first, last, arrived, sems) = refs[:count], refs[count:]
+    parts, (first, last, arrived, sems) = refs[:count], refs[-4:]
     rows = arrived.shape[1]
     finished(started(sems, 0, row_blocks(me_ref[0], parts, arrived, 0)))
     pairs = [
@@ -425,14 +433,14 @@
     finished(started(sems, count, pairs))
 
 
-def rims(me, parts, items):
+def rims(me, parts, items, earlier):
     count = len(parts)
     span, width, columns = parts[0].shape
     rim = struct((items, RIM, width, columns), BF16)
     return pl.pallas_call(
         functools.partial(rims_kernel, count),
         out_shape=[rim, rim],
-        in_specs=[IN_SMEM] + [IN_HBM] * count,
+        in_specs=[IN_SMEM] + [IN_HBM] * (count + len(earlier)),
         out_specs=[IN_HBM] * 2,
         scratch_shapes=[
             pltpu.VMEM((items, span * count // items, width, columns), BF16),
@@ -440,7 +448,7 @@
         ],
         compiler_params=PARAMS,
         name="rims",
-    )(me, *parts)
+    )(me, *parts, *earlier)
 
 
 def sinc_kernel(count, first_channel, me_ref, edge_ref, demod, bias, up_sums, *refs):
@@ -457,10 +465,10 @@
     lane_tiles = 2 * columns // 128
     own_channels = pl.ds(first_channel, width)
     up_high, up_low, down_high, down_low = tables
-    pairs = row_blocks(me, parts, raw, RIM) + list(zip(table_refs, tables))
+    pairs = row_blocks(me, parts, raw, RIM, first_channel) + list(zip(table_refs, tables))
     pairs += [
-        (before, raw.at[:, pl.ds(0, RIM)]),
-        (after, raw.at[:, pl.ds(RIM + rows, RIM)]),
+        (before.at[:, :, own_channels], raw.at[:, pl.ds(0, RIM)]),
+        (after.at[:, :, own_channels], raw.at[:, pl.ds(RIM + rows, RIM)]),
         (cotangent.at[:, :, own_channels], cot),
     ]
     finished(started(sems, 0, pairs))
@@ -501,7 +509,7 @@
                 continue
             for key in (2 * pair, 2 * pair + 1):
                 value, grad = sums[0].pop(key), sums[1].pop(key)
-                sigmoid = 1.0 / (1.0 + jnp.exp(-value))
+                sigmoid = 0.5 + 0.5 * jnp.tanh(0.5 * value)
                 active = value * sigmoid
                 grad = grad * (sigmoid + active * (1.0 - sigmoid))
                 if pair < 0:
@@ -552,16 +560,16 @@
     blocks = count // items
     span = rows // blocks
     pairs = []
-    for x in range(count):
+    for x, part in zip(order(count, width < cotangent.shape[2]), grad_parts):
         dest = me ^ x
-        pairs.append((grad_raw.at[dest // blocks, pl.ds((dest % blocks) * span, span + 2)], grad_parts[x]))
+        pairs.append((grad_raw.at[dest // blocks, pl.ds((dest % blocks) * span, span + 2)], part))
     finished(leaving + started(sems, len(leaving), pairs))
 
 
 def sinc_both(me, edges, demod, bias, tables, up_sums, before, after, cotangent, parts, out, first_channel):
     count = len(parts)
     items, extent, own, columns = cotangent.shape
-    span, width, _ = parts[0].shape
+    span, width = parts[0].shape[0], demod.shape[1]
     rows = extent - 2 * RIM
     wide = pltpu.VMEM((extent, GROUP, 2 * columns), F32)
     outs = pl.pallas_call(
@@ -627,14 +635,24 @@
     )(me, scales, *parts)
 
 
-def summed_everywhere(value):
-    for axis in ("dp", "chan"):
-        size = lax.axis_size(axis)
-        bit = 1
-        while bit < size:
-            value = value + lax.ppermute(value, axis, [(i, i ^ bit) for i in range(size)])
-            bit *= 2
-    return value
+def in_thirds(value, lanes):
+    terms = []
+    for _ in range(3):
+        terms.append(lax.reduce_precision(value, 8, 7))
+        value = value - terms[-1]
+    rows = jnp.stack(terms).astype(BF16).reshape(-1, lanes)
+    return jnp.pad(rows, ((0, -rows.shape[0] % 16), (0, 0)))
+
+
+def from_thirds(rows, shape):
+    terms = rows.astype(F32).reshape(-1)[: 3 * shape[0] * shape[1]].reshape((3,) + shape)
+    return terms[0] + terms[1] + terms[2]
+
+
+def tree_sum(values):
+    while len(values) > 1:
+        values = [a + b for a, b in zip(values[::2], values[1::2])]
+    return values[0]
 
 
 def per_device(
@@ -665,7 +683,6 @@
     before, after = from_neighbours(features, "dp", 2, 1)
     prepared = row_parts(me_ref, before, features, after, count)
     feats = exchange(prepared, "chan")
-    core = (me_dp % 2).astype(jnp.int32)[None]
     pieces, places = weight_pieces(weight, me_dp, feats)
     part = (me_dp % (channels // pieces[0].shape[3])).astype(jnp.int32)[None]
 
@@ -684,17 +701,18 @@
     up_sums = np.sum(table, axis=0)[None]
     edges = jnp.stack([me_dp > 0, me_dp < dp_total - 1]).astype(F32)
 
-    raw_parts = conv_forward(me_ref, part, pieces, places, item_scales, feats, split)
+    raw_parts = conv_forward(me_ref, part, pieces, places, item_scales, feats)
     taps_backward = transposed_taps(
-        me_ref, part, [once(piece, raw_parts[0][0]) for piece in pieces], places, channels
+        me_ref, part, [once(piece, raw_parts[0]) for piece in pieces], places, channels
     )
     output, grad_parts, bias_parts, demod_parts = [], [], [], []
     up = [(i, i + 1) for i in range(dp_total - 1)]
     down = [(j, i) for i, j in up]
+    arrived = exchange(raw_parts, "chan")
+    head, tail = rims(me_ref, arrived, items, [taps_backward, cot])
+    before, after = lax.ppermute(tail, "dp", up), lax.ppermute(head, "dp", down)
     for h in range(split):
         at = slice(h * width, (h + 1) * width)
-        arrived = exchange(raw_parts[h], "chan")
-        head, tail = rims(me_ref, arrived, items)
         result, bias_part, demod_part, parts = sinc_both(
             me_ref,
             edges,
@@ -702,8 +720,8 @@
             out_bias[at, None],
             tables,
             up_sums,
-            lax.ppermute(tail, "dp", up),
-            lax.ppermute(head, "dp", down),
+            before,
+            after,
             cot,
             arrived,
             output,
@@ -712,48 +730,26 @@
         output = [result]
         bias_parts.append(bias_part)
         demod_parts.append(demod_part)
-        grad_parts += exchange(parts, "chan")
+        if h:
+            parts = [once(part, *grad_parts[-4:]) for part in parts]
+        grad_parts += exchange(parts, "chan", split > 1)
     output = output[0]
     bias_part = jnp.sum(jnp.concatenate(bias_parts, axis=1)[:, :, 0], axis=0)
     g_demod = jnp.concatenate(demod_parts, axis=1)[:, :, 0]
 
-    keep, send = conv_weight(me_ref, core, item_scales, grad_parts, feats)
-    modded_parts, style_part = conv_backward(me_ref, keep, taps_backward, grad_parts, feats)
+    modded_parts, style_part, weight_sums = conv_backward(
+        me_ref, item_scales, taps_backward, grad_parts, feats, dp_total
+    )
     modded_parts = exchange(modded_parts, "chan")
     grad_features = scaled(me_ref, own_style[:, :, None], modded_parts, items)
 
-    grad_bias, g_demod_sum = lax.psum((bias_part, g_demod), "dp")
+    grad_bias, g_demod_sum = lax.psum((once(bias_part, style_part), g_demod), "dp")
     cube = demod * demod * demod
     g_style_part = 2.0 * styles * jnp.dot(-0.5 * g_demod * cube, weight_sq, precision=highest)
     g_style_part = g_style_part + jnp.where(
         jnp.arange(items)[:, None] == item, style_part.reshape(1, channels), 0.0
     )
     g_wsq = jnp.dot((-0.5 * g_demod_sum * cube).T, styles * styles, precision=highest)
-
-    lane = channels // 2
-    bit = 1
-    while True:
-        got = lax.ppermute(send, "dp", [(i, i ^ bit) for i in range(dp_total)])
-        g_weight = keep.astype(F32) + got.astype(F32)
-        bit *= 2
-        if bit >= dp_total:
-            break
-        lane //= 2
-        side = (me_dp // bit) % 2
-        keep = lax.dynamic_slice_in_dim(g_weight, side * lane, lane, 2).astype(BF16)
-        send = lax.dynamic_slice_in_dim(g_weight, (1 - side) * lane, lane, 2).astype(BF16)
-    g_weight = g_weight.astype(BF16)
-    g_weight = once(g_weight, *modded_parts)
-    sent = [lax.dynamic_slice_in_dim(g_weight, (me ^ x) * own, own, 1) for x in range(count)]
-    g_weight = sum(part.astype(F32) for part in exchange(sent, "chan"))
-    while bit > 1:
-        bit //= 2
-        got = lax.ppermute(g_weight, "dp", [(i, i ^ bit) for i in range(dp_total)])
-        upper = (me_dp // bit) % 2 == 1
-        g_weight = jnp.concatenate(
-            [jnp.where(upper, got, g_weight), jnp.where(upper, g_weight, got)], axis=2
-        )
-    grad_weight = g_weight.reshape(weight.shape) + 2.0 * weight_full * g_wsq
 
     tags = jnp.stack([labels // 64, labels % 64], axis=1).astype(BF16)
     tagged = jnp.concatenate([once(latents_all, head), jnp.pad(tags, ((0, 0), (0, 126)))], axis=1)
@@ -767,7 +763,30 @@
         counts[:, None] > 0, class_sums / jnp.maximum(counts, 1.0)[:, None], class_means
     )
 
-    g_style = summed_everywhere(g_style_part)
+    share = channels // dp_total
+    weight_sums = weight_sums.reshape(dp_total * 9 * channels, share)
+    weight_sums = lax.psum_scatter(weight_sums, "dp", scatter_dimension=0, tiled=True)
+    weight_sums = once(weight_sums.reshape(9, channels, share), *modded_parts, g_wsq, grad_bias, target)
+    thirds = in_thirds(g_style_part, share)
+    sent = []
+    for x in order(count):
+        part_x = lax.dynamic_slice_in_dim(weight_sums, (me ^ x) * own, own, 1)
+        sent.append(jnp.concatenate([part_x.reshape(9 * own, share), thirds], axis=0))
+    sent = exchange(sent, "chan")
+    g_weight = sum(value[: 9 * own].astype(F32) for value in sent).astype(BF16)
+    style_sums = [from_thirds(value[9 * own :], styles.shape) for value in sent]
+    g_style = tree_sum([style_sums[order(count).index(x)] for x in range(count)])
+    sent = once(jnp.concatenate([g_weight, in_thirds(g_style, share)], axis=0), grad_features)
+    met = [sent] + [swapped(sent, "dp", x) for x in range(1, dp_total)]
+    if share % 128 == 0:
+        me_dp_ref = me_dp.astype(jnp.int32)[None]
+        grad_weight = finished_weight(me_dp_ref, weight.reshape(9, own, channels), g_wsq, met)
+    else:
+        blocks = lax.all_gather(met[0][: 9 * own], "dp", axis=1, tiled=True)
+        grad_weight = blocks.reshape(9, own, channels).astype(F32)
+        grad_weight = grad_weight + 2.0 * weight_full.reshape(9, own, channels) * g_wsq
+    grad_weight = grad_weight.reshape(weight.shape)
+    g_style = tree_sum([from_thirds(value[9 * own :], styles.shape) for value in met])
     grad_affine_bias = jnp.sum(g_style, axis=0)
     grad_affine = jnp.dot(latent.astype(F32).T, g_style, precision=highest)
     grad_latent = jnp.dot(g_style, affine.astype(F32).T, precision=highest)

time: 510 us -> 440 us (0.86)
  starting transfers between devices: 156 us -> 125 us
  waiting for transfers between devices: 146 us -> 120 us
  other arithmetic: 18.7 us -> 8.8 us
    ppermute x61 -> x57, starting transfers between devices: 132 us -> 113 us  [swapped(): lax.ppermute(value, axis, [(i, i ^ bits) for i in range(lax.axis_size(axi...]
    ppermute x61 -> x57, waiting for transfers between devices: 134 us -> 116 us  [swapped(): lax.ppermute(value, axis, [(i, i ^ bits) for i in range(lax.axis_size(axi...]
    pallas_call x1, Pallas kernels: 17.5 us -> 3.44 us  [finished_weight(): pl.pallas_call(functools.partial(finish_kernel, shares), out_shape=struct...]
    pallas_call x1, Pallas kernels: 17.8 us -> 30.3 us  [conv_backward(): pl.pallas_call(functools.partial(backward_kernel, count, split), out_shap...]
    ppermute x9 -> x0, waiting for transfers between devices: 10.4 us -> none  [the longest x5 7.68 us: summed_everywhere(): lax.ppermute(value, axis, [(i, i ^ bit) for i in range(size)])]
    ppermute x9 -> x0, starting transfers between devices: 6.28 us -> none  [the longest x2 3.02 us: per_device(): got = lax.ppermute(send, 'dp', [(i, i ^ bit) for i in range(dp_total)])]
    add x7 -> x2, other arithmetic: 5.36 us -> 0.02 us  [tree_sum(): values = [a + b for a, b in zip(values[::2], values[1::2])]]
    unnamed x120 -> x126, local copies, waits for them, and re-layouts: 11.9 us -> 9.99 us
  transfers between devices with their start and end apart: 79 -> 65, of which waited for: 25 -> 22; matrix products, arithmetic and copies ran while one was open for 7% -> 7% of each run, Pallas kernels for 16% -> 27%
where the time goes in v3:
time: 440 us; the launch traced here: 433 us
  starting transfers between devices  125 us (28%)
  Pallas kernels  123 us (28%)
  waiting for transfers between devices  120 us (27%)
  local copies, waits for them, and re-layouts  22.2 us (5%)
  between operations  16.9 us (4%)
  other arithmetic  8.8 us (2%)
  matrix products  8.23 us (2%)
  blocking collectives  8.18 us (2%)
    ppermute x57, waiting for transfers between devices, swapped(): lax.ppermute(value, axis, [(i, i ^ bits) for i in range(lax.axis_size(axi...  116 us
    ppermute x57, starting transfers between devices, swapped(): lax.ppermute(value, axis, [(i, i ^ bits) for i in range(lax.axis_size(axi...  113 us
    pallas_call x2, Pallas kernels, sinc_both(): pl.pallas_call(functools.partial(sinc_kernel, count, first_channel), out_...  55.1 us
    pallas_call x1, Pallas kernels, conv_backward(): pl.pallas_call(functools.partial(backward_kernel, count, split), out_shap...  30.3 us
    pallas_call x1, Pallas kernels, conv_forward(): pl.pallas_call(functools.partial(forward_kernel, count, places), out_shap...  17.5 us
    unnamed x126, local copies, waits for them, and re-layouts  9.99 us
  transfers between devices with their start and end apart: 65, of which 22 were waited for; matrix products, arithmetic and copies ran while one was open for 7% of the time, Pallas kernels for 27%

profile of v3, /device:TPU:0, one launch (start us, length us, event | category | flops | bytes accessed | tf_op | source)
XLA Modules:
  0.0 433.1 jit_solution(9217482264713194659)
XLA Ops:
  9.1 4.1 collective-permute-start
  17.4 3.5 collective-permute-done.2.after
  21.5 4.9 %row_parts.1 = (bf16[10,64,256]{2,1,0:T(8,128)(2,1)}, bf16[10,64,256]{2,1,0:T(8,128)(2,1)}, bf16[10,64,256]{2,1,0:T(8,128)(2,1)}, bf16[10,64,256]{2,1,0:T(8,128)...) custom-call(s32[1]{0:T(128)} %bitcast.me_ref, ...), custom_call_target="tpu_custom_call" | custom-call | tf_op jit(solution)/shard_map/row_parts/pallas_call | solution.py:108
  30.0 2.5 collective-permute-start.11
  33.9 11.2 %collective-permute-done.3.refs_9_.refs_17_ = bf16[10,64,256]{2,1,0:T(8,128)(2,1)S(1)} collective-permute-done((bf16[10,64,256]{2,1,0:T(8,128)(2,1)}, bf16[10,64,256]{2,1,0:T(8,128)(2,1)S(1)}, u32[]{:S(2)}, u32[]{:S(2)}) %collective-permute-start.3) | collective-permute-done | bytes 327712 | tf_op jit(solution)/shard_map/ppermute | solution.py:53
  45.2 6.2 %collective-permute-start.5 = (bf16[10,64,256]{2,1,0:T(8,128)(2,1)}, bf16[10,64,256]{2,1,0:T(8,128)(2,1)S(1)}, u32[]{:S(2)}, u32[]{:S(2)}) collective-permute-start(bf16[10,64,256]{2,1,0:T(8,128)(2,1)} %get-tuple-element.84), channel_id=1, source_target_pairs={{0,6},{1,7},{2,4},{3,5},{4,2},{5,3},{6,0},{7,1},{8,14},{9,15},{10,... | collective-permute-start | bytes 983048 | tf_op jit(solution)/shard_map/ppermute | solution.py:53
  54.9 6.2 %collective-permute-done.11.refs_10_.refs_18_ = bf16[10,64,256]{2,1,0:T(8,128)(2,1)S(1)} collective-permute-done((bf16[10,64,256]{2,1,0:T(8,128)(2,1)}, bf16[10,64,256]{2,1,0:T(8,128)(2,1)S(1)}, u32[]{:S(2)}, u32[]{:S(2)}) %collective-permute-start.11) | collective-permute-done | bytes 327712 | tf_op jit(solution)/shard_map/ppermute | solution.py:53
  61.0 7.4 %collective-permute-start.13 = (bf16[10,64,256]{2,1,0:T(8,128)(2,1)}, bf16[10,64,256]{2,1,0:T(8,128)(2,1)S(1)}, u32[]{:S(2)}, u32[]{:S(2)}) collective-permute-start(bf16[10,64,256]{2,1,0:T(8,128)(2,1)} %get-tuple-element.88), channel_id=1, source_target_pairs={{0,7},{1,6},{2,5},{3,4},{4,3},{5,2},{6,1},{7,0},{8,15},{9,14},{10,... | collective-permute-start | bytes 983048 | tf_op jit(solution)/shard_map/ppermute | solution.py:53
  72.9 8.5 %collective-permute-start.19 = (bf16[10,64,256]{2,1,0:T(8,128)(2,1)S(1)}, bf16[10,64,256]{2,1,0:T(8,128)(2,1)S(1)}, u32[]{:S(2)}, u32[]{:S(2)}) collective-permute-start(bf16[10,64,256]{2,1,0:T(8,128)(2,1)S(1)} %copy-done.52), channel_id=1, source_target_pairs={{0,2},{1,3},{2,0},{3,1},{4,6},{5,7},{6,4},{7,5},{8,10},{9,11},{10,... | collective-permute-start | bytes 983048 | tf_op jit(solution)/shard_map/ppermute | solution.py:53
  86.0 2.4 collective-permute-done.19.refs_14_.refs_22_
  88.5 7.4 %collective-permute-start.20 = (bf16[10,64,256]{2,1,0:T(8,128)(2,1)}, bf16[10,64,256]{2,1,0:T(8,128)(2,1)S(1)}, u32[]{:S(2)}, u32[]{:S(2)}) collective-permute-start(bf16[10,64,256]{2,1,0:T(8,128)(2,1)} %get-tuple-element.93), channel_id=1, source_target_pairs={{0,3},{1,2},{2,1},{3,0},{4,7},{5,6},{6,5},{7,4},{8,11},{9,10},{10,... | collective-permute-start | bytes 983048 | tf_op jit(solution)/shard_map/ppermute | solution.py:53
  96.0 2.8 copy.63
  99.7 4.6 %collective-permute-done.20.refs_15_.refs_23_ = bf16[10,64,256]{2,1,0:T(8,128)(2,1)S(1)} collective-permute-done((bf16[10,64,256]{2,1,0:T(8,128)(2,1)}, bf16[10,64,256]{2,1,0:T(8,128)(2,1)S(1)}, u32[]{:S(2)}, u32[]{:S(2)}) %collective-permute-start.20) | collective-permute-done | bytes 327712 | tf_op jit(solution)/shard_map/ppermute | solution.py:53
  105.7 3.8 collective-permute-start.28
  110.7 17.5 %conv_forward.1 = (bf16[8,64,256]{2,1,0:T(8,128)(2,1)}, bf16[8,64,256]{2,1,0:T(8,128)(2,1)}, bf16[8,64,256]{2,1,0:T(8,128)(2,1)}, bf16[8,64,256]{2,1,0:T(8,128)(...) custom-call(s32[1]{0:T(128)} %bitcast.me_ref, ...), custom_call_target="tpu_custom_call" | custom-call | tf_op jit(solution)/shard_map/conv_forward/pallas_call | solution.py:271
  128.2 2.7 collective-permute-start.21
  133.6 2.4 collective-permute-start.24
  137.6 23.4 %collective-permute-done.21.refs_1_.refs_8_ = bf16[8,64,256]{2,1,0:T(8,128)(2,1)S(1)} collective-permute-done((bf16[8,64,256]{2,1,0:T(8,128)(2,1)}, bf16[8,64,256]{2,1,0:T(8,128)(2,1)S(1)}, u32[]{:S(2)}, u32[]{:S(2)}) %collective-permute-start.21) | collective-permute-done | bytes 262176 | tf_op jit(solution)/shard_map/ppermute | solution.py:53
  161.0 6.7 %collective-permute-done.22.refs_2_.refs_9_ = bf16[8,64,256]{2,1,0:T(8,128)(2,1)S(1)} collective-permute-done((bf16[8,64,256]{2,1,0:T(8,128)(2,1)}, bf16[8,64,256]{2,1,0:T(8,128)(2,1)S(1)}, u32[]{:S(2)}, u32[]{:S(2)}) %collective-permute-start.22) | collective-permute-done | bytes 262176 | tf_op jit(solution)/shard_map/ppermute | solution.py:53
  167.8 3.1 maximum_bitcast_fusion.refs_9_.refs_2_
  170.9 5.1 %transposed_taps.1.refs_8_.taps_ref = bf16[9,512,512]{2,1,0:T(8,128)(2,1)} custom-call(s32[1]{0:T(128)} %bitcast.me_ref, s32[1]{0:T(128)} %bitcast.5.part_ref, bf16[4,9,64,128]{3,2,1,0:T(8,128)(2,1)} %copy-done.1, bf16[4,9,64,128]{3,2,1,0:T(8,128)(2,1)} %collective-permute-done.6.refs_1_, bf16[4,9,64,128]{3,2,1,0:T(8,128)(2,1)} %constant_dynamic-update-slice_fusion.refs_2_, ...), custom_call_target="tpu_custom_call" | custom-call | tf_op jit(solution)/shard_map/transposed_taps/pallas_call | solution.py:178
  178.3 2.5 rims.1
  183.2 3.1 collective-permute-start.30
  190.0 27.5 %sinc_both.2 = (bf16[64,2,32,256]{3,2,1,0:T(8,128)(2,1)}, f32[2,32,1]{2,1,0:T(8,128)}, f32[2,32,1]{2,1,0:T(8,128)}, bf16[10,32,256]{2,1,0:T(8,128)(2,1)}, bf16[1...) custom-call(s32[1]{0:T(128)} %bitcast.me_ref, ...), custom_call_target="tpu_custom_call" | custom-call | tf_op jit(solution)/shard_map/sinc_both/pallas_call | solution.py:575
  217.5 3.4 collective-permute-start.35
  221.2 2.4 collective-permute-start.37
  227.9 27.6 %sinc_both.3 = (bf16[64,2,32,256]{3,2,1,0:T(8,128)(2,1)}, f32[2,32,1]{2,1,0:T(8,128)}, f32[2,32,1]{2,1,0:T(8,128)}, bf16[10,32,256]{2,1,0:T(8,128)(2,1)}, bf16[1...) custom-call(s32[1]{0:T(128)} %bitcast.me_ref, ...), custom_call_target="tpu_custom_call", output_to_operand_aliasing={{0}: (20, {})} | custom-call | tf_op jit(solution)/shard_map/sinc_both/pallas_call | solution.py:575
  268.6 2.4 collective-permute-start.45
  271.0 5.3 %collective-permute-done.41.refs_11_ = bf16[10,32,256]{2,1,0:T(8,128)(2,1)S(1)} collective-permute-done((bf16[10,32,256]{2,1,0:T(8,128)(2,1)}, bf16[10,32,256]{2,1,0:T(8,128)(2,1)S(1)}, u32[]{:S(2)}, u32[]{:S(2)}) %collective-permute-start.41) | collective-permute-done | bytes 163872 | tf_op jit(solution)/shard_map/ppermute | solution.py:53
  276.4 5.4 %collective-permute-done.44.refs_14_ = bf16[10,32,256]{2,1,0:T(8,128)(2,1)S(1)} collective-permute-done((bf16[10,32,256]{2,1,0:T(8,128)(2,1)}, bf16[10,32,256]{2,1,0:T(8,128)(2,1)S(1)}, u32[]{:S(2)}, u32[]{:S(2)}) %collective-permute-start.44) | collective-permute-done | bytes 163872 | tf_op jit(solution)/shard_map/ppermute | solution.py:53
  281.9 5.0 %collective-permute-done.45.refs_15_ = bf16[10,32,256]{2,1,0:T(8,128)(2,1)S(1)} collective-permute-done((bf16[10,32,256]{2,1,0:T(8,128)(2,1)}, bf16[10,32,256]{2,1,0:T(8,128)(2,1)S(1)}, u32[]{:S(2)}, u32[]{:S(2)}) %collective-permute-start.45) | collective-permute-done | bytes 163872 | tf_op jit(solution)/shard_map/ppermute | solution.py:53
  287.6 30.3 %conv_backward.1 = (bf16[8,64,256]{2,1,0:T(8,128)(2,1)}, bf16[8,64,256]{2,1,0:T(8,128)(2,1)}, bf16[8,64,256]{2,1,0:T(8,128)(2,1)}, bf16[8,64,256]{2,1,0:T(8,128)...) custom-call(s32[1]{0:T(128)} %bitcast.me_ref, ...), custom_call_target="tpu_custom_call" | custom-call | tf_op jit(solution)/shard_map/conv_backward/pallas_call | solution.py:357
  319.1 6.7 %collective-permute-start.46 = (bf16[8,64,256]{2,1,0:T(8,128)(2,1)}, bf16[8,64,256]{2,1,0:T(8,128)(2,1)S(1)}, u32[]{:S(2)}, u32[]{:S(2)}) collective-permute-start(bf16[8,64,256]{2,1,0:T(8,128)(2,1)} %get-tuple-element.139), channel_id=1, source_target_pairs={{0,4},{1,5},{2,6},{3,7},{4,0},{5,1},{6,2},{7,3},{8,12},{9,13},{10,... | collective-permute-start | bytes 786440 | tf_op jit(solution)/shard_map/ppermute | solution.py:53
  328.0 2.7 collective-permute-start.49
  332.7 8.2 %all-reduce.3 = (f32[2,64]{1,0:T(2,128)S(1)}, f32[64]{0:T(128)}) all-reduce(f32[2,64]{1,0:T(2,128)S(1)} %maximum_bitcast_fusion.1, f32[64]{0:T(128)S(1)} %maximum_reduce_fusion), channel_id=1, replica_groups=mesh['dp'=4,'chan'=8] {'dp'}, use_global_device_ids=true, to_apply=%region_2.3 | all-reduce | flops 192 | bytes 1536 | tf_op jit(solution)/shard_map/psum | solution.py:746
  344.8 8.8 %collective-permute-done.46.refs_1_ = bf16[8,64,256]{2,1,0:T(8,128)(2,1)S(1)} collective-permute-done((bf16[8,64,256]{2,1,0:T(8,128)(2,1)}, bf16[8,64,256]{2,1,0:T(8,128)(2,1)S(1)}, u32[]{:S(2)}, u32[]{:S(2)}) %collective-permute-start.46) | collective-permute-done | bytes 262176 | tf_op jit(solution)/shard_map/ppermute | solution.py:53
  353.5 7.7 %collective-permute-done.47.refs_2_ = bf16[8,64,256]{2,1,0:T(8,128)(2,1)S(1)} collective-permute-done((bf16[8,64,256]{2,1,0:T(8,128)(2,1)}, bf16[8,64,256]{2,1,0:T(8,128)(2,1)S(1)}, u32[]{:S(2)}, u32[]{:S(2)}) %collective-permute-start.47) | collective-permute-done | bytes 262176 | tf_op jit(solution)/shard_map/ppermute | solution.py:53
  361.3 5.0 %divide_select_fusion = f32[1000,512]{1,0:T(8,128)} fusion(f32[1000,512]{1,0:T(8,128)} %param.24, bf16[2048,640]{1,0:T(8,128)(2,1)S(1)} %copy-done.43, s32[2048]{0:T(1024)S(1)} %fusion.8, f32[1000]{0:T(1024)S(1)} %broadcast_maximum_fusion, pred[1000]{0:T(1024)(128)(4,1)S(1)} %broadcast_compare_fusion), kind=kOutput, calls=%fused_computation.6 | convolution fusion | flops 2100224000 | bytes 6206464 | tf_op jit(solution)/shard_map/dot_general | solution.py:760
  366.3 7.2 %collective-permute-done.52.refs_7_ = bf16[8,64,256]{2,1,0:T(8,128)(2,1)S(1)} collective-permute-done((bf16[8,64,256]{2,1,0:T(8,128)(2,1)S(1)}, bf16[8,64,256]{2,1,0:T(8,128)(2,1)S(1)}, u32[]{:S(2)}, u32[]{:S(2)}) %collective-permute-start.52) | collective-permute-done | bytes 262176 | tf_op jit(solution)/shard_map/ppermute | solution.py:53
  375.1 2.5 collective-permute-start.56
  378.5 4.6 %scale_features.1 = f32[64,2,32,256]{3,2,1,0:T(8,128)} custom-call(s32[1]{0:T(128)} %bitcast.me_ref, f32[2,64,1]{2,1,0:T(8,128)} %copy.71.scales, bf16[8,64,256]{2,1,0:T(8,128)(2,1)} %get-tuple-element.138.refs_0_, bf16[8,64,256]{2,1,0:T(8,128)(2,1)} %copy-done.16, bf16[8,64,256]{2,1,0:T(8,128)(2,1)} %copy-done.17, bf16[8,64,256]{2,1,0:T(8,128)(2,1)} %copy-done.18, ...), custom_call_target="tpu_custom_call" | custom-call | tf_op jit(solution)/shard_map/scale_features/pallas_call | solution.py:623
  384.7 3.6 collective-permute-start.53
  388.4 8.9 %collective-permute-start.58 = (bf16[608,128]{1,0:T(8,128)(2,1)S(1)}, bf16[608,128]{1,0:T(8,128)(2,1)S(1)}, u32[]{:S(2)}, u32[]{:S(2)}) collective-permute-start(bf16[608,128]{1,0:T(8,128)(2,1)S(1)} %get-tuple-element.205), channel_id=1, source_target_pairs={{0,2},{1,3},{2,0},{3,1},{4,6},{5,7},{6,4},{7,5},{8,10},{9,11},{10,... | collective-permute-start | bytes 466952 | tf_op jit(solution)/shard_map/ppermute | solution.py:53
  397.4 6.7 %collective-permute-done.54 = bf16[608,128]{1,0:T(8,128)(2,1)S(1)} collective-permute-done((bf16[608,128]{1,0:T(8,128)(2,1)S(1)}, bf16[608,128]{1,0:T(8,128)(2,1)S(1)}, u32[]{:S(2)}, u32[]{:S(2)}) %collective-permute-start.54) | collective-permute-done | bytes 155680 | tf_op jit(solution)/shard_map/ppermute | solution.py:53
  405.6 2.7 collective-permute-done.58
  410.6 4.5 %collective-permute-done.62.refs_3_ = bf16[608,128]{1,0:T(8,128)(2,1)S(1)} collective-permute-done((bf16[608,128]{1,0:T(8,128)(2,1)S(1)}, bf16[608,128]{1,0:T(8,128)(2,1)S(1)}, u32[]{:S(2)}, u32[]{:S(2)}) %collective-permute-start.62) | collective-permute-done | bytes 155680 | tf_op jit(solution)/shard_map/ppermute | solution.py:53
  415.0 2.9 collective-permute-done.61.refs_2_
  421.7 3.4 finished_weight.1
  (291 shorter events, 78.6 us)
Async XLA Ops:
  8.0 333.9 %all-gather.2.cloned.1.call-start = ((), (), s32[]{:S(2)}) async-start(), calls=%async_computation.2 | async-start | bytes 2703360 | tf_op jit(solution)/shard_map/all_gather | solution.py:756
  9.1 17.8 %collective-permute-start = (bf16[1,9,64,128]{3,2,1,0:T(8,128)(2,1)S(1)}, bf16[1,9,64,128]{3,2,1,0:T(8,128)(2,1)S(1)}, u32[]{:S(2)}, u32[]{:S(2)}) collective-permute-start(bf16[1,9,64,128]{3,2,1,0:T(8,128)(2,1)S(1)} %bitcast.56), channel_id=1, source_target_pairs={{0,4},{1,5},{2,6},{3,7},{4,0},{5,1},{6,2},{7,3},{8,12},{9,13},{10,... | collective-permute-start | bytes 442376 | tf_op jit(solution)/shard_map/ppermute | solution.py:53
  26.4 18.7 %collective-permute-start.3 = (bf16[10,64,256]{2,1,0:T(8,128)(2,1)}, bf16[10,64,256]{2,1,0:T(8,128)(2,1)S(1)}, u32[]{:S(2)}, u32[]{:S(2)}) collective-permute-start(bf16[10,64,256]{2,1,0:T(8,128)(2,1)} %get-tuple-element.82), channel_id=1, source_target_pairs={{0,4},{1,5},{2,6},{3,7},{4,0},{5,1},{6,2},{7,3},{8,12},{9,13},{10,... | collective-permute-start | bytes 983048 | tf_op jit(solution)/shard_map/ppermute | solution.py:53
  26.8 24.5 %collective-permute-start.7 = (bf16[2,9,64,128]{3,2,1,0:T(8,128)(2,1)S(1)}, bf16[2,9,64,128]{3,2,1,0:T(8,128)(2,1)S(1)}, u32[]{:S(2)}, u32[]{:S(2)}) collective-permute-start(bf16[2,9,64,128]{3,2,1,0:T(8,128)(2,1)S(1)} %pad_maximum_fusion.8), channel_id=1, source_target_pairs={{0,1},{1,0},{2,3},{3,2},{4,5},{5,4},{6,7},{7,6},{8,9},{9,8},{10,11... | collective-permute-start | bytes 884744 | tf_op jit(solution)/shard_map/ppermute | solution.py:53
  28.4 23.7 %collective-permute-start.10 = (bf16[2,9,64,128]{3,2,1,0:T(8,128)(2,1)S(1)}, bf16[2,9,64,128]{3,2,1,0:T(8,128)(2,1)S(1)}, u32[]{:S(2)}, u32[]{:S(2)}) collective-permute-start(bf16[2,9,64,128]{3,2,1,0:T(8,128)(2,1)S(1)} %pad_maximum_fusion.8), channel_id=1, source_target_pairs={{0,2},{1,3},{2,0},{3,1},{4,6},{5,7},{6,4},{7,5},{8,10},{9,11},{10,... | collective-permute-start | bytes 884744 | tf_op jit(solution)/shard_map/ppermute | solution.py:53
  30.0 31.0 %collective-permute-start.11 = (bf16[10,64,256]{2,1,0:T(8,128)(2,1)}, bf16[10,64,256]{2,1,0:T(8,128)(2,1)S(1)}, u32[]{:S(2)}, u32[]{:S(2)}) collective-permute-start(bf16[10,64,256]{2,1,0:T(8,128)(2,1)} %get-tuple-element.86), channel_id=1, source_target_pairs={{0,5},{1,4},{2,7},{3,6},{4,1},{5,0},{6,3},{7,2},{8,13},{9,12},{10,... | collective-permute-start | bytes 983048 | tf_op jit(solution)/shard_map/ppermute | solution.py:53
  32.5 35.9 %collective-permute-start.15 = (bf16[2,9,64,128]{3,2,1,0:T(8,128)(2,1)S(1)}, bf16[2,9,64,128]{3,2,1,0:T(8,128)(2,1)S(1)}, u32[]{:S(2)}, u32[]{:S(2)}) collective-permute-start(bf16[2,9,64,128]{3,2,1,0:T(8,128)(2,1)S(1)} %pad_maximum_fusion.8), channel_id=1, source_target_pairs={{0,3},{1,2},{2,1},{3,0},{4,7},{5,6},{6,5},{7,4},{8,11},{9,10},{10,... | collective-permute-start | bytes 884744 | tf_op jit(solution)/shard_map/ppermute | solution.py:53
  45.2 26.1 %collective-permute-start.5 = (bf16[10,64,256]{2,1,0:T(8,128)(2,1)}, bf16[10,64,256]{2,1,0:T(8,128)(2,1)S(1)}, u32[]{:S(2)}, u32[]{:S(2)}) collective-permute-start(bf16[10,64,256]{2,1,0:T(8,128)(2,1)} %get-tuple-element.84), channel_id=1, source_target_pairs={{0,6},{1,7},{2,4},{3,5},{4,2},{5,3},{6,0},{7,1},{8,14},{9,15},{10,... | collective-permute-start | bytes 983048 | tf_op jit(solution)/shard_map/ppermute | solution.py:53
  51.4 17.8 %collective-permute-start.4 = (bf16[2,9,64,128]{3,2,1,0:T(8,128)(2,1)S(1)}, bf16[2,9,64,128]{3,2,1,0:T(8,128)(2,1)S(1)}, u32[]{:S(2)}, u32[]{:S(2)}) collective-permute-start(bf16[2,9,64,128]{3,2,1,0:T(8,128)(2,1)S(1)} %pad_maximum_fusion.8), channel_id=1, source_target_pairs={{0,16},{8,24},{16,0},{24,8},{1,17},{9,25},{17,1},{25,9},{2,18},{10... | collective-permute-start | bytes 884744 | tf_op jit(solution)/shard_map/ppermute | solution.py:53
  52.1 20.8 %collective-permute-start.8 = (bf16[2,9,64,128]{3,2,1,0:T(8,128)(2,1)S(1)}, bf16[2,9,64,128]{3,2,1,0:T(8,128)(2,1)S(1)}, u32[]{:S(2)}, u32[]{:S(2)}) collective-permute-start(bf16[2,9,64,128]{3,2,1,0:T(8,128)(2,1)S(1)} %collective-permute-done.7), channel_id=1, source_target_pairs={{0,16},{8,24},{16,0},{24,8},{1,17},{9,25},{17,1},{25,9},{2,18},{10... | collective-permute-start | bytes 884744 | tf_op jit(solution)/shard_map/ppermute | solution.py:53
  61.0 23.6 %collective-permute-start.13 = (bf16[10,64,256]{2,1,0:T(8,128)(2,1)}, bf16[10,64,256]{2,1,0:T(8,128)(2,1)S(1)}, u32[]{:S(2)}, u32[]{:S(2)}) collective-permute-start(bf16[10,64,256]{2,1,0:T(8,128)(2,1)} %get-tuple-element.88), channel_id=1, source_target_pairs={{0,7},{1,6},{2,5},{3,4},{4,3},{5,2},{6,1},{7,0},{8,15},{9,14},{10,... | collective-permute-start | bytes 983048 | tf_op jit(solution)/shard_map/ppermute | solution.py:53
  68.4 13.7 %collective-permute-start.12 = (bf16[2,9,64,128]{3,2,1,0:T(8,128)(2,1)S(1)}, bf16[2,9,64,128]{3,2,1,0:T(8,128)(2,1)S(1)}, u32[]{:S(2)}, u32[]{:S(2)}) collective-permute-start(bf16[2,9,64,128]{3,2,1,0:T(8,128)(2,1)S(1)} %collective-permute-done.10), channel_id=1, source_target_pairs={{0,16},{8,24},{16,0},{24,8},{1,17},{9,25},{17,1},{25,9},{2,18},{10... | collective-permute-start | bytes 884744 | tf_op jit(solution)/shard_map/ppermute | solution.py:53
  69.2 15.5 %collective-permute-start.16 = (bf16[2,9,64,128]{3,2,1,0:T(8,128)(2,1)S(1)}, bf16[2,9,64,128]{3,2,1,0:T(8,128)(2,1)S(1)}, u32[]{:S(2)}, u32[]{:S(2)}) collective-permute-start(bf16[2,9,64,128]{3,2,1,0:T(8,128)(2,1)S(1)} %collective-permute-done.15), channel_id=1, source_target_pairs={{0,16},{8,24},{16,0},{24,8},{1,17},{9,25},{17,1},{25,9},{2,18},{10... | collective-permute-start | bytes 884744 | tf_op jit(solution)/shard_map/ppermute | solution.py:53
  71.3 14.6 %collective-permute-start.18 = (bf16[10,64,256]{2,1,0:T(8,128)(2,1)S(1)}, bf16[10,64,256]{2,1,0:T(8,128)(2,1)S(1)}, u32[]{:S(2)}, u32[]{:S(2)}) collective-permute-start(bf16[10,64,256]{2,1,0:T(8,128)(2,1)S(1)} %copy-done.53), channel_id=1, source_target_pairs={{0,1},{1,0},{2,3},{3,2},{4,5},{5,4},{6,7},{7,6},{8,9},{9,8},{10,11... | collective-permute-start | bytes 983048 | tf_op jit(solution)/shard_map/ppermute | solution.py:53
  72.9 15.6 %collective-permute-start.19 = (bf16[10,64,256]{2,1,0:T(8,128)(2,1)S(1)}, bf16[10,64,256]{2,1,0:T(8,128)(2,1)S(1)}, u32[]{:S(2)}, u32[]{:S(2)}) collective-permute-start(bf16[10,64,256]{2,1,0:T(8,128)(2,1)S(1)} %copy-done.52), channel_id=1, source_target_pairs={{0,2},{1,3},{2,0},{3,1},{4,6},{5,7},{6,4},{7,5},{8,10},{9,11},{10,... | collective-permute-start | bytes 983048 | tf_op jit(solution)/shard_map/ppermute | solution.py:53
  82.1 23.6 %collective-permute-start.6 = (bf16[4,9,64,128]{3,2,1,0:T(8,128)(2,1)S(1)}, bf16[4,9,64,128]{3,2,1,0:T(8,128)(2,1)}, u32[]{:S(2)}, u32[]{:S(2)}) collective-permute-start(bf16[4,9,64,128]{3,2,1,0:T(8,128)(2,1)S(1)} %pad_maximum_fusion.refs_0_), channel_id=1, source_target_pairs={{0,8},{8,0},{16,24},{24,16},{1,9},{9,1},{17,25},{25,17},{2,10},{10... | collective-permute-start | bytes 1769480 | tf_op jit(solution)/shard_map/ppermute | solution.py:53
  84.6 26.0 %collective-permute-start.9 = (bf16[4,9,64,128]{3,2,1,0:T(8,128)(2,1)}, bf16[4,9,64,128]{3,2,1,0:T(8,128)(2,1)}, u32[]{:S(2)}, u32[]{:S(2)}) collective-permute-start(bf16[4,9,64,128]{3,2,1,0:T(8,128)(2,1)} %constant_dynamic-update-slice_fusion.refs_2_), channel_id=1, source_target_pairs={{0,8},{8,0},{16,24},{24,16},{1,9},{9,1},{17,25},{25,17},{2,10},{10... | collective-permute-start | bytes 1769480 | tf_op jit(solution)/shard_map/ppermute | solution.py:53
  84.7 26.0 %collective-permute-start.14 = (bf16[4,9,64,128]{3,2,1,0:T(8,128)(2,1)}, bf16[4,9,64,128]{3,2,1,0:T(8,128)(2,1)}, u32[]{:S(2)}, u32[]{:S(2)}) collective-permute-start(bf16[4,9,64,128]{3,2,1,0:T(8,128)(2,1)} %constant_dynamic-update-slice_fusion.2.refs_4_), channel_id=1, source_target_pairs={{0,8},{8,0},{16,24},{24,16},{1,9},{9,1},{17,25},{25,17},{2,10},{10... | collective-permute-start | bytes 1769480 | tf_op jit(solution)/shard_map/ppermute | solution.py:53
  85.9 24.7 %collective-permute-start.17 = (bf16[4,9,64,128]{3,2,1,0:T(8,128)(2,1)}, bf16[4,9,64,128]{3,2,1,0:T(8,128)(2,1)}, u32[]{:S(2)}, u32[]{:S(2)}) collective-permute-start(bf16[4,9,64,128]{3,2,1,0:T(8,128)(2,1)} %constant_dynamic-update-slice_fusion.4.refs_6_), channel_id=1, source_target_pairs={{0,8},{8,0},{16,24},{24,16},{1,9},{9,1},{17,25},{25,17},{2,10},{10... | collective-permute-start | bytes 1769480 | tf_op jit(solution)/shard_map/ppermute | solution.py:53
  88.5 15.9 %collective-permute-start.20 = (bf16[10,64,256]{2,1,0:T(8,128)(2,1)}, bf16[10,64,256]{2,1,0:T(8,128)(2,1)S(1)}, u32[]{:S(2)}, u32[]{:S(2)}) collective-permute-start(bf16[10,64,256]{2,1,0:T(8,128)(2,1)} %get-tuple-element.93), channel_id=1, source_target_pairs={{0,3},{1,2},{2,1},{3,0},{4,7},{5,6},{6,5},{7,4},{8,11},{9,10},{10,... | collective-permute-start | bytes 983048 | tf_op jit(solution)/shard_map/ppermute | solution.py:53
  104.4 29.3 %collective-permute-start.29 = (bf16[64,2,7,256]{3,0,2,1:T(8,128)(2,1)}, bf16[64,2,7,256]{3,0,2,1:T(8,128)(2,1)}, u32[]{:S(2)}, u32[]{:S(2)}) collective-permute-start(bf16[64,2,7,256]{3,0,2,1:T(8,128)(2,1)} %get-tuple-element.191), channel_id=1, source_target_pairs={{8,0},{16,8},{24,16},{9,1},{17,9},{25,17},{10,2},{18,10},{26,18},{... | collective-permute-start | bytes 1376264 | tf_op jit(solution)/shard_map/ppermute | solution.py:49
  105.7 30.4 %collective-permute-start.28 = (bf16[64,2,7,256]{3,0,2,1:T(8,128)(2,1)}, bf16[64,2,7,256]{3,0,2,1:T(8,128)(2,1)}, u32[]{:S(2)}, u32[]{:S(2)}) collective-permute-start(bf16[64,2,7,256]{3,0,2,1:T(8,128)(2,1)} %get-tuple-element.190), channel_id=1, source_target_pairs={{0,8},{8,16},{16,24},{1,9},{9,17},{17,25},{2,10},{10,18},{18,26},{... | collective-permute-start | bytes 1376264 | tf_op jit(solution)/shard_map/ppermute | solution.py:49
  128.2 32.8 %collective-permute-start.21 = (bf16[8,64,256]{2,1,0:T(8,128)(2,1)}, bf16[8,64,256]{2,1,0:T(8,128)(2,1)S(1)}, u32[]{:S(2)}, u32[]{:S(2)}) collective-permute-start(bf16[8,64,256]{2,1,0:T(8,128)(2,1)} %get-tuple-element.95), channel_id=1, source_target_pairs={{0,4},{1,5},{2,6},{3,7},{4,0},{5,1},{6,2},{7,3},{8,12},{9,13},{10,... | collective-permute-start | bytes 786440 | tf_op jit(solution)/shard_map/ppermute | solution.py:53
  130.9 36.7 %collective-permute-start.22 = (bf16[8,64,256]{2,1,0:T(8,128)(2,1)}, bf16[8,64,256]{2,1,0:T(8,128)(2,1)S(1)}, u32[]{:S(2)}, u32[]{:S(2)}) collective-permute-start(bf16[8,64,256]{2,1,0:T(8,128)(2,1)} %get-tuple-element.96), channel_id=1, source_target_pairs={{0,5},{1,4},{2,7},{3,6},{4,1},{5,0},{6,3},{7,2},{8,13},{9,12},{10,... | collective-permute-start | bytes 786440 | tf_op jit(solution)/shard_map/ppermute | solution.py:53
  132.2 43.9 %collective-permute-start.23 = (bf16[8,64,256]{2,1,0:T(8,128)(2,1)}, bf16[8,64,256]{2,1,0:T(8,128)(2,1)S(1)}, u32[]{:S(2)}, u32[]{:S(2)}) collective-permute-start(bf16[8,64,256]{2,1,0:T(8,128)(2,1)} %get-tuple-element.97), channel_id=1, source_target_pairs={{0,6},{1,7},{2,4},{3,5},{4,2},{5,3},{6,0},{7,1},{8,14},{9,15},{10,... | collective-permute-start | bytes 786440 | tf_op jit(solution)/shard_map/ppermute | solution.py:53
  133.6 42.5 %collective-permute-start.24 = (bf16[8,64,256]{2,1,0:T(8,128)(2,1)}, bf16[8,64,256]{2,1,0:T(8,128)(2,1)}, u32[]{:S(2)}, u32[]{:S(2)}) collective-permute-start(bf16[8,64,256]{2,1,0:T(8,128)(2,1)} %get-tuple-element.98), channel_id=1, source_target_pairs={{0,7},{1,6},{2,5},{3,4},{4,3},{5,2},{6,1},{7,0},{8,15},{9,14},{10,... | collective-permute-start | bytes 786440 | tf_op jit(solution)/shard_map/ppermute | solution.py:53
  136.0 40.1 %collective-permute-start.25 = (bf16[8,64,256]{2,1,0:T(8,128)(2,1)}, bf16[8,64,256]{2,1,0:T(8,128)(2,1)}, u32[]{:S(2)}, u32[]{:S(2)}) collective-permute-start(bf16[8,64,256]{2,1,0:T(8,128)(2,1)} %get-tuple-element.99), channel_id=1, source_target_pairs={{0,1},{1,0},{2,3},{3,2},{4,5},{5,4},{6,7},{7,6},{8,9},{9,8},{10,11... | collective-permute-start | bytes 786440 | tf_op jit(solution)/shard_map/ppermute | solution.py:53
  161.0 15.1 %collective-permute-start.26 = (bf16[8,64,256]{2,1,0:T(8,128)(2,1)}, bf16[8,64,256]{2,1,0:T(8,128)(2,1)}, u32[]{:S(2)}, u32[]{:S(2)}) collective-permute-start(bf16[8,64,256]{2,1,0:T(8,128)(2,1)} %get-tuple-element.100), channel_id=1, source_target_pairs={{0,2},{1,3},{2,0},{3,1},{4,6},{5,7},{6,4},{7,5},{8,10},{9,11},{10,... | collective-permute-start | bytes 786440 | tf_op jit(solution)/shard_map/ppermute | solution.py:53
  181.5 192.0 %reduce-scatter.2.cloned.1.call-start = ((), (), s32[]{:S(2)}) async-start(), calls=%async_computation.1 | async-start | bytes 5898240 | tf_op jit(solution)/shard_map/reduce_scatter | solution.py:768
  217.5 37.9 %collective-permute-start.35 = (bf16[10,32,256]{2,1,0:T(8,128)(2,1)}, bf16[10,32,256]{2,1,0:T(8,128)(2,1)S(1)}, u32[]{:S(2)}, u32[]{:S(2)}) collective-permute-start(bf16[10,32,256]{2,1,0:T(8,128)(2,1)} %get-tuple-element.118), channel_id=1, source_target_pairs={{0,4},{1,5},{2,6},{3,7},{4,0},{5,1},{6,2},{7,3},{8,12},{9,13},{10,... | collective-permute-start | bytes 491528 | tf_op jit(solution)/shard_map/ppermute | solution.py:53
  221.0 35.7 %collective-permute-start.36 = (bf16[10,32,256]{2,1,0:T(8,128)(2,1)}, bf16[10,32,256]{2,1,0:T(8,128)(2,1)S(1)}, u32[]{:S(2)}, u32[]{:S(2)}) collective-permute-start(bf16[10,32,256]{2,1,0:T(8,128)(2,1)} %get-tuple-element.119), channel_id=1, source_target_pairs={{0,5},{1,4},{2,7},{3,6},{4,1},{5,0},{6,3},{7,2},{8,13},{9,12},{10,... | collective-permute-start | bytes 491528 | tf_op jit(solution)/shard_map/ppermute | solution.py:53
  221.2 37.2 %collective-permute-start.37 = (bf16[10,32,256]{2,1,0:T(8,128)(2,1)}, bf16[10,32,256]{2,1,0:T(8,128)(2,1)S(1)}, u32[]{:S(2)}, u32[]{:S(2)}) collective-permute-start(bf16[10,32,256]{2,1,0:T(8,128)(2,1)} %get-tuple-element.120), channel_id=1, source_target_pairs={{0,6},{1,7},{2,4},{3,5},{4,2},{5,3},{6,0},{7,1},{8,14},{9,15},{10,... | collective-permute-start | bytes 491528 | tf_op jit(solution)/shard_map/ppermute | solution.py:53
  223.6 34.8 %collective-permute-start.38 = (bf16[10,32,256]{2,1,0:T(8,128)(2,1)}, bf16[10,32,256]{2,1,0:T(8,128)(2,1)S(1)}, u32[]{:S(2)}, u32[]{:S(2)}) collective-permute-start(bf16[10,32,256]{2,1,0:T(8,128)(2,1)} %get-tuple-element.121), channel_id=1, source_target_pairs={{0,7},{1,6},{2,5},{3,4},{4,3},{5,2},{6,1},{7,0},{8,15},{9,14},{10,... | collective-permute-start | bytes 491528 | tf_op jit(solution)/shard_map/ppermute | solution.py:53
  227.1 33.2 %collective-permute-start.32 = (bf16[10,32,256]{2,1,0:T(8,128)(2,1)}, bf16[10,32,256]{2,1,0:T(8,128)(2,1)S(1)}, u32[]{:S(2)}, u32[]{:S(2)}) collective-permute-start(bf16[10,32,256]{2,1,0:T(8,128)(2,1)} %get-tuple-element.115), channel_id=1, source_target_pairs={{0,1},{1,0},{2,3},{3,2},{4,5},{5,4},{6,7},{7,6},{8,9},{9,8},{10,11... | collective-permute-start | bytes 491528 | tf_op jit(solution)/shard_map/ppermute | solution.py:53
  260.3 16.1 %collective-permute-start.41 = (bf16[10,32,256]{2,1,0:T(8,128)(2,1)}, bf16[10,32,256]{2,1,0:T(8,128)(2,1)S(1)}, u32[]{:S(2)}, u32[]{:S(2)}) collective-permute-start(bf16[10,32,256]{2,1,0:T(8,128)(2,1)} %get-tuple-element.129), channel_id=1, source_target_pairs={{0,3},{1,2},{2,1},{3,0},{4,7},{5,6},{6,5},{7,4},{8,11},{9,10},{10,... | collective-permute-start | bytes 491528 | tf_op jit(solution)/shard_map/ppermute | solution.py:53
  262.0 14.4 %collective-permute-start.42 = (bf16[10,32,256]{2,1,0:T(8,128)(2,1)}, bf16[10,32,256]{2,1,0:T(8,128)(2,1)S(1)}, u32[]{:S(2)}, u32[]{:S(2)}) collective-permute-start(bf16[10,32,256]{2,1,0:T(8,128)(2,1)} %get-tuple-element.131), channel_id=1, source_target_pairs={{0,4},{1,5},{2,6},{3,7},{4,0},{5,1},{6,2},{7,3},{8,12},{9,13},{10,... | collective-permute-start | bytes 491528 | tf_op jit(solution)/shard_map/ppermute | solution.py:53
  265.8 16.1 %collective-permute-start.44 = (bf16[10,32,256]{2,1,0:T(8,128)(2,1)}, bf16[10,32,256]{2,1,0:T(8,128)(2,1)S(1)}, u32[]{:S(2)}, u32[]{:S(2)}) collective-permute-start(bf16[10,32,256]{2,1,0:T(8,128)(2,1)} %get-tuple-element.135), channel_id=1, source_target_pairs={{0,6},{1,7},{2,4},{3,5},{4,2},{5,3},{6,0},{7,1},{8,14},{9,15},{10,... | collective-permute-start | bytes 491528 | tf_op jit(solution)/shard_map/ppermute | solution.py:53
  268.6 18.3 %collective-permute-start.45 = (bf16[10,32,256]{2,1,0:T(8,128)(2,1)}, bf16[10,32,256]{2,1,0:T(8,128)(2,1)S(1)}, u32[]{:S(2)}, u32[]{:S(2)}) collective-permute-start(bf16[10,32,256]{2,1,0:T(8,128)(2,1)} %get-tuple-element.137), channel_id=1, source_target_pairs={{0,7},{1,6},{2,5},{3,4},{4,3},{5,2},{6,1},{7,0},{8,15},{9,14},{10,... | collective-permute-start | bytes 491528 | tf_op jit(solution)/shard_map/ppermute | solution.py:53
  319.1 34.4 %collective-permute-start.46 = (bf16[8,64,256]{2,1,0:T(8,128)(2,1)}, bf16[8,64,256]{2,1,0:T(8,128)(2,1)S(1)}, u32[]{:S(2)}, u32[]{:S(2)}) collective-permute-start(bf16[8,64,256]{2,1,0:T(8,128)(2,1)} %get-tuple-element.139), channel_id=1, source_target_pairs={{0,4},{1,5},{2,6},{3,7},{4,0},{5,1},{6,2},{7,3},{8,12},{9,13},{10,... | collective-permute-start | bytes 786440 | tf_op jit(solution)/shard_map/ppermute | solution.py:53
  325.8 35.5 %collective-permute-start.47 = (bf16[8,64,256]{2,1,0:T(8,128)(2,1)}, bf16[8,64,256]{2,1,0:T(8,128)(2,1)S(1)}, u32[]{:S(2)}, u32[]{:S(2)}) collective-permute-start(bf16[8,64,256]{2,1,0:T(8,128)(2,1)} %get-tuple-element.140), channel_id=1, source_target_pairs={{0,5},{1,4},{2,7},{3,6},{4,1},{5,0},{6,3},{7,2},{8,13},{9,12},{10,... | collective-permute-start | bytes 786440 | tf_op jit(solution)/shard_map/ppermute | solution.py:53
  327.0 39.3 %collective-permute-start.48 = (bf16[8,64,256]{2,1,0:T(8,128)(2,1)}, bf16[8,64,256]{2,1,0:T(8,128)(2,1)S(1)}, u32[]{:S(2)}, u32[]{:S(2)}) collective-permute-start(bf16[8,64,256]{2,1,0:T(8,128)(2,1)} %get-tuple-element.141), channel_id=1, source_target_pairs={{0,6},{1,7},{2,4},{3,5},{4,2},{5,3},{6,0},{7,1},{8,14},{9,15},{10,... | collective-permute-start | bytes 786440 | tf_op jit(solution)/shard_map/ppermute | solution.py:53
  328.0 38.3 %collective-permute-start.49 = (bf16[8,64,256]{2,1,0:T(8,128)(2,1)}, bf16[8,64,256]{2,1,0:T(8,128)(2,1)S(1)}, u32[]{:S(2)}, u32[]{:S(2)}) collective-permute-start(bf16[8,64,256]{2,1,0:T(8,128)(2,1)} %get-tuple-element.142), channel_id=1, source_target_pairs={{0,7},{1,6},{2,5},{3,4},{4,3},{5,2},{6,1},{7,0},{8,15},{9,14},{10,... | collective-permute-start | bytes 786440 | tf_op jit(solution)/shard_map/ppermute | solution.py:53
  330.7 35.6 %collective-permute-start.50 = (bf16[8,64,256]{2,1,0:T(8,128)(2,1)S(1)}, bf16[8,64,256]{2,1,0:T(8,128)(2,1)S(1)}, u32[]{:S(2)}, u32[]{:S(2)}) collective-permute-start(bf16[8,64,256]{2,1,0:T(8,128)(2,1)S(1)} %copy-done.56), channel_id=1, source_target_pairs={{0,1},{1,0},{2,3},{3,2},{4,5},{5,4},{6,7},{7,6},{8,9},{9,8},{10,11... | collective-permute-start | bytes 786440 | tf_op jit(solution)/shard_map/ppermute | solution.py:53
  383.1 14.3 %collective-permute-start.55 = (bf16[608,128]{1,0:T(8,128)(2,1)S(1)}, bf16[608,128]{1,0:T(8,128)(2,1)S(1)}, u32[]{:S(2)}, u32[]{:S(2)}) collective-permute-start(bf16[608,128]{1,0:T(8,128)(2,1)S(1)} %get-tuple-element.203), channel_id=1, source_target_pairs={{0,6},{1,7},{2,4},{3,5},{4,2},{5,3},{6,0},{7,1},{8,14},{9,15},{10,... | collective-permute-start | bytes 466952 | tf_op jit(solution)/shard_map/ppermute | solution.py:53
  383.7 20.4 %collective-permute-start.54 = (bf16[608,128]{1,0:T(8,128)(2,1)S(1)}, bf16[608,128]{1,0:T(8,128)(2,1)S(1)}, u32[]{:S(2)}, u32[]{:S(2)}) collective-permute-start(bf16[608,128]{1,0:T(8,128)(2,1)S(1)} %get-tuple-element.207), channel_id=1, source_target_pairs={{0,5},{1,4},{2,7},{3,6},{4,1},{5,0},{6,3},{7,2},{8,13},{9,12},{10,... | collective-permute-start | bytes 466952 | tf_op jit(solution)/shard_map/ppermute | solution.py:53
  384.7 20.9 %collective-permute-start.53 = (bf16[608,128]{1,0:T(8,128)(2,1)S(1)}, bf16[608,128]{1,0:T(8,128)(2,1)S(1)}, u32[]{:S(2)}, u32[]{:S(2)}) collective-permute-start(bf16[608,128]{1,0:T(8,128)(2,1)S(1)} %get-tuple-element.208), channel_id=1, source_target_pairs={{0,4},{1,5},{2,6},{3,7},{4,0},{5,1},{6,2},{7,3},{8,12},{9,13},{10,... | collective-permute-start | bytes 466952 | tf_op jit(solution)/shard_map/ppermute | solution.py:53
  388.3 17.3 %collective-permute-start.59 = (bf16[608,128]{1,0:T(8,128)(2,1)S(1)}, bf16[608,128]{1,0:T(8,128)(2,1)S(1)}, u32[]{:S(2)}, u32[]{:S(2)}) collective-permute-start(bf16[608,128]{1,0:T(8,128)(2,1)S(1)} %get-tuple-element.206), channel_id=1, source_target_pairs={{0,3},{1,2},{2,1},{3,0},{4,7},{5,6},{6,5},{7,4},{8,11},{9,10},{10,... | collective-permute-start | bytes 466952 | tf_op jit(solution)/shard_map/ppermute | solution.py:53
  388.4 19.9 %collective-permute-start.58 = (bf16[608,128]{1,0:T(8,128)(2,1)S(1)}, bf16[608,128]{1,0:T(8,128)(2,1)S(1)}, u32[]{:S(2)}, u32[]{:S(2)}) collective-permute-start(bf16[608,128]{1,0:T(8,128)(2,1)S(1)} %get-tuple-element.205), channel_id=1, source_target_pairs={{0,2},{1,3},{2,0},{3,1},{4,6},{5,7},{6,4},{7,5},{8,10},{9,11},{10,... | collective-permute-start | bytes 466952 | tf_op jit(solution)/shard_map/ppermute | solution.py:53
  (77 other events, 1101.4 us)
Sparse Core Ops, SparseCore 0:
  181.6 70.3 all-gather.1
Sparse Core Ops, SparseCore 1:
  318.0 53.7 reduce-scatter.1
